TPU v7x, 32 devices: a whole 2x2x4 slice. The times are simulated.
32 devices in a mesh: rows: 8 (over z, core), wide: 4 (over y, x).
Axes of the slice: x: 2, y: 2, z: 4, core: 2. Of those that a mesh axis runs over, the one named last changes fastest.
Arguments:
- block_input: bfloat16 [8, 3328, 1152], P('rows', 'wide'), may hold values from -6 to 6
- long_skip: bfloat16 [8, 3328, 1152], P('rows', 'wide'), may hold values from -6 to 6
- segment_ids: int32 [8, 3328], P('rows'), may hold values from 0 to 12, as said below
- item_lengths: int32 [8, 12], P('rows'), may hold values from 0 to 1026, as said below
- skip_weight: bfloat16 [2304, 1152], P('wide'), may hold values from -0.125 to 0.125
- first_gain: bfloat16 [1152], P('wide'), may hold values from 0.25 to 1.75
- first_shift: bfloat16 [1152], P('wide'), may hold values from -1.75 to 1.75
- qkv_weight: bfloat16 [1152, 3456], P('wide'), may hold values from -0.25 to 0.25
- out_weight: bfloat16 [1152, 1152], P('wide'), may hold values from -2 to 2
- second_gain: bfloat16 [1152], P('wide'), may hold values from 0.25 to 1.75
- second_shift: bfloat16 [1152], P('wide'), may hold values from -1.75 to 1.75
- up_weight: bfloat16 [1152, 4608], P('wide'), may hold values from -0.1875 to 0.1875
- down_weight: bfloat16 [4608, 1152], P('wide'), may hold values from -0.09375 to 0.09375
- output_grad: bfloat16 [8, 3328, 1152], P('rows', 'wide'), may hold values from -6 to 6
Outputs:
- layer_output: float32 [8, 3328, 1152], P('rows', 'wide')
- input_grad: float32 [8, 3328, 1152], P('rows', 'wide')
- skip_grad: float32 [8, 3328, 1152], P('rows', 'wide')
- skip_weight_grad: float32 [2304, 1152], P('wide')
- first_gain_grad: float32 [1152], P('wide')
- first_shift_grad: float32 [1152], P('wide')
- qkv_weight_grad: float32 [1152, 3456], P('wide')
- out_weight_grad: float32 [1152, 1152], P('wide')
- second_gain_grad: float32 [1152], P('wide')
- second_shift_grad: float32 [1152], P('wide')
- up_weight_grad: float32 [1152, 4608], P('wide')
- down_weight_grad: float32 [4608, 1152], P('wide')
Inputs may be any that keep to these rules, and one draw needn't show every extreme that they name: `item_lengths`: each row lists the lengths of its items, each 258 or 1026, in the order in which they stand in the row, followed by zeros; the lengths of a row sum to less than 3328, and some row holds 3328 // 1026 long items. `segment_ids`: positions of a row carry the number of their item (0 for the first, counting the entries of item_lengths in order); the positions after the last item carry 12.
All inputs are finite; a program needn't handle non-finite values.
Results may differ from a plain program's by a relative error of at most 0.02.
Values may be sent and summed in bfloat16 or wider, within the bound.
A program may use at most 320 MiB of HBM per device.

v0:
```python
import jax
import jax.numpy as jnp
from jax import lax
from jax.sharding import PartitionSpec as P

HEAD = 72
QBLOCKS = 4


def normalize(values, gain_row, shift_row):
    centred = values - jnp.mean(values, axis=1, keepdims=True)
    spread = jnp.mean(centred * centred, axis=1, keepdims=True)
    inverse = lax.rsqrt(spread + 1e-05)
    scaled = centred * inverse
    return (scaled * gain_row + shift_row, scaled, inverse)


def norm_back(upstream, scaled, inverse, gain_row):
    weighted = upstream * gain_row
    across = (
        weighted
        - jnp.mean(weighted, axis=1, keepdims=True)
        - scaled * jnp.mean(weighted * scaled, axis=1, keepdims=True)
    )
    return (across * inverse, jnp.sum(upstream * scaled, axis=0), jnp.sum(upstream, axis=0))


def outer_sum(left_arr, right_arr):
    return jnp.einsum("td,te->de", left_arr, right_arr, preferred_element_type=jnp.float32)


def times_transposed(left_arr, right_arr):
    return jnp.einsum("te,de->td", left_arr, right_arr, preferred_element_type=jnp.float32)


def exact_gelu(values):
    return jax.nn.gelu(values, approximate=False)


def to_pairs(values, rows_dev, heads_here):
    row_len = values.shape[1]
    return (
        values.reshape(rows_dev, row_len, heads_here, HEAD)
        .transpose(0, 2, 1, 3)
        .reshape(rows_dev * heads_here, row_len, HEAD)
    )


def from_pairs(values, rows_dev, heads_here):
    row_len = values.shape[1]
    return (
        values.reshape(rows_dev, heads_here, row_len, HEAD)
        .transpose(0, 2, 1, 3)
        .reshape(rows_dev, row_len, heads_here * HEAD)
    )


def attend_pair(packed):
    query_rows, key_rows, value_rows, seg_pair, valid_pair = packed
    row_len = query_rows.shape[0]
    block_len = row_len // QBLOCKS
    factor = HEAD ** (-0.5)

    def one_block(inner_args):
        query_blk, seg_blk, valid_blk = inner_args
        scores = (
            jnp.einsum("qd,kd->qk", query_blk, key_rows, preferred_element_type=jnp.float32)
            * factor
        )
        allowed = (seg_blk[:, None] == seg_pair[None, :]) & (
            valid_blk[:, None] == valid_pair[None, :]
        )
        masked = jnp.where(allowed, scores, -1e30)
        largest = jnp.max(masked, axis=1, keepdims=True)
        exponent = jnp.exp(masked - largest)
        totals = jnp.sum(exponent, axis=1, keepdims=True)
        softmax_out = (exponent / totals).astype(jnp.bfloat16)
        mixed_out = jnp.dot(
            softmax_out, value_rows, preferred_element_type=jnp.float32
        ) * valid_blk[:, None].astype(jnp.float32)
        return (mixed_out.astype(jnp.bfloat16), (largest + jnp.log(totals))[:, 0])

    mixed_out, logsum = lax.map(
        one_block,
        (
            query_rows.reshape(QBLOCKS, block_len, HEAD),
            seg_pair.reshape(QBLOCKS, block_len),
            valid_pair.reshape(QBLOCKS, block_len),
        ),
    )
    return (mixed_out.reshape(row_len, HEAD), logsum.reshape(row_len))


def attend_back(packed):
    query_rows, key_rows, value_rows, grad_rows, logsum, seg_pair, valid_pair = packed
    row_len = query_rows.shape[0]
    block_len = row_len // QBLOCKS
    factor = HEAD ** (-0.5)

    def one_block(running, inner_args):
        key_acc, value_acc = running
        query_blk, grad_blk, lse_blk, seg_blk, valid_blk = inner_args
        scores = (
            jnp.einsum("qd,kd->qk", query_blk, key_rows, preferred_element_type=jnp.float32)
            * factor
        )
        allowed = (seg_blk[:, None] == seg_pair[None, :]) & (
            valid_blk[:, None] == valid_pair[None, :]
        )
        masked = jnp.where(allowed, scores, -1e30)
        softmax_out = jnp.exp(masked - lse_blk[:, None])
        grad_masked = grad_blk * valid_blk[:, None].astype(jnp.bfloat16)
        value_acc = value_acc + jnp.einsum(
            "qk,qd->kd",
            softmax_out.astype(jnp.bfloat16),
            grad_masked,
            preferred_element_type=jnp.float32,
        )
        grad_soft = jnp.einsum(
            "qd,kd->qk", grad_masked, value_rows, preferred_element_type=jnp.float32
        )
        inner_sum = jnp.sum(softmax_out * grad_soft, axis=1, keepdims=True)
        grad_scores = (softmax_out * (grad_soft - inner_sum)).astype(jnp.bfloat16)
        grad_query = jnp.dot(grad_scores, key_rows, preferred_element_type=jnp.float32) * factor
        key_acc = (
            key_acc
            + jnp.einsum("qk,qd->kd", grad_scores, query_blk, preferred_element_type=jnp.float32)
            * factor
        )
        return ((key_acc, value_acc), grad_query)

    zero_rows = jnp.zeros((row_len, HEAD), jnp.float32)
    blocks_in = (
        query_rows.reshape(QBLOCKS, block_len, HEAD),
        grad_rows.reshape(QBLOCKS, block_len, HEAD),
        logsum.reshape(QBLOCKS, block_len),
        seg_pair.reshape(QBLOCKS, block_len),
        valid_pair.reshape(QBLOCKS, block_len),
    )
    (key_grad, value_grad), query_grad = lax.scan(one_block, (zero_rows, zero_rows), blocks_in)
    return jnp.stack([query_grad.reshape(row_len, HEAD), key_grad, value_grad]).astype(jnp.bfloat16)


def on_device(
    block_input,
    long_skip,
    segment_ids,
    item_lengths,
    skip_weight,
    first_gain,
    first_shift,
    qkv_weight,
    out_weight,
    second_gain,
    second_shift,
    up_weight,
    down_weight,
    output_grad,
):
    w_skip, w_qkv, w_out, w_up, w_down, gain_first, shift_first, gain_second, shift_second = (
        lax.all_gather(skip_weight, "wide", axis=0, tiled=True),
        lax.all_gather(qkv_weight, "wide", axis=0, tiled=True),
        lax.all_gather(out_weight, "wide", axis=0, tiled=True),
        lax.all_gather(up_weight, "wide", axis=0, tiled=True),
        lax.all_gather(down_weight, "wide", axis=0, tiled=True),
        lax.all_gather(first_gain, "wide", axis=0, tiled=True),
        lax.all_gather(first_shift, "wide", axis=0, tiled=True),
        lax.all_gather(second_gain, "wide", axis=0, tiled=True),
        lax.all_gather(second_shift, "wide", axis=0, tiled=True),
    )
    gain_first = gain_first.astype(jnp.float32)
    shift_first = shift_first.astype(jnp.float32)
    gain_second = gain_second.astype(jnp.float32)
    shift_second = shift_second.astype(jnp.float32)
    rows_dev, tok_wide, features = block_input.shape
    tokens = rows_dev * tok_wide
    joined = jnp.concatenate(
        [block_input.reshape(tokens, features), long_skip.reshape(tokens, features)], axis=1
    )
    hidden = jnp.dot(joined, w_skip, preferred_element_type=jnp.float32)
    normed_one, scaled_one, inverse_one = normalize(hidden, gain_first, shift_first)
    normed_one = normed_one.astype(jnp.bfloat16)
    qkv_local = (
        jnp.dot(normed_one, w_qkv, preferred_element_type=jnp.float32)
        .astype(jnp.bfloat16)
        .reshape(rows_dev, tok_wide, 3, features)
    )
    qkv_heads = lax.all_to_all(qkv_local, "wide", split_axis=3, concat_axis=1, tiled=True)
    row_len = qkv_heads.shape[1]
    heads_here = qkv_heads.shape[3] // HEAD
    valid_mask = (
        jnp.arange(row_len, dtype=jnp.int32)[None, :] < jnp.sum(item_lengths, axis=1)[:, None]
    )
    seg_pairs = jnp.repeat(segment_ids, heads_here, axis=0)
    valid_pairs = jnp.repeat(valid_mask, heads_here, axis=0)
    query_pairs = to_pairs(qkv_heads[:, :, 0], rows_dev, heads_here)
    key_pairs = to_pairs(qkv_heads[:, :, 1], rows_dev, heads_here)
    value_pairs = to_pairs(qkv_heads[:, :, 2], rows_dev, heads_here)
    mixed_pairs, logsum = lax.map(
        attend_pair, (query_pairs, key_pairs, value_pairs, seg_pairs, valid_pairs)
    )
    attended_heads = from_pairs(mixed_pairs, rows_dev, heads_here)
    attended = lax.all_to_all(
        attended_heads, "wide", split_axis=1, concat_axis=2, tiled=True
    ).reshape(tokens, features)
    mid_state = hidden + jnp.dot(attended, w_out, preferred_element_type=jnp.float32)
    normed_two, scaled_two, inverse_two = normalize(mid_state, gain_second, shift_second)
    normed_two = normed_two.astype(jnp.bfloat16)
    upper_proj = jnp.dot(normed_two, w_up, preferred_element_type=jnp.float32)
    active, gelu_pull = jax.vjp(exact_gelu, upper_proj)
    active = active.astype(jnp.bfloat16)
    layer_output = mid_state + jnp.dot(active, w_down, preferred_element_type=jnp.float32)
    grad_output = output_grad.reshape(tokens, features)
    grad_down = outer_sum(active, grad_output)
    grad_active = times_transposed(grad_output, w_down)
    (grad_upper,) = gelu_pull(grad_active)
    grad_upper = grad_upper.astype(jnp.bfloat16)
    grad_up = outer_sum(normed_two, grad_upper)
    grad_second = times_transposed(grad_upper, w_up)
    back_two, gain_two_grad, shift_two_grad = norm_back(
        grad_second, scaled_two, inverse_two, gain_second
    )
    grad_mid = grad_output.astype(jnp.float32) + back_two
    grad_mid_low = grad_mid.astype(jnp.bfloat16)
    grad_out_w = outer_sum(attended, grad_mid_low)
    grad_attended = (
        times_transposed(grad_mid_low, w_out)
        .astype(jnp.bfloat16)
        .reshape(rows_dev, tok_wide, features)
    )
    grad_heads = lax.all_to_all(grad_attended, "wide", split_axis=2, concat_axis=1, tiled=True)
    grad_pairs = to_pairs(grad_heads, rows_dev, heads_here)
    stacked = lax.map(
        attend_back,
        (query_pairs, key_pairs, value_pairs, grad_pairs, logsum, seg_pairs, valid_pairs),
    )
    stacked = (
        stacked.reshape(rows_dev, heads_here, 3, row_len, HEAD)
        .transpose(0, 3, 2, 1, 4)
        .reshape(rows_dev, row_len, 3, heads_here * HEAD)
    )
    grad_qkv = lax.all_to_all(stacked, "wide", split_axis=1, concat_axis=3, tiled=True).reshape(
        tokens, 3 * features
    )
    grad_qkv_w = outer_sum(normed_one, grad_qkv)
    grad_first = times_transposed(grad_qkv, w_qkv)
    back_one, gain_one_grad, shift_one_grad = norm_back(
        grad_first, scaled_one, inverse_one, gain_first
    )
    grad_hidden = (grad_mid + back_one).astype(jnp.bfloat16)
    grad_skip_w = outer_sum(joined, grad_hidden)
    grad_joined = times_transposed(grad_hidden, w_skip)
    input_grad = grad_joined[:, :features].reshape(rows_dev, tok_wide, features)
    skip_grad = grad_joined[:, features:].reshape(rows_dev, tok_wide, features)
    small_grads = jnp.stack([gain_one_grad, shift_one_grad, gain_two_grad, shift_two_grad], axis=1)
    shares = (
        lax.psum_scatter(
            grad_skip_w.astype(jnp.bfloat16), "wide", scatter_dimension=0, tiled=True
        ).astype(jnp.float32),
        lax.psum_scatter(
            grad_qkv_w.astype(jnp.bfloat16), "wide", scatter_dimension=0, tiled=True
        ).astype(jnp.float32),
        lax.psum_scatter(
            grad_out_w.astype(jnp.bfloat16), "wide", scatter_dimension=0, tiled=True
        ).astype(jnp.float32),
        lax.psum_scatter(
            grad_up.astype(jnp.bfloat16), "wide", scatter_dimension=0, tiled=True
        ).astype(jnp.float32),
        lax.psum_scatter(
            grad_down.astype(jnp.bfloat16), "wide", scatter_dimension=0, tiled=True
        ).astype(jnp.float32),
        lax.psum_scatter(
            small_grads.astype(jnp.bfloat16), "wide", scatter_dimension=0, tiled=True
        ).astype(jnp.float32),
    )
    summed = (
        lax.psum(shares[0].astype(jnp.bfloat16), "rows").astype(jnp.float32),
        lax.psum(shares[1].astype(jnp.bfloat16), "rows").astype(jnp.float32),
        lax.psum(shares[2].astype(jnp.bfloat16), "rows").astype(jnp.float32),
        lax.psum(shares[3].astype(jnp.bfloat16), "rows").astype(jnp.float32),
        lax.psum(shares[4].astype(jnp.bfloat16), "rows").astype(jnp.float32),
        lax.psum(shares[5].astype(jnp.bfloat16), "rows").astype(jnp.float32),
    )
    small_sum = summed[5]
    return (
        layer_output.reshape(rows_dev, tok_wide, features),
        input_grad,
        skip_grad,
        summed[0],
        small_sum[:, 0],
        small_sum[:, 1],
        summed[1],
        summed[2],
        small_sum[:, 2],
        small_sum[:, 3],
        summed[3],
        summed[4],
    )


def solution(mesh):
    placed = (
        P("rows", "wide", None),
        P("rows", "wide", None),
        P("rows", None),
        P("rows", None),
        P("wide", None),
        P("wide"),
        P("wide"),
        P("wide", None),
        P("wide", None),
        P("wide"),
        P("wide"),
        P("wide", None),
        P("wide", None),
        P("rows", "wide", None),
    )
    return jax.shard_map(
        on_device,
        mesh=mesh,
        in_specs=placed,
        out_specs=(
            P("rows", "wide", None),
            P("rows", "wide", None),
            P("rows", "wide", None),
            P("wide", None),
            P("wide"),
            P("wide"),
            P("wide", None),
            P("wide", None),
            P("wide"),
            P("wide"),
            P("wide", None),
            P("wide", None),
        ),
        check_vma=False,
    )
```

profile of v0, /device:TPU:0, one launch (start us, length us, event | category | flops | bytes accessed | tf_op | source)
XLA Modules:
  0.0 2148.0 jit_solution(6429273783510494325)
XLA Ops:
  12.3 18.3 all-reduce.5
  30.6 44.1 %all-gather.6.cloned.1.call-done = bf16[2304,1152]{1,0:T(8,128)(2,1)} async-done(((bf16[576,1152]{1,0:T(8,128)(2,1)}), bf16[2304,1152]{1,0:T(8,128)(2,1)}) %all-gather.6.cloned.1.call-update) | async-done | bytes 5308432 | tf_op jit(solution)/shard_map/all_gather | solution.py:161
  74.7 8.3 fusion.51
  85.6 75.0 %all-gather.8.cloned.1.call-done = bf16[1152,3456]{1,0:T(8,128)(2,1)} async-done(((bf16[288,3456]{1,0:T(8,128)(2,1)}), bf16[1152,3456]{1,0:T(8,128)(2,1)}) %all-gather.8.cloned.1.call-update) | async-done | bytes 7962640 | tf_op jit(solution)/shard_map/all_gather | solution.py:162
  160.7 13.9 convolution_convert_fusion.5
  174.6 9.0 copy.68
  183.6 19.4 copy.69
  203.0 5.8 all-to-all-start
  210.8 126.7 %all-to-all-done = bf16[1,832,3,1152]{1,2,0,3:T(4,128)(2,1)} async-done(((bf16[1,832,3,1152]{1,2,0,3:T(4,128)(2,1)}), bf16[1,832,3,1152]{1,2,0,3:T(4,128)(2,1)}, u32[]{:S(2)}, u32[]{:S(2)}) %all-to-all-start) | async-done | bytes 5750816 | tf_op jit(solution)/shard_map/all_to_all | solution.py:188
  347.5 11.6 all_to_all.49
  376.6 246.3 %while.50 = (s32[]{:T(128)}, bf16[4,3328,72]{1,2,0:T(8,128)(2,1)}, f32[4,3328]{1,0:T(4,128)}, bf16[4,3328,72]{2,1,0:T(8,128)(2,1)}, s32[4,3328]{1,0:T(4,128)}, /...) while((s32[]{:T(128)}, bf16[4,3328,72]{1,2,0:T(8,128)(2,1)}, ...), condition=%wide.region_8.9_spmd, body=%wide.region_3.8_spmd.sunk | while | flops 828019712 | bytes 85530184 | solution.py:199
  380.5 55.0 %while.53 = (s32[]{:T(128)}, bf16[4,832,72]{1,2,0:T(8,128)(2,1)S(1)}, f32[4,832]{1,0:T(4,128)S(1)}, s32[4,832]{1,0:T(4,128)S(1)}, s32[3328]{0:T(1024)S(1)}, /*in...) while((s32[]{:T(128)}, ...), condition=%wide.region_7.7_spmd, body=%wide.region_4.6_spmd.sunk | while | flops 828019712 | bytes 79658840 | solution.py:83
  387.8 6.3 fusion.114
  401.9 6.3 fusion.114
  415.5 6.3 fusion.114
  429.1 6.3 fusion.114
  442.4 54.5 %while.53 = (s32[]{:T(128)}, bf16[4,832,72]{1,2,0:T(8,128)(2,1)S(1)}, f32[4,832]{1,0:T(4,128)S(1)}, s32[4,832]{1,0:T(4,128)S(1)}, s32[3328]{0:T(1024)S(1)}, /*in...) while((s32[]{:T(128)}, ...), condition=%wide.region_7.7_spmd, body=%wide.region_4.6_spmd.sunk | while | flops 828019712 | bytes 79658840 | solution.py:83
  449.7 6.3 fusion.114
  463.3 6.3 fusion.114
  477.0 6.3 fusion.114
  490.6 6.3 fusion.114
  503.9 54.5 %while.53 = (s32[]{:T(128)}, bf16[4,832,72]{1,2,0:T(8,128)(2,1)S(1)}, f32[4,832]{1,0:T(4,128)S(1)}, s32[4,832]{1,0:T(4,128)S(1)}, s32[3328]{0:T(1024)S(1)}, /*in...) while((s32[]{:T(128)}, ...), condition=%wide.region_7.7_spmd, body=%wide.region_4.6_spmd.sunk | while | flops 828019712 | bytes 79658840 | solution.py:83
  511.2 6.3 fusion.114
  524.8 6.3 fusion.114
  538.4 6.3 fusion.114
  552.1 6.3 fusion.114
  565.3 54.5 %while.53 = (s32[]{:T(128)}, bf16[4,832,72]{1,2,0:T(8,128)(2,1)S(1)}, f32[4,832]{1,0:T(4,128)S(1)}, s32[4,832]{1,0:T(4,128)S(1)}, s32[3328]{0:T(1024)S(1)}, /*in...) while((s32[]{:T(128)}, ...), condition=%wide.region_7.7_spmd, body=%wide.region_4.6_spmd.sunk | while | flops 828019712 | bytes 79658840 | solution.py:83
  572.7 6.3 fusion.114
  586.3 6.3 fusion.114
  599.9 6.3 fusion.114
  613.5 6.3 fusion.114
  622.9 11.9 copy.76
  635.3 21.6 %reduce.34 = bf16[3328,288]{1,0:T(8,128)(2,1)S(1)} reduce(bf16[3328,1,288]{2,1,0:T(2,128)(2,1)} %bitcast.197, bf16[]{:T(256)} %broadcast.181), dimensions={1}, to_apply=%bitcast.109.reduce_sub_computation | reduce | bytes 3833858
  665.2 21.8 %all-to-all-done.1 = bf16[4,2,119808]{2,1,0:T(2,128)(2,1)S(1)} async-done(((bf16[4,2,119808]{2,1,0:T(2,128)(2,1)}), bf16[4,2,119808]{2,1,0:T(2,128)(2,1)S(1)}, u32[]{:S(2)}, u32[]{:S(2)}) %all-to-all-start.1) | async-done | bytes 1916960 | tf_op jit(solution)/shard_map/all_to_all | solution.py:203
  692.5 12.0 copy.77
  710.5 6.8 fusion.52
  719.8 48.2 %multiply_convert_fusion.1 = (bf16[832,4608]{1,0:T(8,128)(2,1)}, f32[832,4608]{1,0:T(8,128)}, f32[832,4608]{1,0:T(8,128)}) fusion(bf16[1152,4608]{1,0:T(8,128)(2,1)} %all-gather.12.cloned.1.call-done, f32[832,1152]{1,0:T(8,128)} %copy-done.8, f32[1152]{0:T(1024)S(1)} %convert_element_type.126, f32[1152]{0:T(1024)S(1)} %convert_element_type.125, ...), kind=kOutput, calls=%fused_computation.63 | convolution fusion | flops 9087197184 | bytes 52805120 | tf_op jit(solution)/shard_map/dot_general | solution.py:209
  768.0 24.4 %add_convert_fusion = bf16[832,4608]{1,0:T(8,128)(2,1)} fusion(f32[832,4608]{1,0:T(8,128)} %get-tuple-element.422, f32[832,4608]{1,0:T(8,128)} %get-tuple-element.440, bf16[4608,1152]{1,0:T(8,128)(2,1)} %all-gather.14.cloned.1.call-done, bf16[1,832,1152]{2,1,0:T(8,128)(2,1)S(1)} %copy-done.13), kind=kOutput, calls=%fused_computation.62 | convolution fusion | flops 8886878208 | bytes 50872320 | tf_op jit(solution)/shard_map/te,de->td/dot_general | solution.py:33
  792.4 19.7 multiply_reduce_fusion.1
  818.6 8.4 copy.79
  827.1 13.2 reduce.35
  847.2 22.3 %all-to-all-done.2 = bf16[4,2,119808]{2,1,0:T(2,128)(2,1)S(1)} async-done(((bf16[4,2,119808]{2,1,0:T(2,128)(2,1)}), bf16[4,2,119808]{2,1,0:T(2,128)(2,1)S(1)}, u32[]{:S(2)}, u32[]{:S(2)}) %all-to-all-start.2) | async-done | bytes 1916960 | tf_op jit(solution)/shard_map/all_to_all | solution.py:231
  880.2 460.8 %while.52 = (s32[]{:T(128)}, bf16[4,3,3328,72]{2,3,0,1:T(8,128)(2,1)}, bf16[4,3328,72]{2,1,0:T(8,128)(2,1)}, bf16[4,3328,72]{1,2,0:T(8,128)(2,1)}, f32[4,3328]{1...) while((s32[]{:T(128)}, ...), condition=%wide.region_17.18_spmd, body=%wide.region_13.17_spmd.sunk | while | flops 2033001984 | bytes 213637568 | solution.py:233
  889.2 104.3 %while.54 = (s32[]{:T(128)}, f32[3328,72]{0,1:T(8,128)S(1)}, f32[3328,72]{0,1:T(8,128)S(1)}, bf16[4,832,72]{1,2,0:T(8,128)(2,1)S(1)}, s32[4,832]{1,0:T(4,128)S(1...) while((s32[]{:T(128)}, f32[3328,72]{0,1:T(8,128)S(1)}, ...), condition=%wide.region_16.16_spmd.clone, body=%wide.region_14.15_spmd.clone.sunk | while | flops 2028209664 | bytes 201003664 | solution.py:140
  1004.4 104.3 %while.54 = (s32[]{:T(128)}, f32[3328,72]{0,1:T(8,128)S(1)}, f32[3328,72]{0,1:T(8,128)S(1)}, bf16[4,832,72]{1,2,0:T(8,128)(2,1)S(1)}, s32[4,832]{1,0:T(4,128)S(1...) while((s32[]{:T(128)}, f32[3328,72]{0,1:T(8,128)S(1)}, ...), condition=%wide.region_16.16_spmd.clone, body=%wide.region_14.15_spmd.clone.sunk | while | flops 2028209664 | bytes 201003664 | solution.py:140
  1119.5 104.2 %while.54 = (s32[]{:T(128)}, f32[3328,72]{0,1:T(8,128)S(1)}, f32[3328,72]{0,1:T(8,128)S(1)}, bf16[4,832,72]{1,2,0:T(8,128)(2,1)S(1)}, s32[4,832]{1,0:T(4,128)S(1...) while((s32[]{:T(128)}, f32[3328,72]{0,1:T(8,128)S(1)}, ...), condition=%wide.region_16.16_spmd.clone, body=%wide.region_14.15_spmd.clone.sunk | while | flops 2028209664 | bytes 201003664 | solution.py:140
  1234.6 104.3 %while.54 = (s32[]{:T(128)}, f32[3328,72]{0,1:T(8,128)S(1)}, f32[3328,72]{0,1:T(8,128)S(1)}, bf16[4,832,72]{1,2,0:T(8,128)(2,1)S(1)}, s32[4,832]{1,0:T(4,128)S(1...) while((s32[]{:T(128)}, f32[3328,72]{0,1:T(8,128)S(1)}, ...), condition=%wide.region_16.16_spmd.clone, body=%wide.region_14.15_spmd.clone.sunk | while | flops 2028209664 | bytes 201003664 | solution.py:140
  1340.9 16.2 copy.86
  1357.1 6.1 all-to-all-start.3
  1363.3 6.5 convolution_convert_fusion.4
  1369.8 126.1 %all-to-all-done.3 = bf16[1,3328,3,288]{3,2,0,1:T(4,128)(2,1)} async-done(((bf16[1,3328,3,288]{3,2,0,1:T(4,128)(2,1)}), bf16[1,3328,3,288]{3,2,0,1:T(4,128)(2,1)}, u32[]{:S(2)}, u32[]{:S(2)}) %all-to-all-start.3) | async-done | bytes 5750816 | tf_op jit(solution)/shard_map/all_to_all | solution.py:242
  1496.0 16.5 copy.87
  1512.5 15.4 multiply_reduce_fusion.2
  1531.0 8.0 convolution_convert_fusion.3
  1539.7 17.5 convolution_convert_fusion.1
  1558.8 18.1 convolution_convert_fusion
  1577.6 14.9 convolution_convert_fusion.2
  1594.2 7.1 reduce-scatter.9.cloned.1.call-done
  1601.3 107.7 %reduce-scatter.15.cloned.1.call-done = bf16[288,4608]{1,0:T(8,128)(2,1)} async-done(((bf16[1152,4608]{1,0:T(8,128)(2,1)}), bf16[288,4608]{1,0:T(8,128)(2,1)}) %reduce-scatter.15.cloned.1.call-update) | async-done | bytes 2654224 | tf_op jit(solution)/shard_map/reduce_scatter | solution.py:266
  1709.1 107.7 %reduce-scatter.17.cloned.1.call-done = bf16[1152,1152]{1,0:T(8,128)(2,1)} async-done(((bf16[4608,1152]{1,0:T(8,128)(2,1)}), bf16[1152,1152]{1,0:T(8,128)(2,1)}) %reduce-scatter.17.cloned.1.call-update) | async-done | bytes 2654224 | tf_op jit(solution)/shard_map/reduce_scatter | solution.py:269
  1816.8 86.3 %reduce-scatter.11.cloned.1.call-done = bf16[288,3456]{1,0:T(8,128)(2,1)} async-done(((bf16[1152,3456]{1,0:T(8,128)(2,1)}), bf16[288,3456]{1,0:T(8,128)(2,1)}) %reduce-scatter.11.cloned.1.call-update) | async-done | bytes 1990672 | tf_op jit(solution)/shard_map/reduce_scatter | solution.py:260
  1903.2 16.9 fusion.35
  1931.9 16.2 psum.43
  1948.7 179.4 %all-reduce.8.cloned.1.call-done = (bf16[576,1152]{1,0:T(8,128)(2,1)}, bf16[288,3456]{1,0:T(8,128)(2,1)}, bf16[288,1152]{1,0:T(8,128)(2,1)}, bf16[288,4608]{1,0:T(8,128)(2,1)}, bf16[1152,1152]{1,0:T(8,128)(2,1)}) async-done(((bf16[576,1152]{1,0:T(8,128)(2,1)}, bf16[288,3456]{1,0:T(8,128)(2,1)}, bf16[288,1152]{1,0:T(8,128)(2,1)}, bf16[288,4608]{1,0:T(8,128)(2,1)}, bf16[1152,1152]{1,0:T(8,128)(2,1)}), ...) | async-done | bytes 9289744 | tf_op jit(solution)/shard_map/psum | solution.py:277
  (745 shorter events, 720.0 us)
Async XLA Ops:
  7.2 4.4 copy-start.44
  7.2 4.6 copy-start.45
  7.2 4.9 copy-start.46
  7.2 67.5 %copy-start.48 = (bf16[1,832,1152]{2,1,0:T(8,128)(2,1)S(1)}, bf16[1,832,1152]{2,1,0:T(8,128)(2,1)}, u32[]{:S(2)}) copy-start(bf16[1,832,1152]{2,1,0:T(8,128)(2,1)} %param.23) | copy-start | bytes 5750788
  7.2 67.5 %all-gather.6.cloned.1.call-start = ((), (), s32[]{:S(2)}) async-start(), calls=%async_computation.10 | async-start | bytes 6635520 | tf_op jit(solution)/shard_map/all_gather | solution.py:161
  8.0 152.7 %all-gather.8.cloned.1.call-start = ((), (), s32[]{:S(2)}) async-start(), calls=%async_computation.11 | async-start | bytes 9953280 | tf_op jit(solution)/shard_map/all_gather | solution.py:162
  8.7 701.8 %all-gather.10.cloned.1.call-start = ((), (), s32[]{:S(2)}) async-start(), calls=%async_computation.12 | async-start | bytes 3317760 | tf_op jit(solution)/shard_map/all_gather | solution.py:163
  9.5 710.3 %all-gather.12.cloned.1.call-start = ((), (), s32[]{:S(2)}) async-start(), calls=%async_computation.13 | async-start | bytes 13271040 | tf_op jit(solution)/shard_map/all_gather | solution.py:164
  30.6 130.0 %copy-start.26 = (f32[1152]{0:T(1024)}, f32[1152]{0:T(1024)S(1)}, u32[]{:S(2)}) copy-start(f32[1152]{0:T(1024)S(1)} %convert_element_type.121) | copy-start | bytes 13828
  30.6 130.0 %copy-start.35 = (f32[1152]{0:T(1024)}, f32[1152]{0:T(1024)S(1)}, u32[]{:S(2)}) copy-start(f32[1152]{0:T(1024)S(1)} %convert_element_type.122) | copy-start | bytes 13828
  83.1 91.5 %copy-start.22 = (f32[832]{0:T(1024)}, f32[832]{0:T(1024)S(1)}, u32[]{:S(2)}) copy-start(f32[832]{0:T(1024)S(1)} %broadcast_multiply_fusion.5) | copy-start | bytes 9988
  85.6 89.0 %copy-start.30 = (f32[832]{0:T(1024)}, f32[832]{0:T(1024)S(1)}, u32[]{:S(2)}) copy-start(f32[832]{0:T(1024)S(1)} %add_rsqrt_fusion.1) | copy-start | bytes 9988
  203.0 6.4 copy-start.34
  203.0 6.5 copy-start.51
  203.0 134.5 %all-to-all-start = ((bf16[1,832,3,1152]{1,2,0,3:T(4,128)(2,1)}), bf16[1,832,3,1152]{1,2,0,3:T(4,128)(2,1)}, u32[]{:S(2)}, u32[]{:S(2)}) async-start(bf16[1,832,3,1152]{1,2,0,3:T(4,128)(2,1)} %copy.69), calls=%async_computation | async-start | bytes 16515072 | tf_op jit(solution)/shard_map/all_to_all | solution.py:188
  208.9 559.1 %all-gather.14.cloned.1.call-start = ((), (), s32[]{:S(2)}) async-start(), calls=%async_computation.14 | async-start | bytes 13271040 | tf_op jit(solution)/shard_map/all_gather | solution.py:165
  397.1 4.7 copy-start.3
  622.9 34.0 %copy-start.17 = (pred[4,3328]{1,0:T(4,128)(4,1)}, pred[4,3328]{1,0:T(4,128)(4,1)S(1)}, u32[]{:S(2)}) copy-start(pred[4,3328]{1,0:T(4,128)(4,1)S(1)} %get-tuple-element.977) | copy-start | bytes 39940
  657.0 8.1 copy-start.40
  657.0 8.2 copy-start.39
  661.5 25.4 %all-to-all-start.1 = ((bf16[4,2,119808]{2,1,0:T(2,128)(2,1)}), bf16[4,2,119808]{2,1,0:T(2,128)(2,1)S(1)}, u32[]{:S(2)}, u32[]{:S(2)}) async-start(bf16[4,2,119808]{2,1,0:T(2,128)(2,1)} %reshape.343), calls=%async_computation.1 | async-start | bytes 3833856 | tf_op jit(solution)/shard_map/all_to_all | solution.py:203
  665.1 147.0 %copy-start.28 = (f32[1152]{0:T(1024)}, f32[1152]{0:T(1024)S(1)}, u32[]{:S(2)}) copy-start(f32[1152]{0:T(1024)S(1)} %convert_element_type.125) | copy-start | bytes 13828
  665.2 54.6 %copy-start.37 = (f32[1152]{0:T(1024)}, f32[1152]{0:T(1024)S(1)}, u32[]{:S(2)}) copy-start(f32[1152]{0:T(1024)S(1)} %convert_element_type.126) | copy-start | bytes 13828
  717.3 94.8 %copy-start.24 = (f32[832]{0:T(1024)}, f32[832]{0:T(1024)S(1)}, u32[]{:S(2)}) copy-start(f32[832]{0:T(1024)S(1)} %broadcast_multiply_fusion.4) | copy-start | bytes 9988
  719.7 92.4 %copy-start.32 = (f32[832]{0:T(1024)}, f32[832]{0:T(1024)S(1)}, u32[]{:S(2)}) copy-start(f32[832]{0:T(1024)S(1)} %add_rsqrt_fusion) | copy-start | bytes 9988
  719.7 48.3 %copy-start.13 = (bf16[1,832,1152]{2,1,0:T(8,128)(2,1)S(1)}, bf16[1,832,1152]{2,1,0:T(8,128)(2,1)}, u32[]{:S(2)}) copy-start(bf16[1,832,1152]{2,1,0:T(8,128)(2,1)} %param.35) | copy-start | bytes 5750788
  768.0 24.4 %copy-start.9 = (f32[832,1152]{1,0:T(8,128)S(1)}, f32[832,1152]{1,0:T(8,128)}, u32[]{:S(2)}) copy-start(f32[832,1152]{1,0:T(8,128)} %copy-done.8) | copy-start | bytes 11501572
  843.6 26.0 %all-to-all-start.2 = ((bf16[4,2,119808]{2,1,0:T(2,128)(2,1)}), bf16[4,2,119808]{2,1,0:T(2,128)(2,1)S(1)}, u32[]{:S(2)}, u32[]{:S(2)}) async-start(bf16[4,2,119808]{2,1,0:T(2,128)(2,1)} %reshape.345), calls=%async_computation.2 | async-start | bytes 3833856 | tf_op jit(solution)/shard_map/all_to_all | solution.py:231
  905.5 7.5 copy-start.1
  931.5 7.5 copy-start.1
  957.6 7.5 copy-start.1
  983.6 7.5 copy-start.1
  1020.6 7.5 copy-start.1
  1046.7 4.3 copy-start.2
  1046.7 7.5 copy-start.1
  1072.7 7.5 copy-start.1
  1098.8 7.5 copy-start.1
  1135.7 7.5 copy-start.1
  1161.8 7.5 copy-start.1
  1187.9 7.5 copy-start.1
  1213.9 7.5 copy-start.1
  1250.9 7.5 copy-start.1
  1277.0 7.5 copy-start.1
  1303.0 7.5 copy-start.1
  1329.1 7.5 copy-start.1
  1357.1 6.1 copy-start.11
  1357.1 138.8 %all-to-all-start.3 = ((bf16[1,3328,3,288]{3,2,0,1:T(4,128)(2,1)}), bf16[1,3328,3,288]{3,2,0,1:T(4,128)(2,1)}, u32[]{:S(2)}, u32[]{:S(2)}) async-start(bf16[1,3328,3,288]{3,2,0,1:T(4,128)(2,1)} %copy.86), calls=%async_computation.3 | async-start | bytes 20447232 | tf_op jit(solution)/shard_map/all_to_all | solution.py:242
  1363.2 231.0 %reduce-scatter.13.cloned.1.call-start = ((), (), s32[]{:S(2)}) async-start(), calls=%async_computation.17 | async-start | bytes 3317760 | tf_op jit(solution)/shard_map/reduce_scatter | solution.py:263
  1369.8 231.5 %reduce-scatter.9.cloned.1.call-start = ((), (), s32[]{:S(2)}) async-start(), calls=%async_computation.15 | async-start | bytes 6635520 | tf_op jit(solution)/shard_map/reduce_scatter | solution.py:257
  1496.0 16.5 copy-start.23
  1496.0 16.5 copy-start.27
  1496.0 16.5 copy-start.31
  1512.5 15.5 copy-start.5
  1512.5 15.5 copy-start.7
  1539.0 170.1 %reduce-scatter.15.cloned.1.call-start = ((), (), s32[]{:S(2)}) async-start(), calls=%async_computation.18 | async-start | bytes 13271040 | tf_op jit(solution)/shard_map/reduce_scatter | solution.py:266
  1557.3 259.6 %reduce-scatter.17.cloned.1.call-start = ((), (), s32[]{:S(2)}) async-start(), calls=%async_computation.19 | async-start | bytes 13271040 | tf_op jit(solution)/shard_map/reduce_scatter | solution.py:269
  1576.9 326.2 %reduce-scatter.11.cloned.1.call-start = ((), (), s32[]{:S(2)}) async-start(), calls=%async_computation.16 | async-start | bytes 9953280 | tf_op jit(solution)/shard_map/reduce_scatter | solution.py:260
  1592.5 338.4 %reduce-scatter.19.cloned.1.call-start = ((), (), s32[]{:S(2)}) async-start(), calls=%async_computation.20 | async-start | bytes 368640
  1594.2 534.0 %all-reduce.8.cloned.1.call-start = ((), (), s32[]{:S(2)}) async-start(), calls=%async_computation.21 | async-start | bytes 18579456 | tf_op jit(solution)/shard_map/psum | solution.py:277
  1903.1 17.0 slice-start
  1903.1 17.0 copy-start.16
  1903.2 17.0 slice-start.1
  2128.1 4.9 copy-start.10
  2133.1 5.1 copy-start.20
  (70 other events, 242.5 us)
Sparse Core Ops, SparseCore 0:
  9.9 64.7 all-gather.5
  76.5 84.0 all-gather.7
  162.5 39.9 all-gather.9
  204.1 181.4 all-gather.11
  387.3 106.1 all-gather.13
  1369.9 102.7 reduce-scatter.12
  1539.1 62.1 reduce-scatter.8
  1604.4 104.5 reduce-scatter.14
  1712.2 104.5 reduce-scatter.16
  1819.8 83.2 reduce-scatter.10
  1906.7 24.1 reduce-scatter.18
  1933.8 194.3 all-reduce.7
where the time goes:
time: 2160 us; the launch traced here: 2150 us
  waiting for transfers between devices  909 us (42%)
  matrix products  637 us (29%)
  local copies, waits for them, and re-layouts  383 us (18%)
  other arithmetic  146 us (7%)
  blocking collectives  34.5 us (2%)
    psum x1, waiting for transfers between devices, on_device(): lax.psum(shares[0].astype(jnp.bfloat16), 'rows').astype(jnp.float32)  179 us
    while x136, local copies, waits for them, and re-layouts  133 us
    dot_general x32, matrix products, one_block(): jnp.einsum('qd,kd->qk', query_blk, key_rows, preferred_element_type=jnp.f...  132 us
    all_to_all x1, waiting for transfers between devices, on_device(): lax.all_to_all(qkv_local, 'wide', split_axis=3, concat_axis=1, tiled=True)  127 us
    all_to_all x1, waiting for transfers between devices, on_device(): lax.all_to_all(stacked, 'wide', split_axis=1, concat_axis=3, tiled=True)  126 us
    reduce_scatter x1, waiting for transfers between devices, on_device(): lax.psum_scatter(grad_down.astype(jnp.bfloat16), 'wide', scatter_dimensio...  108 us
    reduce_scatter x1, waiting for transfers between devices, on_device(): lax.psum_scatter(grad_up.astype(jnp.bfloat16), 'wide', scatter_dimension=...  108 us
    dot_general x16, matrix products, one_block(): jnp.dot(softmax_out, value_rows, preferred_element_type=jnp.float32)  101 us
  transfers between devices with their start and end apart: 16, of which 12 were waited for; matrix products, arithmetic and copies ran while one was open for 25% of the time, Pallas kernels for 0%

commit v1 on v0

v1 whole, which is shorter than its diff:
```python
import functools
import jax, jax.numpy as jnp
from jax import lax
from jax.experimental import pallas as pl
from jax.experimental.pallas import tpu as pltpu
HEAD=72; SHORT=258; LONG=1026; NITEM=12
LOG2E=1.4426950408889634
SCALE=HEAD**-0.5
QT=384

def kwin(n): return (n + 29 + 31)//32*32
def qwin(n): return (n + 15 + QT-1)//QT*QT

def nt(a,b): return lax.dot_general(a,b,(((1,),(1,)),((),())),preferred_element_type=jnp.float32)
def nn(a,b): return lax.dot_general(a,b,(((1,),(0,)),((),())),preferred_element_type=jnp.float32)
def tn(a,b): return lax.dot_general(a,b,(((0,),(0,)),((),())),preferred_element_type=jnp.float32)

def windows(start, size, row_len):
    k0 = pl.multiple_of(jnp.minimum(start//16*16, row_len-kwin(size)),16)
    q0 = pl.multiple_of(jnp.minimum(start//16*16, row_len-qwin(size)),16)
    return k0,q0

def split_heads(src_ref, dst_ref, count, chunk=416):
    rows=src_ref.shape[0]
    @pl.loop(0, rows//chunk)
    def _(i):
        r=pl.ds(pl.multiple_of(i*chunk,16),chunk)
        block=src_ref[r,:]
        for j in range(count):
            dst_ref[j,r,:]=block[:,j*HEAD:(j+1)*HEAD]

def join_heads(src_ref, dst_ref, count, chunk=416):
    rows=dst_ref.shape[0]
    @pl.loop(0, rows//chunk)
    def _(i):
        r=pl.ds(pl.multiple_of(i*chunk,16),chunk)
        dst_ref[r,:]=jnp.concatenate([src_ref[j,r,:] for j in range(count)],axis=1)

def zero(ref, chunk=416):
    rows=ref.shape[1]
    @pl.loop(0, rows//chunk)
    def _(i):
        r=pl.ds(pl.multiple_of(i*chunk,16),chunk)
        for j in range(ref.shape[0]):
            ref[j,r,:]=jnp.zeros((chunk,ref.shape[2]),ref.dtype)

def for_items(len_ref, one):
    def step(i, start):
        size=len_ref[0,i]
        @pl.when(size==LONG)
        def _(): one(i,start,LONG)
        @pl.when(size==SHORT)
        def _(): one(i,start,SHORT)
        return start+size
    lax.fori_loop(0,len_ref.shape[1],step,jnp.int32(0))

def mask_edges(values, start, k0, size, fill):
    n=values.shape[0]; body=size//32*32
    off=start-k0
    top=lax.broadcasted_iota(jnp.int32,(32,values.shape[1]),0)
    low=jnp.where(top>=off,values[:32],fill)
    high=jnp.where(top+body<off+size,values[body:],fill)
    return jnp.concatenate([low,values[32:body],high],axis=0)

def attend_kernel(heads, len_ref, qkv_ref, out_ref, lse_ref, split_ref, acc_ref):
    row_len=qkv_ref.shape[0]
    split_heads(qkv_ref, split_ref, 3*heads)
    zero(acc_ref)
    lse_ref[...]=jnp.zeros_like(lse_ref)
    def one(item,start,size):
        k0,q0=windows(start,size,row_len)
        kr=pl.ds(k0,kwin(size))
        @pl.loop(0,qwin(size)//QT)
        def _(t):
            qr=pl.ds(pl.multiple_of(q0+t*QT,16),QT)
            col=q0+t*QT+lax.broadcasted_iota(jnp.int32,(1,QT),1)
            live=(col>=start)&(col<start+size)
            for h in range(heads):
                s=nt(split_ref[heads+h,kr,:],split_ref[h,qr,:])
                s=mask_edges(s,start,k0,size,-1e30)
                m=jnp.max(s,axis=0,keepdims=True)
                p=jnp.exp2((s-m)*(SCALE*LOG2E))
                l=jnp.sum(p,axis=0,keepdims=True)
                o=tn(split_ref[2*heads+h,kr,:],p.astype(jnp.bfloat16))
                o=jnp.where(live,o/l,0.0)
                acc_ref[h,qr,:]+=o.T.astype(jnp.bfloat16)
                lse_ref[item,pl.ds(t*heads+h,1),:]=m*(SCALE*LOG2E)+jnp.log2(l)
    for_items(len_ref,one)
    join_heads(acc_ref,out_ref,heads)

def attend_back_kernel(heads, len_ref, qkv_ref, grad_ref, lse_ref, out_ref, split_ref, gsplit_ref, acc_ref, dk_ref, dv_ref):
    row_len=qkv_ref.shape[0]
    split_heads(qkv_ref, split_ref, 3*heads)
    split_heads(grad_ref, gsplit_ref, heads)
    zero(acc_ref)
    def one(item,start,size):
        k0,q0=windows(start,size,row_len)
        kw=kwin(size)
        kr=pl.ds(k0,kw)
        for h in range(heads):
            dk_ref[h,:kw,:]=jnp.zeros((kw,HEAD),jnp.float32)
            dv_ref[h,:kw,:]=jnp.zeros((kw,HEAD),jnp.float32)
        @pl.loop(0,qwin(size)//QT)
        def _(t):
            qr=pl.ds(pl.multiple_of(q0+t*QT,16),QT)
            col=q0+t*QT+lax.broadcasted_iota(jnp.int32,(1,QT),1)
            live=(col>=start)&(col<start+size)
            for h in range(heads):
                k=split_ref[heads+h,kr,:]; q=split_ref[h,qr,:]; g=gsplit_ref[h,qr,:]
                lse=jnp.where(live,lse_ref[item,pl.ds(t*heads+h,1),:],1e30)
                s=nt(k,q)
                p=jnp.exp2(s*(SCALE*LOG2E)-lse)
                p=mask_edges(p,start,k0,size,0.0)
                dv_ref[h,:kw,:]+=nn(p.astype(jnp.bfloat16),g)
                dp=nt(split_ref[2*heads+h,kr,:],g)
                delta=jnp.sum(p*dp,axis=0,keepdims=True)
                ds=(p*(dp-delta)).astype(jnp.bfloat16)
                dk_ref[h,:kw,:]+=nn(ds,q)
                dq=tn(k,ds)*SCALE
                acc_ref[h,qr,:]+=dq.T.astype(jnp.bfloat16)
        for h in range(heads):
            acc_ref[heads+h,kr,:]+=(dk_ref[h,:kw,:]*SCALE).astype(jnp.bfloat16)
            acc_ref[2*heads+h,kr,:]+=dv_ref[h,:kw,:].astype(jnp.bfloat16)
    for_items(len_ref,one)
    join_heads(acc_ref,out_ref,3*heads)

VM=pl.BlockSpec(memory_space=pltpu.VMEM); SM=pl.BlockSpec(memory_space=pltpu.SMEM)
def attend(lens,qkv,heads):
    n=qkv.shape[0]
    nt_=heads*(qwin(LONG)//QT)
    return pl.pallas_call(functools.partial(attend_kernel,heads),
      out_shape=(jax.ShapeDtypeStruct((n,heads*HEAD),jnp.bfloat16),jax.ShapeDtypeStruct((NITEM,nt_,QT),jnp.float32)),
      in_specs=[SM,VM],out_specs=(VM,VM),
      scratch_shapes=[pltpu.VMEM((3*heads,n,HEAD),jnp.bfloat16),pltpu.VMEM((heads,n,HEAD),jnp.bfloat16)],
      compiler_params=pltpu.CompilerParams(vmem_limit_bytes=56*2**20))(lens,qkv)
def attend_back(lens,qkv,grad,lse,heads):
    n=qkv.shape[0]
    return pl.pallas_call(functools.partial(attend_back_kernel,heads),
      out_shape=jax.ShapeDtypeStruct((n,3*heads*HEAD),jnp.bfloat16),
      in_specs=[SM,VM,VM,VM],out_specs=VM,
      scratch_shapes=[pltpu.VMEM((3*heads,n,HEAD),jnp.bfloat16),pltpu.VMEM((heads,n,HEAD),jnp.bfloat16),pltpu.VMEM((3*heads,n,HEAD),jnp.bfloat16),
        pltpu.VMEM((heads,kwin(LONG),HEAD),jnp.float32),pltpu.VMEM((heads,kwin(LONG),HEAD),jnp.float32)],
      compiler_params=pltpu.CompilerParams(vmem_limit_bytes=60*2**20))(lens,qkv,grad,lse)


F32=jnp.float32; BF=jnp.bfloat16
ANY=pl.BlockSpec(memory_space=pl.ANY)

def gelu_parts(u):
    z=jnp.exp2(u*u*(-0.5*1.4426950408889634))
    t=1.0/(1.0+(0.3275911*0.7071067811865476)*jnp.abs(u))
    poly=((((1.061405429*t-1.453152027)*t+1.421413741)*t-0.284496736)*t+0.254829592)*t
    tail=0.5*poly*z
    cdf=jnp.where(u>=0,1.0-tail,tail)
    return u*cdf, cdf+u*(z*0.3989422804014327)

def mlp_kernel(tile, hidden_ref, att_ref, outw_ref, gain_ref, shift_ref, g_ref, upo_ref, uph_ref, dno_ref, dnh_ref,
               lay_ref, gmid_ref, gatt_ref, gow_ref, small_ref, gupo_ref, guph_ref, gdno_ref, gdnh_ref,
               att_s, n2_s, xhat_s, rstd_s, act_s, gu_s, upb, dnb, gub, gdb, in_sem, out_sem):
    parts,tokens,cols=att_ref.shape
    d=hidden_ref.shape[1]
    tc=tokens//2 if tokens>416 else tokens
    nch=tokens//tc
    half=upo_ref.shape[1]; steps=half//tile
    cc=d//3; fc=256

    def fetch(j,act):
        slot=lax.rem(j,2)
        for first,(us,ds) in ((True,(uph_ref,dnh_ref)),(False,(upo_ref,dno_ref))):
            cond=(j<steps) if first else (j>=steps)
            @pl.when(cond)
            def _():
                k=j if first else j-steps
                off=pl.multiple_of(k*tile,tile)
                act(pltpu.make_async_copy(us.at[:,pl.ds(off,tile)],upb.at[slot],in_sem.at[slot,0]))
                act(pltpu.make_async_copy(ds.at[pl.ds(off,tile),:],dnb.at[slot],in_sem.at[slot,1]))
    def flush(j,act):
        slot=lax.rem(j,2)
        for first,(us,ds) in ((True,(guph_ref,gdnh_ref)),(False,(gupo_ref,gdno_ref))):
            cond=(j<steps) if first else (j>=steps)
            @pl.when(cond)
            def _():
                k=j if first else j-steps
                off=pl.multiple_of(k*tile,tile)
                act(pltpu.make_async_copy(gub.at[slot],us.at[:,pl.ds(off,tile)],out_sem.at[slot,0]))
                act(pltpu.make_async_copy(gdb.at[slot],ds.at[pl.ds(off,tile),:],out_sem.at[slot,1]))
    start=lambda c: c.start()
    wait=lambda c: c.wait()
    fetch(jnp.int32(0),start)
    gain=gain_ref[...]; shift=shift_ref[...]
    sub=tc//2
    @pl.loop(0,2*nch)
    def _(i):
        r=pl.ds(pl.multiple_of(i*sub,16),sub)
        joined=jnp.concatenate([att_ref[p,r,:] for p in range(parts)],axis=1)
        att_s[r,:]=joined
        mid=hidden_ref[r,:]+nn(joined,outw_ref[...])
        lay_ref[r,:]=mid
        cen=mid-jnp.mean(mid,axis=1,keepdims=True)
        inv=lax.rsqrt(jnp.mean(cen*cen,axis=1,keepdims=True)+1e-5)
        xhat=cen*inv
        xhat_s[r,:]=xhat
        rstd_s[r,:]=jnp.broadcast_to(inv,(sub,128))
        n2_s[r,:]=(xhat*gain+shift).astype(BF)
        gmid_ref[r,:]=jnp.zeros((sub,d),F32)
    @pl.loop(0,2*steps)
    def _(j):
        slot=lax.rem(j,2)
        @pl.when(j+1<2*steps)
        def _(): fetch(j+1,start)
        fetch(j,wait)
        @pl.when(j>=2)
        def _(): flush(j-2,wait)
        @pl.loop(0,nch)
        def _(i):
            r=pl.ds(pl.multiple_of(i*tc,16),tc)
            for k in range(tile//fc):
                f=pl.ds(k*fc,fc)
                u=nn(n2_s[r,:],upb[slot,:,f])
                a,dg=gelu_parts(u)
                act_s[r,f]=a.astype(BF)
                ga=nt(g_ref[r,:],dnb[slot,f,:])
                gu_s[r,f]=(ga*dg).astype(BF)
        @pl.loop(0,nch)
        def _(i):
            r=pl.ds(pl.multiple_of(i*tc,16),tc)
            for k in range(3):
                cr=pl.ds(k*cc,cc)
                lay_ref[r,cr]+=nn(act_s[r,:],dnb[slot,:,cr])
                gmid_ref[r,cr]+=nt(gu_s[r,:],upb[slot,cr,:])
        for k in range(tile//fc):
            f=pl.ds(k*fc,fc)
            gdb[slot,f,:]=tn(act_s[:,f],g_ref[...]).astype(BF)
        for k in range(3):
            cr=pl.ds(k*cc,cc)
            gub[slot,cr,:]=tn(n2_s[:,cr],gu_s[...]).astype(BF)
        flush(j,start)
    small_ref[...]=jnp.zeros_like(small_ref)
    @pl.loop(0,2*nch)
    def _(i):
        r=pl.ds(pl.multiple_of(i*sub,16),sub)
        gs=gmid_ref[r,:]; xhat=xhat_s[r,:]
        small_ref[0:1,:]+=jnp.sum(gs*xhat,axis=0,keepdims=True)
        small_ref[1:2,:]+=jnp.sum(gs,axis=0,keepdims=True)
        e=gs*gain
        back=e-jnp.mean(e,axis=1,keepdims=True)-xhat*jnp.mean(e*xhat,axis=1,keepdims=True)
        gm=g_ref[r,:].astype(F32)+back*rstd_s[r,0:1]
        gmid_ref[r,:]=gm
        low=gm.astype(BF)
        n2_s[r,:]=low
        ga=nt(low,outw_ref[...]).astype(BF)
        for p in range(parts):
            gatt_ref[p,r,:]=ga[:,p*cols:(p+1)*cols]
    for k in range(3):
        cr=pl.ds(k*cc,cc)
        gow_ref[cr,:]=tn(att_s[:,cr],n2_s[...]).astype(BF)
    flush(jnp.int32(2*steps-2),wait)
    flush(jnp.int32(2*steps-1),wait)

def mlp(hidden,att,outw,gain,shift,g,upo,uph,dno,dnh):
    tokens,d=hidden.shape; half=upo.shape[1]; tile=half//3
    S=jax.ShapeDtypeStruct
    flops=2*tokens*d*(half*2*6+d*3)
    return pl.pallas_call(functools.partial(mlp_kernel,tile),
        out_shape=(S((tokens,d),F32),S((tokens,d),F32),S(att.shape,BF),S((d,d),BF),S((8,d),F32),
                   S(upo.shape,BF),S(upo.shape,BF),S(dno.shape,BF),S(dno.shape,BF)),
        in_specs=[VM]*6+[ANY]*4,
        out_specs=(VM,)*5+(ANY,)*4,
        scratch_shapes=[pltpu.VMEM((tokens,d),BF),pltpu.VMEM((tokens,d),BF),pltpu.VMEM((tokens,d),F32),pltpu.VMEM((tokens,128),F32),
            pltpu.VMEM((tokens,tile),BF),pltpu.VMEM((tokens,tile),BF),
            pltpu.VMEM((2,d,tile),BF),pltpu.VMEM((2,tile,d),BF),pltpu.VMEM((2,d,tile),BF),pltpu.VMEM((2,tile,d),BF),
            pltpu.SemaphoreType.DMA((2,2)),pltpu.SemaphoreType.DMA((2,2))],
        compiler_params=pltpu.CompilerParams(vmem_limit_bytes=62*2**20),
        cost_estimate=pl.CostEstimate(flops=flops,bytes_accessed=60*2**20,transcendentals=tokens*half*2))(
        hidden,att,outw,gain,shift,g,upo,uph,dno,dnh)


from jax.sharding import Mesh, PartitionSpec as P
WIDE=("y","x"); ROWS=("z","core")
SWAP=[(0,1),(1,0)]

def swap_cores(values):
    return lax.ppermute(values,"core",SWAP)

def pick(values, index, axis):
    return lax.dynamic_index_in_dim(values,index,axis,keepdims=False)

def place_halves(mine, other, core, axis):
    first=jnp.where(core==0,mine,other); second=jnp.where(core==0,other,mine)
    return jnp.stack([first,second],axis=axis)

def dot(a,b): return jnp.dot(a,b,preferred_element_type=F32)

def norm(values):
    cen=values-jnp.mean(values,axis=1,keepdims=True)
    inv=lax.rsqrt(jnp.mean(cen*cen,axis=1,keepdims=True)+1e-5)
    return cen*inv,inv

def on_device(nw, block_input, long_skip, segment_ids, item_lengths, skip_weight, first_gain, first_shift, qkv_weight,
              out_weight, second_gain, second_shift, up_weight, down_weight, output_grad):
    core=lax.axis_index("core")
    _,tokens,d=block_input.shape
    heads=qkv_weight.shape[1]//(3*HEAD*nw); hd=heads*HEAD
    ff=up_weight.shape[1]; fb=ff//(2*nw)
    gather=lambda v: lax.all_gather(v,WIDE,axis=0,tiled=True)
    vec=gather(jnp.stack([first_gain,first_shift,second_gain,second_shift],axis=1)).T.astype(F32)
    gain1,shift1,gain2,shift2=[vec[i:i+1] for i in range(4)]
    w_skip=gather(skip_weight)
    joined=jnp.concatenate([block_input[0],long_skip[0]],axis=1)
    w_heads=qkv_weight.reshape(d//nw,3,nw,hd).transpose(2,0,1,3)
    w_heads=lax.all_to_all(w_heads,WIDE,0,0).reshape(d,3*hd)
    hidden=dot(joined,w_skip)
    xhat1,inv1=norm(hidden)
    normed_all=gather((xhat1*gain1+shift1).astype(BF))
    qkv=dot(normed_all,w_heads).astype(BF)
    w_out=gather(out_weight)
    up_mine=gather(pick(up_weight.reshape(d//nw,nw,2,fb),core,2).reshape(d//nw,nw*fb))
    down_mine=gather(pick(down_weight.reshape(2,fb,d),core,0))
    up_other,down_other=swap_cores(up_mine),swap_cores(down_mine)
    att,lse=attend(item_lengths,qkv,heads)
    att=lax.all_to_all(att.reshape(nw,tokens,hd),WIDE,0,0)
    lay,gmid,gatt,gow,small,gupo,guph,gdno,gdnh=mlp(hidden,att,w_out,gain2,shift2,output_grad[0],up_mine,up_other,down_mine,down_other)
    grad_heads=lax.all_to_all(gatt,WIDE,0,0).reshape(nw*tokens,hd)

    def reduce_mine(mine,other):
        both=(mine.astype(F32)+swap_cores(other).astype(F32)).astype(BF)
        share=lax.psum_scatter(both,WIDE,scatter_dimension=0,tiled=True)
        return lax.psum(share,"z")
    def both_cores(mine,axis):
        return place_halves(mine,swap_cores(mine),core,axis).astype(F32)
    up_share=both_cores(reduce_mine(gupo,guph).reshape(d//nw,nw,fb),2).reshape(d//nw,ff)
    down_share=both_cores(reduce_mine(gdno,gdnh),0).reshape(ff//nw,d)
    def by_rows(grad):
        rows=grad.shape[0]//nw
        cut=grad.reshape(nw,2,rows//2,grad.shape[1])
        mine=reduce_mine(pick(cut,core,1).reshape(-1,grad.shape[1]),pick(cut,1-core,1).reshape(-1,grad.shape[1]))
        return both_cores(mine,0).reshape(rows,-1)
    out_share=by_rows(gow)
    grad_qkv=attend_back(item_lengths,qkv,grad_heads,lse,heads)
    part_first=nt(grad_qkv,w_heads).astype(BF)
    grad_first=lax.psum_scatter(part_first,WIDE,scatter_dimension=0,tiled=True).astype(F32)
    gqkv=tn(normed_all,grad_qkv).astype(BF).reshape(nw,2,d//nw//2,3*hd)
    gqkv=(pick(gqkv,core,1).astype(F32)+swap_cores(pick(gqkv,1-core,1)).astype(F32)).astype(BF)
    gqkv=lax.all_to_all(lax.psum(gqkv,"z"),WIDE,0,0).reshape(nw,-1,3,hd).transpose(1,2,0,3)
    qkv_share=both_cores(gqkv,0).reshape(d//nw,-1)
    e1=grad_first*gain1
    back=inv1*(e1-jnp.mean(e1,axis=1,keepdims=True)-xhat1*jnp.mean(e1*xhat1,axis=1,keepdims=True))
    grad_hidden=(gmid+back).astype(BF)
    skip_share=by_rows(tn(joined,grad_hidden).astype(BF))
    grad_joined=nt(grad_hidden,w_skip)
    smalls=jnp.stack([jnp.sum(grad_first*xhat1,axis=0),jnp.sum(grad_first,axis=0),small[0],small[1]],axis=1)
    smalls=lax.psum(lax.psum_scatter(smalls.astype(BF),WIDE,scatter_dimension=0,tiled=True),ROWS).astype(F32)
    return (lay[None],grad_joined[:,:d][None],grad_joined[:,d:][None],skip_share,smalls[:,0],smalls[:,1],qkv_share,out_share,
            smalls[:,2],smalls[:,3],up_share,down_share)

def solution(mesh):
    rows,wide=mesh.devices.shape
    side=2 if wide==4 else int(wide**0.5)
    grid=Mesh(mesh.devices.reshape(rows//2,2,wide//side,side),("z","core","y","x"))
    tok=P(ROWS,WIDE,None); row=P(ROWS,None); mat=P(WIDE,None); vec=P(WIDE)
    return jax.shard_map(functools.partial(on_device,wide),mesh=grid,
        in_specs=(tok,tok,row,row,mat,vec,vec,mat,mat,vec,vec,mat,mat,tok),
        out_specs=(tok,tok,tok,mat,vec,vec,mat,mat,vec,vec,mat,mat),check_vma=False)
```

time: 2160 us -> 1210 us (0.56)
  matrix products: 637 us -> 66 us
  local copies, waits for them, and re-layouts: 383 us -> 106 us
  waiting for transfers between devices: 909 us -> 666 us
  Pallas kernels: 0 us -> 223 us
  other arithmetic: 146 us -> 43.2 us
  blocking collectives: 34.5 us -> 73.5 us
    dot_general x127 -> x6, matrix products: 637 us -> 66 us  [the longest x2 22.9 us: nt(): lax.dot_general(a, b, (((1,), (1,)), ((), ())), preferred_element_type=jn...]
    all_to_all x4 -> x2, waiting for transfers between devices: 297 us -> 58.7 us  [the longest x1 49.1 us: on_device(): w_heads = lax.all_to_all(w_heads, WIDE, 0, 0).reshape(d, 3 * hd)]
    pallas_call x0 -> x3, Pallas kernels: none -> 223 us  [the longest x1 104 us: mlp(): pl.pallas_call(functools.partial(mlp_kernel, tile), out_shape=(S((tokens,...]
    while x143 -> x0, local copies, waits for them, and re-layouts: 147 us -> none
    reduce_scatter x5 -> x4, waiting for transfers between devices: 309 us -> 171 us  [the longest x3 128 us: reduce_mine(): share = lax.psum_scatter(both, WIDE, scatter_dimension=0, tiled=True)]
    all_gather x5, waiting for transfers between devices: 119 us -> 192 us  [on_device(): gather = lambda v: lax.all_gather(v, WIDE, axis=0, tiled=True)]
    all_to_all x0 -> x2, blocking collectives: none -> 48 us  [the longest x1 24.5 us: on_device(): att = lax.all_to_all(att.reshape(nw, tokens, hd), WIDE, 0, 0)]
    all_to_all x8 -> x3, local copies, waits for them, and re-layouts: 57.1 us -> 11.7 us  [the longest x1 4.29 us: on_device(): att = lax.all_to_all(att.reshape(nw, tokens, hd), WIDE, 0, 0)]
  transfers between devices with their start and end apart: 16 -> 26, of which waited for: 12 -> 18; matrix products, arithmetic and copies ran while one was open for 25% -> 15% of each run, Pallas kernels for 0% -> 4%
where the time goes in v1:
time: 1210 us; the launch traced here: 1200 us
  waiting for transfers between devices  666 us (55%)
  Pallas kernels  223 us (18%)
  local copies, waits for them, and re-layouts  106 us (9%)
  blocking collectives  73.5 us (6%)
  matrix products  66 us (5%)
  other arithmetic  43.2 us (4%)
  between operations  14.9 us (1%)
    all_gather x5, waiting for transfers between devices, on_device(): gather = lambda v: lax.all_gather(v, WIDE, axis=0, tiled=True)  192 us
    psum x1, waiting for transfers between devices, reduce_mine(): return lax.psum(share, 'z')  169 us
    reduce_scatter x3, waiting for transfers between devices, reduce_mine(): share = lax.psum_scatter(both, WIDE, scatter_dimension=0, tiled=True)  128 us
    pallas_call x1, Pallas kernels, mlp(): pl.pallas_call(functools.partial(mlp_kernel, tile), out_shape=(S((tokens,...  104 us
    pallas_call x1, Pallas kernels, attend_back(): pl.pallas_call(functools.partial(attend_back_kernel, heads), out_shape=ja...  75.4 us
    unnamed x14, waiting for transfers between devices  49.6 us
    all_to_all x1, waiting for transfers between devices, on_device(): w_heads = lax.all_to_all(w_heads, WIDE, 0, 0).reshape(d, 3 * hd)  49.1 us
    pallas_call x1, Pallas kernels, attend(): pl.pallas_call(functools.partial(attend_kernel, heads), out_shape=(jax.Sh...  43.5 us
  transfers between devices with their start and end apart: 26, of which 18 were waited for; matrix products, arithmetic and copies ran while one was open for 15% of the time, Pallas kernels for 4%

profile of v1, /device:TPU:0, one launch (start us, length us, event | category | flops | bytes accessed | tf_op | source)
XLA Modules:
  0.0 1203.5 jit_solution(16346629223555548816)
XLA Ops:
  8.0 7.3 reshape.122
  15.2 10.8 dynamic-slice_reduce_fusion
  26.1 4.2 reshape.123
  31.7 9.6 all-gather.1
  42.1 32.5 %all-gather.8.cloned.1.call-done = bf16[2304,1152]{1,0:T(8,128)(2,1)} async-done(((bf16[576,1152]{1,0:T(8,128)(2,1)}), bf16[2304,1152]{1,0:T(8,128)(2,1)}) %all-gather.8.cloned.1.call-update) | async-done | bytes 5308432 | tf_op jit(solution)/shard_map/all_gather | solution.py:305
  74.6 8.9 fusion.16
  84.1 1.3 copy-done
  85.4 1.9 add_convert_fusion.2
  87.4 51.7 %all-gather.14.cloned.1.call-done.upo_ref = bf16[1152,2304]{1,0:T(8,128)(2,1)} async-done(((bf16[288,2304]{1,0:T(8,128)(2,1)}), bf16[1152,2304]{1,0:T(8,128)(2,1)}) %all-gather.14.cloned.1.call-update) | async-done | bytes 5308432 | tf_op jit(solution)/shard_map/all_gather | solution.py:305
  139.0 64.4 %all-gather.16.cloned.1.call-done = bf16[1,2304,1152]{2,1,0:T(8,128)(2,1)} async-done(((bf16[1,576,1152]{2,1,0:T(8,128)(2,1)}), bf16[1,2304,1152]{2,1,0:T(8,128)(2,1)}) %all-gather.16.cloned.1.call-update) | async-done | bytes 5308432 | tf_op jit(solution)/shard_map/all_gather | solution.py:305
  203.5 3.5 reshape.119
  206.9 5.0 copy.93
  212.0 4.7 all-to-all-start
  217.3 49.1 %all-to-all-done = bf16[4,288,3,288]{1,3,2,0:T(8,128)(2,1)} async-done(((bf16[4,288,3,288]{1,3,2,0:T(8,128)(2,1)}), bf16[4,288,3,288]{1,3,2,0:T(8,128)(2,1)}, u32[]{:S(2)}, u32[]{:S(2)}) %all-to-all-start) | async-done | bytes 1990688 | tf_op jit(solution)/shard_map/all_to_all | solution.py:311
  266.4 3.1 copy.94
  269.5 3.4 reshape.120
  272.9 43.0 %all-gather.10.cloned.1.call-done = bf16[3328,1152]{1,0:T(8,128)(2,1)} async-done(((bf16[832,1152]{1,0:T(8,128)(2,1)}), bf16[3328,1152]{1,0:T(8,128)(2,1)}) %all-gather.10.cloned.1.call-update) | async-done | bytes 7667728 | tf_op jit(solution)/shard_map/all_gather | solution.py:305
  315.8 13.3 %convolution_convert_fusion.2.qkv_ref = bf16[3328,864]{1,0:T(8,128)(2,1)} fusion(bf16[3328,1152]{1,0:T(8,128)(2,1)} %all-gather.10.cloned.1.call-done, bf16[1152,864]{0,1:T(8,128)(2,1)} %reshape.120), kind=kOutput, calls=%fused_computation.4 | convolution fusion | flops 6627778560 | bytes 15409152 | tf_op jit(solution)/shard_map/dot_general | solution.py:292
  329.2 43.5 %shard_map.220 = (bf16[3328,288]{1,0:T(8,128)(2,1)}, f32[12,12,384]{2,1,0:T(8,128)}) custom-call(s32[1,12]{1,0:T(1,128)} %len_ref.3, bf16[3328,864]{1,0:T(8,128)(2,1)} %convolution_convert_fusion.2.qkv_ref), custom_call_target="tpu_custom_call" | custom-call | tf_op jit(solution)/shard_map/pallas_call | solution.py:131
  372.7 3.1 copy.96
  375.8 24.5 %all_to_all.20 = bf16[4,832,288]{1,2,0:T(8,128)(2,1)} all-to-all(bf16[4,832,288]{1,2,0:T(8,128)(2,1)S(1)} %copy.96), channel_id=1, replica_groups=mesh['z'=4,'core'=2,'y'=2,'x'=2] {'y','x'}, dimensions={0} | all-to-all | bytes 3833856 | tf_op jit(solution)/shard_map/all_to_all | solution.py:321
  400.2 4.3 copy.98.att_ref
  404.5 104.2 %shard_map.221 = (f32[832,1152]{1,0:T(8,128)}, f32[832,1152]{1,0:T(8,128)}, bf16[4,832,288]{2,1,0:T(8,128)(2,1)}, bf16[1152,1152]{1,0:T(8,128)(2,1)}, f32[8,1152...) custom-call(f32[832,1152]{1,0:T(8,128)} %copy-done, ...), custom_call_target="tpu_custom_call" | custom-call | flops 59624128512 | bytes 62914560 | tf_op jit(solution)/shard_map/pallas_call | solution.py:264
  508.8 3.1 copy.99
  511.9 23.5 %all_to_all.21 = bf16[4,832,288]{1,2,0:T(8,128)(2,1)} all-to-all(bf16[4,832,288]{1,2,0:T(8,128)(2,1)S(1)} %copy.99), channel_id=1, replica_groups=mesh['z'=4,'core'=2,'y'=2,'x'=2] {'y','x'}, dimensions={0} | all-to-all | bytes 3833856 | tf_op jit(solution)/shard_map/all_to_all | solution.py:323
  535.4 4.3 copy.100
  539.7 75.4 %shard_map.222 = bf16[3328,864]{1,0:T(8,128)(2,1)} custom-call(s32[1,12]{1,0:T(1,128)} %len_ref.3, bf16[3328,864]{1,0:T(8,128)(2,1)} %convolution_convert_fusion.2.qkv_ref, bf16[3328,288]{1,0:T(8,128)(2,1)} %bitcast.89, f32[12,12,384]{2,1,0:T(8,128)} %get-tuple-element.27.lse_ref), custom_call_target="tpu_custom_call" | custom-call | tf_op jit(solution)/shard_map/pallas_call | solution.py:138
  615.1 12.8 %convolution_convert_fusion = bf16[3328,1152]{1,0:T(8,128)(2,1)} fusion(bf16[3328,864]{1,0:T(8,128)(2,1)} %shard_map.222, bf16[1152,864]{0,1:T(8,128)(2,1)S(1)} %copy-done.4), kind=kOutput, calls=%fused_computation | convolution fusion | flops 6628737024 | bytes 15409152 | tf_op jit(solution)/shard_map/dot_general | solution.py:14
  628.1 9.0 collective-permute-done.8
  637.0 6.2 add_convert_fusion.1
  643.5 1.5 copy-done.3
  645.4 8.6 collective-permute-done.6
  654.0 1.5 fusion.10
  655.6 8.3 add_convert_fusion
  663.9 43.4 %reduce-scatter.11.cloned.1.call-done = bf16[832,1152]{1,0:T(8,128)(2,1)} async-done(((bf16[3328,1152]{1,0:T(8,128)(2,1)}), bf16[832,1152]{1,0:T(8,128)(2,1)}) %reduce-scatter.11.cloned.1.call-update) | async-done | bytes 1916944 | tf_op jit(solution)/shard_map/reduce_scatter | solution.py:341
  707.3 4.3 fusion.9
  711.7 3.2 fusion.7
  715.0 6.6 convolution_convert_fusion.1
  722.1 4.9 collective-permute-done.2
  727.1 2.4 fusion
  730.0 14.2 %convolution_convert_fusion.3 = bf16[1152,864]{0,1:T(8,128)(2,1)} fusion(bf16[3328,1152]{1,0:T(8,128)(2,1)} %all-gather.10.cloned.1.call-done, bf16[3328,864]{1,0:T(8,128)(2,1)} %shard_map.222), kind=kOutput, calls=%fused_computation.24 | convolution fusion | flops 6625898496 | bytes 15409152 | tf_op jit(solution)/shard_map/dot_general | solution.py:16
  744.2 4.1 copy.101
  749.8 2.4 collective-permute-done.4
  752.3 2.4 fusion.12
  754.7 18.2 %reduce-scatter.15.cloned.1.call-done = bf16[288,2304]{1,0:T(8,128)(2,1)} async-done(((bf16[1152,2304]{1,0:T(8,128)(2,1)}), bf16[288,2304]{1,0:T(8,128)(2,1)}) %reduce-scatter.15.cloned.1.call-update) | async-done | bytes 1327120 | tf_op jit(solution)/shard_map/reduce_scatter | solution.py:327
  772.9 3.4 reshape.132
  777.6 28.6 %reduce-scatter.21.cloned.1.call-done = bf16[144,1152]{1,0:T(8,128)(2,1)} async-done(((bf16[576,1152]{1,0:T(8,128)(2,1)}), bf16[144,1152]{1,0:T(8,128)(2,1)}) %reduce-scatter.21.cloned.1.call-update) | async-done | bytes 331792
  806.3 65.9 %reduce-scatter.17.cloned.1.call-done = bf16[576,1152]{1,0:T(8,128)(2,1)} async-done(((bf16[2304,1152]{1,0:T(8,128)(2,1)}), bf16[576,1152]{1,0:T(8,128)(2,1)}) %reduce-scatter.17.cloned.1.call-update) | async-done | bytes 1327120 | tf_op jit(solution)/shard_map/reduce_scatter | solution.py:327
  872.1 43.6 %reduce-scatter.13.cloned.1.call-done = bf16[288,1152]{1,0:T(8,128)(2,1)} async-done(((bf16[1152,1152]{1,0:T(8,128)(2,1)}), bf16[288,1152]{1,0:T(8,128)(2,1)}) %reduce-scatter.13.cloned.1.call-update) | async-done | bytes 663568 | tf_op jit(solution)/shard_map/reduce_scatter | solution.py:327
  917.3 10.1 fusion.17
  927.4 169.0 %all-reduce.4.cloned.1.call-done = (bf16[288,1152]{1,0:T(8,128)(2,1)}, bf16[4,144,864]{2,1,0:T(8,128)(2,1)}, bf16[144,1152]{1,0:T(8,128)(2,1)}, bf16[288,4,576]{2,0,1:T(8,128)(2,1)}, bf16[576,1152]{1,0:T(8,128)(2,1)}) async-done(((bf16[288,1152]{1,0:T(8,128)(2,1)}, bf16[4,144,864]{2,1,0:T(8,128)(2,1)}, bf16[144,1152]{1,0:T(8,128)(2,1)}, bf16[288,4,576]{2,0,1:T(8,128)(2,1)}, bf16[576,1152]{1,0:T(8,128)(2,1)}), ...) | async-done | bytes 4644880 | tf_op jit(solution)/shard_map/psum | solution.py:328
  1096.4 7.0 slice_bitcast_fusion
  1103.4 19.6 %reduce-scatter.19.cloned.1.call-done = bf16[288,4]{1,0:T(8,128)(2,1)} async-done(((bf16[1152,4]{1,0:T(8,128)(2,1)}), bf16[288,4]{1,0:T(8,128)(2,1)}) %reduce-scatter.19.cloned.1.call-update) | async-done | bytes 2320
  1124.0 15.9 %psum.43 = bf16[288,4]{0,1:T(4,128)(2,1)S(1)} all-reduce(bf16[288,4]{0,1:T(4,128)(2,1)S(1)} %copy.109), channel_id=1, replica_groups=mesh['z'=4,'core'=2,'y'=2,'x'=2] {'z','core'}, use_global_device_ids=true, to_apply=%region_10.11 | all-reduce | flops 1152 | bytes 4608 | tf_op jit(solution)/shard_map/psum | solution.py:352
  1141.0 3.5 all-to-all-start.3
  1147.0 1.8 bitcast_convert_fusion.1
  1148.8 9.6 all-to-all-done.3
  1160.9 2.1 select_bitcast_fusion.1
  1163.4 7.0 copy.106
  1170.4 9.3 reshape.139
  1179.8 2.0 select_bitcast_fusion.3
  1182.0 2.9 bitcast_convert_fusion
  1185.9 4.4 copy.103
  1190.3 6.1 reshape.136
  (113 shorter events, 19.0 us)
Async XLA Ops:
  7.2 67.4 %all-gather.8.cloned.1.call-start = ((), (), s32[]{:S(2)}) async-start(), calls=%async_computation.10 | async-start | bytes 6635520 | tf_op jit(solution)/shard_map/all_gather | solution.py:305
  7.9 131.1 %all-gather.14.cloned.1.call-start = ((), (), s32[]{:S(2)}) async-start(), calls=%async_computation.13 | async-start | bytes 6635520 | tf_op jit(solution)/shard_map/all_gather | solution.py:305
  26.1 4.3 copy-start.6
  30.3 1.3 copy-start.10
  30.3 1.4 copy-start.11
  30.3 1.4 copy-start.12
  30.3 1.4 copy-start.13
  30.3 173.2 %all-gather.16.cloned.1.call-start = ((), (), s32[]{:S(2)}) async-start(), calls=%async_computation.18 | async-start | bytes 6635520 | tf_op jit(solution)/shard_map/all_gather | solution.py:305
  31.6 284.3 %all-gather.10.cloned.1.call-start = ((), (), s32[]{:S(2)}) async-start(), calls=%async_computation.11 | async-start | bytes 9584640 | tf_op jit(solution)/shard_map/all_gather | solution.py:305
  83.5 1.9 copy-start
  139.0 265.5 %collective-permute-start = (bf16[1152,2304]{1,0:T(8,128)(2,1)}, bf16[1152,2304]{1,0:T(8,128)(2,1)}, u32[]{:S(2)}, u32[]{:S(2)}) collective-permute-start(bf16[1152,2304]{1,0:T(8,128)(2,1)} %all-gather.14.cloned.1.call-done.upo_ref), channel_id=1, source_target_pairs={{0,4},{4,0},{1,5},{5,1},{2,6},{6,2},{3,7},{7,3},{8,12},{12,8},{9,1... | collective-permute-start | bytes 15925256 | tf_op jit(solution)/shard_map/ppermute | solution.py:283
  203.5 201.1 %collective-permute-start.1 = (bf16[2304,1152]{1,0:T(8,128)(2,1)}, bf16[2304,1152]{1,0:T(8,128)(2,1)}, u32[]{:S(2)}, u32[]{:S(2)}) collective-permute-start(bf16[2304,1152]{1,0:T(8,128)(2,1)} %bitcast.99), channel_id=1, source_target_pairs={{0,4},{4,0},{1,5},{5,1},{2,6},{6,2},{3,7},{7,3},{8,12},{12,8},{9,1... | collective-permute-start | bytes 15925256 | tf_op jit(solution)/shard_map/ppermute | solution.py:283
  212.0 54.4 %all-to-all-start = ((bf16[4,288,3,288]{1,3,2,0:T(8,128)(2,1)}), bf16[4,288,3,288]{1,3,2,0:T(8,128)(2,1)}, u32[]{:S(2)}, u32[]{:S(2)}) async-start(bf16[4,288,3,288]{1,3,2,0:T(8,128)(2,1)} %copy.93), calls=%async_computation | async-start | bytes 5308416 | tf_op jit(solution)/shard_map/all_to_all | solution.py:311
  216.6 187.9 %all-gather.12.cloned.1.call-start = ((), (), s32[]{:S(2)}) async-start(), calls=%async_computation.12 | async-start | bytes 3317760 | tf_op jit(solution)/shard_map/all_gather | solution.py:305
  217.2 490.1 %reduce-scatter.11.cloned.1.call-start = ((), (), s32[]{:S(2)}) async-start(), calls=%async_computation.14 | async-start | bytes 9584640 | tf_op jit(solution)/shard_map/reduce_scatter | solution.py:341
  539.7 75.4 %copy-start.4 = (bf16[1152,864]{0,1:T(8,128)(2,1)S(1)}, bf16[1152,864]{0,1:T(8,128)(2,1)}, u32[]{:S(2)}) copy-start(bf16[1152,864]{0,1:T(8,128)(2,1)} %reshape.120) | copy-start | bytes 5971972
  627.9 145.0 %reduce-scatter.15.cloned.1.call-start = ((), (), s32[]{:S(2)}) async-start(), calls=%async_computation.16 | async-start | bytes 6635520 | tf_op jit(solution)/shard_map/reduce_scatter | solution.py:327
  628.0 9.0 collective-permute-start.8
  643.2 1.7 copy-start.3
  643.2 163.1 %reduce-scatter.21.cloned.1.call-start = ((), (), s32[]{:S(2)}) async-start(), calls=%async_computation.20 | async-start | bytes 1658880
  643.3 12.3 %collective-permute-start.10 = (bf16[2304,1152]{1,0:T(8,128)(2,1)}, bf16[2304,1152]{1,0:T(8,128)(2,1)}, u32[]{:S(2)}, u32[]{:S(2)}) collective-permute-start(bf16[2304,1152]{1,0:T(8,128)(2,1)} %get-tuple-element.33), channel_id=1, source_target_pairs={{0,4},{4,0},{1,5},{5,1},{2,6},{6,2},{3,7},{7,3},{8,12},{12,8},{9,1... | collective-permute-start | bytes 15925256 | tf_op jit(solution)/shard_map/ppermute | solution.py:283
  645.1 8.8 collective-permute-start.6
  655.5 216.6 %reduce-scatter.17.cloned.1.call-start = ((), (), s32[]{:S(2)}) async-start(), calls=%async_computation.17 | async-start | bytes 6635520 | tf_op jit(solution)/shard_map/reduce_scatter | solution.py:327
  663.9 251.8 %reduce-scatter.13.cloned.1.call-start = ((), (), s32[]{:S(2)}) async-start(), calls=%async_computation.15 | async-start | bytes 3317760 | tf_op jit(solution)/shard_map/reduce_scatter | solution.py:327
  707.3 4.3 copy-start.1
  707.3 4.4 copy-start.2
  711.7 3.2 copy-start.14
  711.7 3.3 copy-start.15
  715.0 6.6 copy-start.5
  722.1 5.0 collective-permute-start.2
  729.5 366.9 %all-reduce.4.cloned.1.call-start = ((), (), s32[]{:S(2)}) async-start(), calls=%async_computation.21 | async-start | bytes 9658368 | tf_op jit(solution)/shard_map/psum | solution.py:328
  749.6 2.7 collective-permute-start.4
  777.6 138.3 %copy-start.9 = (f32[8,1152]{1,0:T(8,128)S(1)}, f32[8,1152]{1,0:T(8,128)}, u32[]{:S(2)}) copy-start(f32[8,1152]{1,0:T(8,128)} %get-tuple-element.28) | copy-start | bytes 110596
  915.7 207.3 %reduce-scatter.19.cloned.1.call-start = ((), (), s32[]{:S(2)}) async-start(), calls=%async_computation.19 | async-start | bytes 368640
  1096.4 48.1 %copy-start.7 = (bf16[288,1152]{1,0:T(8,128)(2,1)S(1)}, bf16[288,1152]{1,0:T(8,128)(2,1)}, u32[]{:S(2)}) copy-start(bf16[288,1152]{1,0:T(8,128)(2,1)} %get-tuple-element.43) | copy-start | bytes 1990660
  1096.4 48.2 %copy-start.8 = (bf16[144,1152]{1,0:T(8,128)(2,1)S(1)}, bf16[144,1152]{1,0:T(8,128)(2,1)}, u32[]{:S(2)}) copy-start(bf16[144,1152]{1,0:T(8,128)(2,1)} %get-tuple-element.45) | copy-start | bytes 995332
  1096.4 48.2 %collective-permute-start.7 = (bf16[144,1152]{1,0:T(8,128)(2,1)}, bf16[144,1152]{1,0:T(8,128)(2,1)S(1)}, u32[]{:S(2)}, u32[]{:S(2)}) collective-permute-start(bf16[144,1152]{1,0:T(8,128)(2,1)} %get-tuple-element.45), channel_id=1, source_target_pairs={{0,4},{4,0},{1,5},{5,1},{2,6},{6,2},{3,7},{7,3},{8,12},{12,8},{9,1... | collective-permute-start | bytes 995336 | tf_op jit(solution)/shard_map/ppermute | solution.py:283
  1140.5 39.3 %collective-permute-start.11 = (bf16[576,1152]{1,0:T(8,128)(2,1)}, bf16[576,1152]{1,0:T(8,128)(2,1)}, u32[]{:S(2)}, u32[]{:S(2)}) collective-permute-start(bf16[576,1152]{1,0:T(8,128)(2,1)} %get-tuple-element.47), channel_id=1, source_target_pairs={{0,4},{4,0},{1,5},{5,1},{2,6},{6,2},{3,7},{7,3},{8,12},{12,8},{9,1... | collective-permute-start | bytes 3981320 | tf_op jit(solution)/shard_map/ppermute | solution.py:283
  1140.5 20.4 %collective-permute-start.9 = (bf16[288,4,576]{2,0,1:T(8,128)(2,1)}, bf16[288,4,576]{2,0,1:T(8,128)(2,1)}, u32[]{:S(2)}, u32[]{:S(2)}) collective-permute-start(bf16[288,4,576]{2,0,1:T(8,128)(2,1)} %get-tuple-element.46), channel_id=1, source_target_pairs={{0,4},{4,0},{1,5},{5,1},{2,6},{6,2},{3,7},{7,3},{8,12},{12,8},{9,1... | collective-permute-start | bytes 3981320 | tf_op jit(solution)/shard_map/ppermute | solution.py:283
  1141.0 17.4 %all-to-all-start.3 = ((bf16[4,144,864]{2,1,0:T(8,128)(2,1)}), bf16[4,144,864]{2,1,0:T(8,128)(2,1)S(1)}, u32[]{:S(2)}, u32[]{:S(2)}) async-start(bf16[4,144,864]{2,1,0:T(8,128)(2,1)} %get-tuple-element.44), calls=%async_computation.5 | async-start | bytes 2064384 | tf_op jit(solution)/shard_map/all_to_all | solution.py:344
  1144.5 2.2 collective-permute-start.3
  1160.8 24.1 %collective-permute-start.5 = (bf16[144,3,4,288]{3,0,2,1:T(8,128)(2,1)}, bf16[144,3,4,288]{3,0,2,1:T(8,128)(2,1)S(1)}, u32[]{:S(2)}, u32[]{:S(2)}) collective-permute-start(bf16[144,3,4,288]{3,0,2,1:T(8,128)(2,1)} %bitcast.87), channel_id=1, source_target_pairs={{0,4},{4,0},{1,5},{5,1},{2,6},{6,2},{3,7},{7,3},{8,12},{12,8},{9,1... | collective-permute-start | bytes 2985992 | tf_op jit(solution)/shard_map/ppermute | solution.py:283
Sparse Core Ops, SparseCore 0:
  9.8 64.6 all-gather.7
  77.0 61.9 all-gather.13
  141.5 61.9 all-gather.15
  205.7 110.0 all-gather.9
  317.5 39.9 all-gather.11
  628.0 79.2 reduce-scatter.10
  710.9 61.9 reduce-scatter.14
  776.5 29.7 reduce-scatter.20
  810.1 61.9 reduce-scatter.16
  875.8 39.8 reduce-scatter.12
  919.3 177.0 all-reduce.3
  1099.8 23.1 reduce-scatter.18

commit v2 on v1

--- a/solution.py
+++ b/solution.py
@@ -132,7 +132,8 @@
       out_shape=(jax.ShapeDtypeStruct((n,heads*HEAD),jnp.bfloat16),jax.ShapeDtypeStruct((NITEM,nt_,QT),jnp.float32)),
       in_specs=[SM,VM],out_specs=(VM,VM),
       scratch_shapes=[pltpu.VMEM((3*heads,n,HEAD),jnp.bfloat16),pltpu.VMEM((heads,n,HEAD),jnp.bfloat16)],
-      compiler_params=pltpu.CompilerParams(vmem_limit_bytes=56*2**20))(lens,qkv)
+      compiler_params=pltpu.CompilerParams(vmem_limit_bytes=56*2**20),
+      cost_estimate=pl.CostEstimate(flops=heads*n*n*HEAD*4,bytes_accessed=12*2**20,transcendentals=heads*n*n//3))(lens,qkv)
 def attend_back(lens,qkv,grad,lse,heads):
     n=qkv.shape[0]
     return pl.pallas_call(functools.partial(attend_back_kernel,heads),
@@ -140,7 +141,8 @@
       in_specs=[SM,VM,VM,VM],out_specs=VM,
       scratch_shapes=[pltpu.VMEM((3*heads,n,HEAD),jnp.bfloat16),pltpu.VMEM((heads,n,HEAD),jnp.bfloat16),pltpu.VMEM((3*heads,n,HEAD),jnp.bfloat16),
         pltpu.VMEM((heads,kwin(LONG),HEAD),jnp.float32),pltpu.VMEM((heads,kwin(LONG),HEAD),jnp.float32)],
-      compiler_params=pltpu.CompilerParams(vmem_limit_bytes=60*2**20))(lens,qkv,grad,lse)
+      compiler_params=pltpu.CompilerParams(vmem_limit_bytes=60*2**20),
+      cost_estimate=pl.CostEstimate(flops=heads*n*n*HEAD*10,bytes_accessed=20*2**20,transcendentals=heads*n*n//3))(lens,qkv,grad,lse)
 
 
 F32=jnp.float32; BF=jnp.bfloat16
@@ -275,6 +277,238 @@
         hidden,att,outw,gain,shift,g,upo,uph,dno,dnh)
 
 
+MESH=pl.DeviceIdType.MESH
+
+def place():
+    x,y,c=lax.axis_index("x"),lax.axis_index("y"),lax.axis_index("core")
+    return x,y,c,2*y+x,2*y+1-x,2-2*y+x,3-2*y-x
+
+class Links:
+    def __init__(self,send,recv):
+        self.send,self.recv,self.sent=send,recv,[]
+        x,y,c=lax.axis_index("x"),lax.axis_index("y"),lax.axis_index("core")
+        self.to={"X":{"x":1-x},"Y":{"y":1-y},"D":{"x":1-x,"y":1-y},"C":{"core":1-c}}
+    def meet(self,who):
+        barrier=pltpu.get_barrier_semaphore()
+        for t in who:
+            pl.semaphore_signal(barrier,inc=1,device_id=self.to[t],device_id_type=MESH)
+        pl.semaphore_wait(barrier,len(who))
+    def start(self,k,t,src,dst):
+        copy=pltpu.make_async_remote_copy(src_ref=src,dst_ref=dst,send_sem=self.send.at[k],recv_sem=self.recv.at[k],
+                                          device_id=self.to[t],device_id_type=MESH)
+        copy.start()
+        self.sent.append(copy)
+    def got(self,k,t,dst):
+        pltpu.make_async_remote_copy(src_ref=dst,dst_ref=dst,send_sem=self.send.at[k],recv_sem=self.recv.at[k],
+                                     device_id=self.to[t],device_id_type=MESH).wait_recv()
+    def finish(self):
+        for copy in self.sent: copy.wait_send()
+
+def first_kernel(block_ref,long_ref,skip_ref,qkvw_ref,vec_ref,
+                 hidden_out,normed_out,qkv_out,heads_out,wskip_out,vec_out,
+                 ws,ns,hs,piece,hid,qs,vs,send,recv,local):
+    x,y,c,w,wx,wy,wd=place()
+    tokens,d=block_ref.shape
+    sr=skip_ref.shape[0]; half=sr//2; part=half//2
+    kr=qkvw_ref.shape[0]; kh=kr//2; hd=qkvw_ref.shape[1]//12
+    tc=tokens//4
+    mul=pl.multiple_of
+    net=Links(send,recv)
+    net.meet("XYDC")
+    def srows(b,core,p): return pl.ds(mul(b*sr+core*half+p*part,16),part)
+    def mine(p): return pl.ds(mul(c*half+p*part,16),part)
+    net.start(0,"X",skip_ref.at[mine(0)],ws.at[srows(w,c,0)])
+    net.start(2,"Y",skip_ref.at[mine(1)],ws.at[srows(w,c,1)])
+    net.start(1,"X",skip_ref.at[mine(1)],ws.at[srows(w,c,1)])
+    net.start(3,"Y",skip_ref.at[mine(0)],ws.at[srows(w,c,0)])
+    own=pltpu.make_async_copy(skip_ref,ws.at[pl.ds(mul(w*sr,16),sr)],local.at[0])
+    own.start()
+    for k,t in ((30,"X"),(31,"Y"),(32,"D")): net.start(k,t,vec_ref,vs.at[w])
+    vs[w]=vec_ref[...]
+    for p in range(4):
+        piece[p]=jnp.concatenate([qkvw_ref[:,(s*4+p)*hd:(s*4+p+1)*hd] for s in range(3)],axis=1)
+    own_heads=pltpu.make_async_copy(piece.at[w],hs.at[pl.ds(mul(w*kr,16),kr)],local.at[1])
+    own_heads.start()
+    def pass_on(k,t,b,p,onward):
+        r=srows(b,c,p)
+        net.got(k,t,ws.at[r])
+        for k2,t2 in onward: net.start(k2,t2,ws.at[r],ws.at[r])
+    pass_on(0,"X",wx,0,((4,"Y"),(6,"C")))
+    pass_on(2,"Y",wy,1,((5,"X"),(7,"C")))
+    pass_on(1,"X",wx,1,((8,"C"),))
+    pass_on(3,"Y",wy,0,((9,"C"),))
+    def hrows(b,core): return pl.ds(mul(b*kr+core*kh,16),kh)
+    cut=pl.ds(mul(c*kh,16),kh)
+    net.start(12,"X",piece.at[wx,cut],hs.at[hrows(w,c)])
+    net.start(13,"Y",piece.at[wy,cut],hs.at[hrows(w,c)])
+    net.start(14,"D",piece.at[wd,cut],hs.at[hrows(w,c)])
+    own.wait()
+    net.got(6,"C",ws.at[srows(wx,1-c,0)])
+    net.got(8,"C",ws.at[srows(wx,1-c,1)])
+    near=pl.ds(mul(y*d,16),d); far=pl.ds(mul((1-y)*d,16),d)
+    def tok(i): return pl.ds(mul(i*tc,16),tc)
+    @pl.loop(0,4)
+    def _(i):
+        lhs=jnp.where(y==0,block_ref[tok(i),:],long_ref[tok(i),:])
+        hid[tok(i),:]=nn(lhs,ws[near,:])
+    pass_on(4,"Y",wd,0,((10,"C"),))
+    pass_on(5,"X",wd,1,((11,"C"),))
+    net.got(7,"C",ws.at[srows(wy,1-c,1)])
+    net.got(9,"C",ws.at[srows(wy,1-c,0)])
+    net.got(10,"C",ws.at[srows(wd,1-c,0)])
+    net.got(11,"C",ws.at[srows(wd,1-c,1)])
+    for k,t,b in ((30,"X",wx),(31,"Y",wy),(32,"D",wd)): net.got(k,t,vs.at[b])
+    gain=jnp.concatenate([vs[p,0:1,:] for p in range(4)],axis=1)
+    shift=jnp.concatenate([vs[p,1:2,:] for p in range(4)],axis=1)
+    def nrows(b,i): return pl.ds(mul(b*tokens+i*tc,16),tc)
+    def spread(i,t):
+        net.start((18 if t=="X" else 22)+i,t,ns.at[nrows(w,i)],ns.at[nrows(w,i)])
+    for i in range(4):
+        r=tok(i)
+        lhs=jnp.where(y==0,long_ref[r,:],block_ref[r,:])
+        h=hid[r,:]+nn(lhs,ws[far,:])
+        hid[r,:]=h
+        cen=h-jnp.mean(h,axis=1,keepdims=True)
+        inv=lax.rsqrt(jnp.mean(cen*cen,axis=1,keepdims=True)+1e-5)
+        ns[nrows(w,i),:]=(cen*inv*gain+shift).astype(BF)
+        spread(i,"XYXY"[i])
+    for i,t in ((1,"X"),(0,"Y"),(3,"X"),(2,"Y")): spread(i,t)
+    outs=[]
+    def put(k,src,dst):
+        copy=pltpu.make_async_copy(src,dst,local.at[k]); copy.start(); outs.append(copy)
+    put(2,ws,wskip_out); put(3,hid,hidden_out); put(7,vs,vec_out)
+    for j,(t,b) in enumerate((("X",wx),("Y",wy),("D",wd))):
+        net.got(12+j,t,hs.at[hrows(b,c)])
+        net.start(15+j,"C",hs.at[hrows(b,c)],hs.at[hrows(b,c)])
+    for j,b in enumerate((wx,wy,wd)):
+        net.got(15+j,"C",hs.at[hrows(b,1-c)])
+    own_heads.wait()
+    put(4,hs,heads_out)
+    def project(b,i): qs[nrows(b,i),:]=nn(ns[nrows(b,i),:],hs[...]).astype(BF)
+    @pl.loop(0,4)
+    def _(i): project(w,i)
+    for i,t,b,k,k2,t2 in ((0,"X",wx,18,26,"Y"),(1,"Y",wy,22,27,"X"),(2,"X",wx,18,28,"Y"),(3,"Y",wy,22,29,"X")):
+        net.got(k+i,t,ns.at[nrows(b,i)])
+        net.start(k2,t2,ns.at[nrows(b,i)],ns.at[nrows(b,i)])
+    @pl.loop(0,2)
+    def _(i): project(wx,2*i)
+    @pl.loop(0,2)
+    def _(i): project(wy,2*i+1)
+    for i in (1,3):
+        net.got(18+i,"X",ns.at[nrows(wx,i)])
+        project(wx,i)
+        net.got(22+i-1,"Y",ns.at[nrows(wy,i-1)])
+        project(wy,i-1)
+    for i,t,k in ((0,"Y",26),(1,"X",27),(2,"Y",28),(3,"X",29)):
+        net.got(k,t,ns.at[nrows(wd,i)])
+        project(wd,i)
+    put(5,ns,normed_out); put(6,qs,qkv_out)
+    for copy in outs: copy.wait()
+    net.finish()
+
+def first(block,long,skipw,qkvw,vecs):
+    tokens,d=block.shape; S=jax.ShapeDtypeStruct; hd3=qkvw.shape[1]//4
+    V=pltpu.VMEM
+    return pl.pallas_call(first_kernel,
+        out_shape=(S((tokens,d),F32),S((4*tokens,d),BF),S((4*tokens,hd3),BF),S((d,hd3),BF),S((2*d,d),BF),S((4,)+vecs.shape,F32)),
+        in_specs=[VM]*5,out_specs=(ANY,)*6,
+        scratch_shapes=[V((2*d,d),BF),V((4*tokens,d),BF),V((d,hd3),BF),V((4,d//4,hd3),BF),V((tokens,d),F32),V((4*tokens,hd3),BF),V((4,)+vecs.shape,F32),
+            pltpu.SemaphoreType.DMA((33,)),pltpu.SemaphoreType.DMA((33,)),pltpu.SemaphoreType.DMA((8,))],
+        compiler_params=pltpu.CompilerParams(vmem_limit_bytes=56*2**20,collective_id=0,has_side_effects=True),
+        cost_estimate=pl.CostEstimate(flops=2*tokens*d*d*5,bytes_accessed=40*2**20,transcendentals=0))(
+        block,long,skipw,qkvw,vecs)
+
+def last_kernel(gq_ref,heads_ref,normed_ref,hidden_ref,gmid_ref,gain_ref,block_ref,long_ref,wskip_ref,
+                gin_ref,gsk_ref,small_ref,gqkv_out,gskip_out,
+                big,part,rx,ry,dx,dy,gw,gwr,gsr,send,recv,local):
+    x,y,c,w,wx,wy,wd=place()
+    tokens,d=block_ref.shape
+    tc=tokens//4; kr=d//4; kh=kr//2; sr=d//2; sh=sr//2
+    mul=pl.multiple_of
+    net=Links(send,recv)
+    load=pltpu.make_async_copy(normed_ref,big,local.at[0])
+    load.start()
+    net.meet("XYC")
+    def tok(i): return pl.ds(i*tc,tc)
+    def partial(b,i):
+        return nt(gq_ref[pl.ds(mul(b*tokens+i*tc,16),tc),:],heads_ref[...])
+    for i,t,dst,k in ((0,"X",dx,0),(2,"Y",dy,2),(1,"X",dx,1),(3,"Y",dy,3)):
+        part[2,tok(i),:]=partial(wd,i).astype(BF)
+        net.start(k,t,part.at[2,tok(i)],dst.at[tok(i%2)])
+    for i,t,b,dst,k in ((0,"X",wx,rx,4),(2,"Y",wy,ry,10),(1,"X",wx,rx,5),(3,"Y",wy,ry,11)):
+        s=0 if t=="X" else 1
+        part[s,tok(i),:]=partial(b,i).astype(BF)
+        net.start(k,t,part.at[s,tok(i)],dst.at[tok(i)])
+    for i,t,b,dst,k,src,k2,t2 in ((2,"X",wx,rx,6,dy,2,"Y"),(0,"Y",wy,ry,8,dx,0,"X"),(3,"X",wx,rx,7,dy,3,"Y"),(1,"Y",wy,ry,9,dx,1,"X")):
+        s=0 if t=="X" else 1
+        mine=partial(b,i)
+        net.got(k2,t2,src.at[tok(i%2)])
+        part[s,tok(i),:]=(mine+src[tok(i%2),:].astype(F32)).astype(BF)
+        net.start(k,t,part.at[s,tok(i)],dst.at[tok(i)])
+    @pl.loop(0,4)
+    def _(i):
+        r=pl.ds(mul(i*tc,16),tc)
+        gin_ref[r,:]=nt(gq_ref[pl.ds(mul(w*tokens+i*tc,16),tc),:],heads_ref[...])
+    load.wait()
+    cc=d//3
+    for k in range(3):
+        cr=pl.ds(k*cc,cc)
+        gw[cr,:]=tn(big[:,cr],gq_ref[...]).astype(BF)
+    def rows(b,core): return pl.ds(mul(b*kr+core*kh,16),kh)
+    for b in range(4):
+        net.start(12+b,"C",gw.at[rows(b,1-c)],gwr.at[pl.ds(b*kh,kh)])
+    outs=[]
+    for b in range(4):
+        r=pl.ds(b*kh,kh)
+        net.got(12+b,"C",gwr.at[r])
+        gwr[r,:]=(gwr[r,:].astype(F32)+gw[rows(b,c),:].astype(F32)).astype(BF)
+    copy=pltpu.make_async_copy(gwr,gqkv_out,local.at[1]); copy.start(); outs.append(copy)
+    small_ref[...]=jnp.zeros_like(small_ref)
+    gain=gain_ref[...]
+    for i in (0,2,1,3):
+        r=tok(i)
+        net.got(4+i,"X",rx.at[r])
+        net.got(8+i,"Y",ry.at[r])
+        gf=gin_ref[r,:]+rx[r,:].astype(F32)+ry[r,:].astype(F32)
+        h=hidden_ref[r,:]
+        cen=h-jnp.mean(h,axis=1,keepdims=True)
+        inv=lax.rsqrt(jnp.mean(cen*cen,axis=1,keepdims=True)+1e-5)
+        xhat=cen*inv
+        small_ref[0:1,:]+=jnp.sum(gf*xhat,axis=0,keepdims=True)
+        small_ref[1:2,:]+=jnp.sum(gf,axis=0,keepdims=True)
+        e=gf*gain
+        back=e-jnp.mean(e,axis=1,keepdims=True)-xhat*jnp.mean(e*xhat,axis=1,keepdims=True)
+        gh=(gmid_ref[r,:]+back*inv).astype(BF)
+        big[pl.ds(2*d+i*tc,tc),:]=gh
+        gin_ref[r,:]=nt(gh,wskip_ref[:d,:])
+        gsk_ref[r,:]=nt(gh,wskip_ref[d:,:])
+    for k in range(6):
+        src=block_ref if k<3 else long_ref
+        big[pl.ds(k*cc,cc),:]=tn(src[:,(k%3)*cc:(k%3+1)*cc],big[2*d:2*d+tokens,:]).astype(BF)
+    def srows(b,core): return pl.ds(mul(b*sr+core*sh,16),sh)
+    for b in range(4):
+        net.start(16+b,"C",big.at[srows(b,1-c)],gsr.at[pl.ds(b*sh,sh)])
+    for b in range(4):
+        r=pl.ds(b*sh,sh)
+        net.got(16+b,"C",gsr.at[r])
+        gsr[r,:]=(gsr[r,:].astype(F32)+big[srows(b,c),:].astype(F32)).astype(BF)
+    copy=pltpu.make_async_copy(gsr,gskip_out,local.at[2]); copy.start(); outs.append(copy)
+    for copy in outs: copy.wait()
+    net.finish()
+
+def last(gq,heads,normed,hidden,gmid,gain,block,long,wskip):
+    tokens,d=block.shape; S=jax.ShapeDtypeStruct; hd3=gq.shape[1]
+    V=pltpu.VMEM
+    return pl.pallas_call(last_kernel,
+        out_shape=(S((tokens,d),F32),S((tokens,d),F32),S((8,d),F32),S((d//2,hd3),BF),S((d,d),BF)),
+        in_specs=[VM,VM,ANY]+[VM]*6,out_specs=(VM,VM,VM,ANY,ANY),
+        scratch_shapes=[V((4*tokens,d),BF),V((3,tokens,d),BF),V((tokens,d),BF),V((tokens,d),BF),V((tokens//2,d),BF),V((tokens//2,d),BF),
+            V((d,hd3),BF),V((d//2,hd3),BF),V((d,d),BF),
+            pltpu.SemaphoreType.DMA((20,)),pltpu.SemaphoreType.DMA((20,)),pltpu.SemaphoreType.DMA((3,))],
+        compiler_params=pltpu.CompilerParams(vmem_limit_bytes=63*2**20,collective_id=1,has_side_effects=True),
+        cost_estimate=pl.CostEstimate(flops=2*tokens*d*d*10,bytes_accessed=60*2**20,transcendentals=0))(
+        gq,heads,normed,hidden,gmid,gain,block,long,wskip)
+
 from jax.sharding import Mesh, PartitionSpec as P
 WIDE=("y","x"); ROWS=("z","core")
 SWAP=[(0,1),(1,0)]
@@ -303,54 +537,73 @@
     heads=qkv_weight.shape[1]//(3*HEAD*nw); hd=heads*HEAD
     ff=up_weight.shape[1]; fb=ff//(2*nw)
     gather=lambda v: lax.all_gather(v,WIDE,axis=0,tiled=True)
-    vec=gather(jnp.stack([first_gain,first_shift,second_gain,second_shift],axis=1)).T.astype(F32)
-    gain1,shift1,gain2,shift2=[vec[i:i+1] for i in range(4)]
-    w_skip=gather(skip_weight)
-    joined=jnp.concatenate([block_input[0],long_skip[0]],axis=1)
-    w_heads=qkv_weight.reshape(d//nw,3,nw,hd).transpose(2,0,1,3)
-    w_heads=lax.all_to_all(w_heads,WIDE,0,0).reshape(d,3*hd)
-    hidden=dot(joined,w_skip)
-    xhat1,inv1=norm(hidden)
-    normed_all=gather((xhat1*gain1+shift1).astype(BF))
-    qkv=dot(normed_all,w_heads).astype(BF)
+    near=nw==4
+    vecs=jnp.stack([first_gain,first_shift,second_gain,second_shift]+[first_gain]*4).astype(F32)
+    if near:
+        hidden,normed_all,qkv,w_heads,w_skip,vecs=first(block_input[0],long_skip[0],skip_weight,qkv_weight,vecs)
+        vec=vecs.transpose(1,0,2).reshape(8,d)
+        gain1,shift1,gain2,shift2=[vec[i:i+1] for i in range(4)]
+        qkv,up_weight,down_weight,out_weight=lax.optimization_barrier((qkv,up_weight,down_weight,out_weight))
+    else:
+        vec=gather(vecs.astype(BF).T).T.astype(F32)
+        gain1,shift1,gain2,shift2=[vec[i:i+1] for i in range(4)]
+        w_skip=gather(skip_weight)
+        joined=jnp.concatenate([block_input[0],long_skip[0]],axis=1)
+        w_heads=qkv_weight.reshape(d//nw,3,nw,hd).transpose(2,0,1,3)
+        w_heads=lax.all_to_all(w_heads,WIDE,0,0).reshape(d,3*hd)
+        hidden=dot(joined,w_skip)
+        xhat1,inv1=norm(hidden)
+        normed_all=gather((xhat1*gain1+shift1).astype(BF))
+        qkv=dot(normed_all,w_heads).astype(BF)
     w_out=gather(out_weight)
     up_mine=gather(pick(up_weight.reshape(d//nw,nw,2,fb),core,2).reshape(d//nw,nw*fb))
     down_mine=gather(pick(down_weight.reshape(2,fb,d),core,0))
+    att,lse=attend(item_lengths,qkv,heads)
+    att,up_mine,down_mine=lax.optimization_barrier((att,up_mine,down_mine))
     up_other,down_other=swap_cores(up_mine),swap_cores(down_mine)
-    att,lse=attend(item_lengths,qkv,heads)
     att=lax.all_to_all(att.reshape(nw,tokens,hd),WIDE,0,0)
     lay,gmid,gatt,gow,small,gupo,guph,gdno,gdnh=mlp(hidden,att,w_out,gain2,shift2,output_grad[0],up_mine,up_other,down_mine,down_other)
     grad_heads=lax.all_to_all(gatt,WIDE,0,0).reshape(nw*tokens,hd)
 
-    def reduce_mine(mine,other):
+    def scatter(mine,other):
         both=(mine.astype(F32)+swap_cores(other).astype(F32)).astype(BF)
-        share=lax.psum_scatter(both,WIDE,scatter_dimension=0,tiled=True)
-        return lax.psum(share,"z")
+        return lax.psum_scatter(both,WIDE,scatter_dimension=0,tiled=True)
     def both_cores(mine,axis):
         return place_halves(mine,swap_cores(mine),core,axis).astype(F32)
-    up_share=both_cores(reduce_mine(gupo,guph).reshape(d//nw,nw,fb),2).reshape(d//nw,ff)
-    down_share=both_cores(reduce_mine(gdno,gdnh),0).reshape(ff//nw,d)
     def by_rows(grad):
-        rows=grad.shape[0]//nw
-        cut=grad.reshape(nw,2,rows//2,grad.shape[1])
-        mine=reduce_mine(pick(cut,core,1).reshape(-1,grad.shape[1]),pick(cut,1-core,1).reshape(-1,grad.shape[1]))
-        return both_cores(mine,0).reshape(rows,-1)
-    out_share=by_rows(gow)
+        cut=grad.reshape(nw,2,-1,grad.shape[1])
+        return scatter(pick(cut,core,1).reshape(-1,grad.shape[1]),pick(cut,1-core,1).reshape(-1,grad.shape[1]))
+    early=scatter(gupo,guph),scatter(gdno,gdnh),by_rows(gow)
     grad_qkv=attend_back(item_lengths,qkv,grad_heads,lse,heads)
-    part_first=nt(grad_qkv,w_heads).astype(BF)
-    grad_first=lax.psum_scatter(part_first,WIDE,scatter_dimension=0,tiled=True).astype(F32)
-    gqkv=tn(normed_all,grad_qkv).astype(BF).reshape(nw,2,d//nw//2,3*hd)
-    gqkv=(pick(gqkv,core,1).astype(F32)+swap_cores(pick(gqkv,1-core,1)).astype(F32)).astype(BF)
-    gqkv=lax.all_to_all(lax.psum(gqkv,"z"),WIDE,0,0).reshape(nw,-1,3,hd).transpose(1,2,0,3)
+    grad_qkv,early=lax.optimization_barrier((grad_qkv,early))
+    early=lax.psum(early,"z")
+    if near:
+        gin,gsk,small1,gqkv,gskip=last(grad_qkv,w_heads,normed_all,hidden,gmid,gain1,block_input[0],long_skip[0],w_skip)
+        gqkv=gqkv.reshape(nw,-1,3*hd)
+        gskip=lax.psum_scatter(gskip,WIDE,scatter_dimension=0,tiled=True)
+    else:
+        part_first=nt(grad_qkv,w_heads).astype(BF)
+        grad_first=lax.psum_scatter(part_first,WIDE,scatter_dimension=0,tiled=True).astype(F32)
+        gqkv=tn(normed_all,grad_qkv).astype(BF).reshape(nw,2,d//nw//2,3*hd)
+        gqkv=(pick(gqkv,core,1).astype(F32)+swap_cores(pick(gqkv,1-core,1)).astype(F32)).astype(BF)
+        e1=grad_first*gain1
+        across=inv1*(e1-jnp.mean(e1,axis=1,keepdims=True)-xhat1*jnp.mean(e1*xhat1,axis=1,keepdims=True))
+        grad_hidden=(gmid+across).astype(BF)
+        gskip=by_rows(tn(joined,grad_hidden).astype(BF))
+        grad_joined=nt(grad_hidden,w_skip)
+        gin,gsk=grad_joined[:,:d],grad_joined[:,d:]
+        small1=jnp.stack([jnp.sum(grad_first*xhat1,axis=0),jnp.sum(grad_first,axis=0)])
+    gqkv,gskip,early=lax.optimization_barrier((gqkv,gskip,early))
+    gqkv,gskip=lax.psum((gqkv,gskip),"z")
+    up_share=both_cores(early[0].reshape(d//nw,nw,fb),2).reshape(d//nw,ff)
+    down_share=both_cores(early[1],0).reshape(ff//nw,d)
+    out_share=both_cores(early[2],0).reshape(d//nw,d)
+    skip_share=both_cores(gskip,0).reshape(2*d//nw,d)
+    gqkv=lax.all_to_all(gqkv,WIDE,0,0).reshape(nw,-1,3,hd).transpose(1,2,0,3)
     qkv_share=both_cores(gqkv,0).reshape(d//nw,-1)
-    e1=grad_first*gain1
-    back=inv1*(e1-jnp.mean(e1,axis=1,keepdims=True)-xhat1*jnp.mean(e1*xhat1,axis=1,keepdims=True))
-    grad_hidden=(gmid+back).astype(BF)
-    skip_share=by_rows(tn(joined,grad_hidden).astype(BF))
-    grad_joined=nt(grad_hidden,w_skip)
-    smalls=jnp.stack([jnp.sum(grad_first*xhat1,axis=0),jnp.sum(grad_first,axis=0),small[0],small[1]],axis=1)
+    smalls=jnp.stack([small1[0],small1[1],small[0],small[1]],axis=1)
     smalls=lax.psum(lax.psum_scatter(smalls.astype(BF),WIDE,scatter_dimension=0,tiled=True),ROWS).astype(F32)
-    return (lay[None],grad_joined[:,:d][None],grad_joined[:,d:][None],skip_share,smalls[:,0],smalls[:,1],qkv_share,out_share,
+    return (lay[None],gin[None],gsk[None],skip_share,smalls[:,0],smalls[:,1],qkv_share,out_share,
             smalls[:,2],smalls[:,3],up_share,down_share)
 
 def solution(mesh):

time: 1210 us -> 947 us (0.78)
  waiting for transfers between devices: 666 us -> 308 us
  Pallas kernels: 223 us -> 428 us
  matrix products: 66 us -> 0 us
  local copies, waits for them, and re-layouts: 106 us -> 88.1 us
  blocking collectives: 73.5 us -> 57.8 us
  other arithmetic: 43.2 us -> 30.3 us
    pallas_call x0 -> x2, Pallas kernels: none -> 205 us  [the longest x1 109 us: first(): pl.pallas_call(first_kernel, out_shape=(S((tokens, d), F32), S((4 * token...]
    all_gather x5 -> x3, waiting for transfers between devices: 192 us -> 75.9 us  [on_device(): gather = lambda v: lax.all_gather(v, WIDE, axis=0, tiled=True)]
    reduce_scatter x4 -> x3, waiting for transfers between devices: 171 us -> 68.2 us  [the longest x1 42.2 us: on_device(): gskip = lax.psum_scatter(gskip, WIDE, scatter_dimension=0, tiled=True)]
    psum x1 -> x2, waiting for transfers between devices: 169 us -> 90.2 us  [the longest x1 67.8 us: on_device(): gqkv, gskip = lax.psum((gqkv, gskip), 'z')]
    dot_general x6 -> x0, matrix products: 66 us -> none  [the longest x2 22.9 us: nt(): lax.dot_general(a, b, (((1,), (1,)), ((), ())), preferred_element_type=jn...]
    all_to_all x2, waiting for transfers between devices: 58.7 us -> 29.6 us  [the longest x1 29.6 us: on_device(): att = lax.all_to_all(att.reshape(nw, tokens, hd), WIDE, 0, 0)]
    all_to_all x1 -> x0, blocking collectives: 24.5 us -> none  [on_device(): att = lax.all_to_all(att.reshape(nw, tokens, hd), WIDE, 0, 0)]
    unnamed x14 -> x11, waiting for transfers between devices: 49.6 us -> 26.9 us
  transfers between devices with their start and end apart: 26 -> 22, of which waited for: 18 -> 10; matrix products, arithmetic and copies ran while one was open for 15% -> 10% of each run, Pallas kernels for 4% -> 23%
where the time goes in v2:
time: 947 us; the launch traced here: 938 us
  Pallas kernels  428 us (45%)
  waiting for transfers between devices  308 us (33%)
  local copies, waits for them, and re-layouts  88.1 us (9%)
  blocking collectives  57.8 us (6%)
  other arithmetic  30.3 us (3%)
  between operations  14.9 us (2%)
  starting transfers between devices  11.1 us (1%)
    pallas_call x1, Pallas kernels, first(): pl.pallas_call(first_kernel, out_shape=(S((tokens, d), F32), S((4 * token...  109 us
    pallas_call x1, Pallas kernels, mlp(): pl.pallas_call(functools.partial(mlp_kernel, tile), out_shape=(S((tokens,...  104 us
    pallas_call x1, Pallas kernels, last(): pl.pallas_call(last_kernel, out_shape=(S((tokens, d), F32), S((tokens, d)...  95.3 us
    all_gather x3, waiting for transfers between devices, on_device(): gather = lambda v: lax.all_gather(v, WIDE, axis=0, tiled=True)  75.9 us
    pallas_call x1, Pallas kernels, attend_back(): pl.pallas_call(functools.partial(attend_back_kernel, heads), out_shape=ja...  75.2 us
    psum x1, waiting for transfers between devices, on_device(): gqkv, gskip = lax.psum((gqkv, gskip), 'z')  67.8 us
    pallas_call x1, Pallas kernels, attend(): pl.pallas_call(functools.partial(attend_kernel, heads), out_shape=(jax.Sh...  43.5 us
    reduce_scatter x1, waiting for transfers between devices, on_device(): gskip = lax.psum_scatter(gskip, WIDE, scatter_dimension=0, tiled=True)  42.2 us
  transfers between devices with their start and end apart: 22, of which 10 were waited for; matrix products, arithmetic and copies ran while one was open for 10% of the time, Pallas kernels for 23%

profile of v2, /device:TPU:0, one launch (start us, length us, event | category | flops | bytes accessed | tf_op | source)
XLA Modules:
  0.0 937.8 jit_solution(16341819160954742063)
XLA Ops:
  7.2 0.7 stack.68
  7.9 0.7 stack.69
  8.6 0.7 stack.70
  9.3 0.7 stack.71
  10.0 0.6 convert_element_type.72.vec_ref
  10.6 109.2 %shard_map.220 = (f32[832,1152]{1,0:T(8,128)}, bf16[3328,1152]{1,0:T(8,128)(2,1)}, bf16[3328,864]{1,0:T(8,128)(2,1)}, bf16[1152,864]{1,0:T(8,128)(2,1)}, bf16[23...) custom-call(bf16[832,1152]{1,0:T(8,128)(2,1)} %bitcast.76, bf16[832,1152]{1,0:T(8,128)(2,1)} %bitcast.78, ...), custom_call_target="tpu_custom_call" | custom-call | flops 11041505280 | bytes 41943040 | tf_op jit(solution)/shard_map/pallas_call | solution.py:412
  119.8 1.2 constant_dynamic-slice_fusion.2
  121.3 7.3 reshape.84
  128.5 10.8 %dynamic-slice_reduce_fusion = bf16[288,4,576]{2,1,0:T(4,128)(2,1)} fusion(bf16[288,4,2,576]{3,2,1,0:T(2,128)(2,1)S(1)} %reshape.84, s32[]{:T(128)S(6)} %select_n.71), kind=kLoop, calls=%fused_computation.3 | loop fusion | bytes 2654212 | tf_op jit(solution)/shard_map/jit(dynamic_index_in_dim)/dynamic_slice | solution.py:520
  139.4 4.2 reshape.85
  143.7 43.5 %shard_map.221 = (bf16[3328,288]{1,0:T(8,128)(2,1)}, f32[12,12,384]{2,1,0:T(8,128)}) custom-call(s32[1,12]{1,0:T(1,128)} %len_ref.3, bf16[3328,864]{1,0:T(8,128)(2,1)} %get-tuple-element.52.qkv_ref), custom_call_target="tpu_custom_call" | custom-call | flops 12759072768 | bytes 12582912 | tf_op jit(solution)/shard_map/pallas_call | solution.py:131
  187.2 60.3 %all-gather.5.cloned.1.call-done.upo_ref = bf16[1152,2304]{1,0:T(8,128)(2,1)} async-done(((bf16[288,2304]{1,0:T(8,128)(2,1)}), bf16[1152,2304]{1,0:T(8,128)(2,1)}) %all-gather.5.cloned.1.call-update) | async-done | bytes 5308432 | tf_op jit(solution)/shard_map/all_gather | solution.py:539
  247.5 0.5 collective-permute-start.1
  248.1 4.3 copy.55
  252.3 3.6 all-to-all-start
  256.0 1.0 slice_reduce_fusion
  257.0 0.7 slice.49.shift_ref
  257.7 0.7 slice.47.gain_ref
  258.3 29.6 %all-to-all-done = bf16[4,832,288]{1,2,0:T(8,128)(2,1)S(1)} async-done(((bf16[4,832,288]{1,2,0:T(8,128)(2,1)}), bf16[4,832,288]{1,2,0:T(8,128)(2,1)S(1)}, u32[]{:S(2)}, u32[]{:S(2)}) %all-to-all-start) | async-done | bytes 1916960 | tf_op jit(solution)/shard_map/all_to_all | solution.py:564
  288.0 2.7 copy.56.att_ref
  290.7 15.6 %all-gather.7.cloned.1.call-done.outw_ref = bf16[1152,1152]{1,0:T(8,128)(2,1)} async-done(((bf16[288,1152]{1,0:T(8,128)(2,1)}), bf16[1152,1152]{1,0:T(8,128)(2,1)}) %all-gather.7.cloned.1.call-update) | async-done | bytes 2654224 | tf_op jit(solution)/shard_map/all_gather | solution.py:539
  306.3 104.5 %shard_map.222 = (f32[832,1152]{1,0:T(8,128)}, f32[832,1152]{1,0:T(8,128)}, bf16[4,832,288]{2,1,0:T(8,128)(2,1)}, bf16[1152,1152]{1,0:T(8,128)(2,1)}, f32[8,1152...) custom-call(f32[832,1152]{1,0:T(8,128)} %get-tuple-element.50.hidden, ...), custom_call_target="tpu_custom_call" | custom-call | flops 59624128512 | bytes 62914560 | tf_op jit(solution)/shard_map/pallas_call | solution.py:266
  410.9 1.9 constant_dynamic-slice_fusion.1
  412.8 0.5 collective-permute-start.4
  413.3 8.1 collective-permute-done.4
  421.5 1.5 fusion
  423.1 7.8 add_convert_fusion.1
  431.1 8.8 collective-permute-done.3
  439.9 6.3 add_convert_fusion
  446.3 3.1 copy.57
  449.4 41.9 %all_to_all.15 = bf16[4,832,288]{1,2,0:T(8,128)(2,1)} all-to-all(bf16[4,832,288]{1,2,0:T(8,128)(2,1)S(1)} %copy.57), channel_id=1, replica_groups=mesh['z'=4,'core'=2,'y'=2,'x'=2] {'y','x'}, dimensions={0} | all-to-all | bytes 3833856 | tf_op jit(solution)/shard_map/all_to_all | solution.py:566
  491.3 4.3 copy.58
  495.7 75.2 %shard_map.223.gq_ref = bf16[3328,864]{1,0:T(8,128)(2,1)} custom-call(s32[1,12]{1,0:T(1,128)} %len_ref.3, bf16[3328,864]{1,0:T(8,128)(2,1)} %get-tuple-element.52.qkv_ref, bf16[3328,288]{1,0:T(8,128)(2,1)} %bitcast.67, f32[12,12,384]{2,1,0:T(8,128)} %get-tuple-element.63.lse_ref), custom_call_target="tpu_custom_call" | custom-call | flops 31897681920 | bytes 20971520 | tf_op jit(solution)/shard_map/pallas_call | solution.py:139
  570.9 26.0 %reduce-scatter.12.cloned.1.call-done = bf16[576,1152]{1,0:T(8,128)(2,1)} async-done(((bf16[2304,1152]{1,0:T(8,128)(2,1)}), bf16[576,1152]{1,0:T(8,128)(2,1)}) %reduce-scatter.12.cloned.1.call-update) | async-done | bytes 1327120 | tf_op jit(solution)/shard_map/reduce_scatter | solution.py:570
  597.0 0.5 reduce-scatter.14.cloned.1.call-start
  597.5 0.7 slice.51.gain_ref
  598.1 95.3 %shard_map.224 = (f32[832,1152]{1,0:T(8,128)}, f32[832,1152]{1,0:T(8,128)}, f32[8,1152]{1,0:T(8,128)}, bf16[576,864]{1,0:T(8,128)(2,1)}, bf16[1152,1152]{1,0:T(8,128)(2,1)}) custom-call(bf16[3328,864]{1,0:T(8,128)(2,1)} %shard_map.223.gq_ref, bf16[1152,864]{1,0:T(8,128)(2,1)} %get-tuple-element.70.heads_ref, ...), custom_call_target="tpu_custom_call" | custom-call | flops 22083010560 | bytes 62914560 | tf_op jit(solution)/shard_map/pallas_call | solution.py:502
  693.6 0.7 copy-done.5
  694.3 22.4 %all-reduce.8.cloned.1.call-done = (bf16[288,2304]{1,0:T(8,128)(2,1)}, bf16[576,1152]{1,0:T(8,128)(2,1)}, bf16[144,1152]{1,0:T(8,128)(2,1)}) async-done(((bf16[288,2304]{1,0:T(8,128)(2,1)}, bf16[576,1152]{1,0:T(8,128)(2,1)}, bf16[144,1152]{1,0:T(8,128)(2,1)}), (bf16[288,2304]{1,0:T(8,128)(2,1)}, bf16[576,1152]{1,0:T(8,128)(2,1)}, bf16[144,1152]{1,0:T(8,128)(2,1)})) %all-reduce.8.cloned.1.call-update) | async-done | bytes 2986000 | tf_op jit(solution)/shard_map/psum | solution.py:579
  716.7 42.2 %reduce-scatter.14.cloned.1.call-done = bf16[288,1152]{1,0:T(8,128)(2,1)} async-done(((bf16[1152,1152]{1,0:T(8,128)(2,1)}), bf16[288,1152]{1,0:T(8,128)(2,1)}) %reduce-scatter.14.cloned.1.call-update) | async-done | bytes 663568 | tf_op jit(solution)/shard_map/reduce_scatter | solution.py:583
  758.9 0.9 copy.66
  759.9 26.8 %reduce-scatter.16.cloned.1.call-done = bf16[288,4]{1,0:T(8,128)(2,1)} async-done(((bf16[1152,4]{1,0:T(8,128)(2,1)}), bf16[288,4]{1,0:T(8,128)(2,1)}) %reduce-scatter.16.cloned.1.call-update) | async-done | bytes 2320
  786.7 1.0 copy.67
  787.6 15.9 %psum.46 = bf16[288,4]{0,1:T(4,128)(2,1)S(1)} all-reduce(bf16[288,4]{0,1:T(4,128)(2,1)S(1)} %copy.67), channel_id=1, replica_groups=mesh['z'=4,'core'=2,'y'=2,'x'=2] {'z','core'}, use_global_device_ids=true, to_apply=%region_9.10 | all-reduce | flops 1152 | bytes 4608 | tf_op jit(solution)/shard_map/psum | solution.py:605
  803.6 0.6 slice_reduce_fusion.3
  804.2 3.4 reshape.93
  807.7 1.3 copy.62
  809.7 1.2 bitcast_convert_fusion.2
  811.2 1.8 pad_maximum_fusion
  813.0 67.8 %all-reduce.6.cloned.1.call-done = (bf16[288,1152]{1,0:T(8,128)(2,1)}, bf16[4,144,864]{2,1,0:T(8,128)(2,1)}) async-done(((bf16[288,1152]{1,0:T(8,128)(2,1)}, bf16[4,144,864]{2,1,0:T(8,128)(2,1)}), (bf16[288,1152]{1,0:T(8,128)(2,1)}, bf16[4,144,864]{2,1,0:T(8,128)(2,1)})) %all-reduce.6.cloned.1.call-update) | async-done | bytes 1658896 | tf_op jit(solution)/shard_map/psum | solution.py:597
  880.8 3.9 all-to-all-start.2
  884.7 4.5 bitcast_convert_fusion
  889.2 1.8 select_bitcast_fusion.1
  891.5 7.1 copy.65
  898.5 9.1 reshape.98
  907.7 1.2 reshape.92
  909.1 0.6 collective-permute-start.6
  909.7 1.2 select_bitcast_fusion.7
  911.0 1.8 bitcast_convert_fusion.1
  913.2 0.5 maximum_convert_fusion.1
  913.7 4.4 copy.60
  918.1 6.1 reshape.96
  924.3 4.4 copy.82
  928.6 1.9 copy.83
  (64 shorter events, 3.4 us)
Async XLA Ops:
  7.2 180.0 %all-gather.9.cloned.1.call-start = ((), (), s32[]{:S(2)}) async-start(), calls=%async_computation.13 | async-start | bytes 6635520 | tf_op jit(solution)/shard_map/all_gather | solution.py:539
  10.6 109.2 %copy-start.2 = (bf16[1152,1152]{1,0:T(8,128)(2,1)S(1)}, bf16[1152,1152]{1,0:T(8,128)(2,1)}, u32[]{:S(2)}) copy-start(bf16[1152,1152]{1,0:T(8,128)(2,1)} %param.25) | copy-start | bytes 7962628
  121.0 126.5 %all-gather.5.cloned.1.call-start = ((), (), s32[]{:S(2)}) async-start(), calls=%async_computation.8 | async-start | bytes 6635520 | tf_op jit(solution)/shard_map/all_gather | solution.py:539
  143.6 162.6 %all-gather.7.cloned.1.call-start = ((), (), s32[]{:S(2)}) async-start(), calls=%async_computation.9 | async-start | bytes 3317760 | tf_op jit(solution)/shard_map/all_gather | solution.py:539
  247.5 58.8 %collective-permute-start = (bf16[1152,2304]{1,0:T(8,128)(2,1)}, bf16[1152,2304]{1,0:T(8,128)(2,1)}, u32[]{:S(2)}, u32[]{:S(2)}) collective-permute-start(bf16[1152,2304]{1,0:T(8,128)(2,1)} %all-gather.5.cloned.1.call-done.upo_ref), channel_id=1, source_target_pairs={{0,4},{4,0},{1,5},{5,1},{2,6},{6,2},{3,7},{7,3},{8,12},{12,8},{9,1... | collective-permute-start | bytes 15925256 | tf_op jit(solution)/shard_map/ppermute | solution.py:517
  247.5 58.8 %collective-permute-start.1 = (bf16[2304,1152]{1,0:T(8,128)(2,1)}, bf16[2304,1152]{1,0:T(8,128)(2,1)}, u32[]{:S(2)}, u32[]{:S(2)}) collective-permute-start(bf16[2304,1152]{1,0:T(8,128)(2,1)} %bitcast.73), channel_id=1, source_target_pairs={{0,4},{4,0},{1,5},{5,1},{2,6},{6,2},{3,7},{7,3},{8,12},{12,8},{9,1... | collective-permute-start | bytes 15925256 | tf_op jit(solution)/shard_map/ppermute | solution.py:517
  252.3 35.6 %all-to-all-start = ((bf16[4,832,288]{1,2,0:T(8,128)(2,1)}), bf16[4,832,288]{1,2,0:T(8,128)(2,1)S(1)}, u32[]{:S(2)}, u32[]{:S(2)}) async-start(bf16[4,832,288]{1,2,0:T(8,128)(2,1)} %copy.55), calls=%async_computation | async-start | bytes 4128768 | tf_op jit(solution)/shard_map/all_to_all | solution.py:564
  256.0 315.0 %reduce-scatter.18.cloned.1.call-start = ((), (), s32[]{:S(2)}) async-start(), calls=%async_computation.15 | async-start | bytes 1658880
  410.8 12.3 %collective-permute-start.2 = (bf16[1152,2304]{1,0:T(8,128)(2,1)}, bf16[1152,2304]{1,0:T(8,128)(2,1)}, u32[]{:S(2)}, u32[]{:S(2)}) collective-permute-start(bf16[1152,2304]{1,0:T(8,128)(2,1)} %get-tuple-element.65), channel_id=1, source_target_pairs={{0,4},{4,0},{1,5},{5,1},{2,6},{6,2},{3,7},{7,3},{8,12},{12,8},{9,1... | collective-permute-start | bytes 15925256 | tf_op jit(solution)/shard_map/ppermute | solution.py:517
  412.8 8.7 collective-permute-start.4
  423.0 147.9 %reduce-scatter.10.cloned.1.call-start = ((), (), s32[]{:S(2)}) async-start(), calls=%async_computation.10 | async-start | bytes 6635520 | tf_op jit(solution)/shard_map/reduce_scatter | solution.py:570
  430.9 166.1 %reduce-scatter.12.cloned.1.call-start = ((), (), s32[]{:S(2)}) async-start(), calls=%async_computation.11 | async-start | bytes 6635520 | tf_op jit(solution)/shard_map/reduce_scatter | solution.py:570
  430.9 9.0 collective-permute-start.3
  446.2 270.4 %all-reduce.8.cloned.1.call-start = ((), (), s32[]{:S(2)}) async-start(), calls=%async_computation.17 | async-start | bytes 5971968 | tf_op jit(solution)/shard_map/psum | solution.py:579
  597.0 161.9 %reduce-scatter.14.cloned.1.call-start = ((), (), s32[]{:S(2)}) async-start(), calls=%async_computation.12 | async-start | bytes 3317760 | tf_op jit(solution)/shard_map/reduce_scatter | solution.py:583
  693.5 0.8 copy-start.5
  693.5 0.8 copy-start.6
  693.5 93.1 %reduce-scatter.16.cloned.1.call-start = ((), (), s32[]{:S(2)}) async-start(), calls=%async_computation.14 | async-start | bytes 368640
  758.9 50.6 %collective-permute-start.7 = (bf16[144,1152]{1,0:T(8,128)(2,1)}, bf16[144,1152]{1,0:T(8,128)(2,1)S(1)}, u32[]{:S(2)}, u32[]{:S(2)}) collective-permute-start(bf16[144,1152]{1,0:T(8,128)(2,1)} %get-tuple-element.85), channel_id=1, source_target_pairs={{0,4},{4,0},{1,5},{5,1},{2,6},{6,2},{3,7},{7,3},{8,12},{12,8},{9,1... | collective-permute-start | bytes 995336 | tf_op jit(solution)/shard_map/ppermute | solution.py:517
  759.8 120.9 %all-reduce.6.cloned.1.call-start = ((), (), s32[]{:S(2)}) async-start(), calls=%async_computation.16 | async-start | bytes 3391488 | tf_op jit(solution)/shard_map/psum | solution.py:597
  803.5 7.4 collective-permute-start.9
  807.7 1.8 copy-start.4
  809.0 80.3 %collective-permute-start.8 = (bf16[288,4,576]{2,0,1:T(8,128)(2,1)}, bf16[288,4,576]{2,0,1:T(8,128)(2,1)}, u32[]{:S(2)}, u32[]{:S(2)}) collective-permute-start(bf16[288,4,576]{2,0,1:T(8,128)(2,1)} %copy.62), channel_id=1, source_target_pairs={{0,4},{4,0},{1,5},{5,1},{2,6},{6,2},{3,7},{7,3},{8,12},{12,8},{9,1... | collective-permute-start | bytes 3981320 | tf_op jit(solution)/shard_map/ppermute | solution.py:517
  809.5 1.4 copy-start.1
  880.8 26.9 %all-to-all-start.2 = ((bf16[4,144,864]{2,1,0:T(8,128)(2,1)}), bf16[4,144,864]{2,1,0:T(8,128)(2,1)S(1)}, u32[]{:S(2)}, u32[]{:S(2)}) async-start(bf16[4,144,864]{2,1,0:T(8,128)(2,1)} %get-tuple-element.96), calls=%async_computation.5 | async-start | bytes 2064384 | tf_op jit(solution)/shard_map/all_to_all | solution.py:602
  884.7 25.0 %collective-permute-start.5 = (bf16[288,1152]{1,0:T(8,128)(2,1)}, bf16[288,1152]{1,0:T(8,128)(2,1)}, u32[]{:S(2)}, u32[]{:S(2)}) collective-permute-start(bf16[288,1152]{1,0:T(8,128)(2,1)} %get-tuple-element.95), channel_id=1, source_target_pairs={{0,4},{4,0},{1,5},{5,1},{2,6},{6,2},{3,7},{7,3},{8,12},{12,8},{9,1... | collective-permute-start | bytes 1990664 | tf_op jit(solution)/shard_map/ppermute | solution.py:517
  907.7 2.0 copy-start.3
  909.1 3.7 collective-permute-start.6
  924.3 4.4 copy-start
Sparse Core Ops, SparseCore 0:
  121.1 61.9 all-gather.8
  185.5 61.9 all-gather.4
  249.4 56.8 all-gather.6
  423.1 29.6 reduce-scatter.17
  456.6 74.6 reduce-scatter.9
  534.9 61.9 reduce-scatter.11
  599.7 116.9 all-reduce.7
  719.9 38.8 reduce-scatter.13
  762.4 24.1 reduce-scatter.15
  809.6 71.1 all-reduce.5

commit v3 on v2

--- a/solution.py
+++ b/solution.py
@@ -418,96 +418,275 @@
         cost_estimate=pl.CostEstimate(flops=2*tokens*d*d*5,bytes_accessed=40*2**20,transcendentals=0))(
         block,long,skipw,qkvw,vecs)
 
-def last_kernel(gq_ref,heads_ref,normed_ref,hidden_ref,gmid_ref,gain_ref,block_ref,long_ref,wskip_ref,
-                gin_ref,gsk_ref,small_ref,gqkv_out,gskip_out,
-                big,part,rx,ry,dx,dy,gw,gwr,gsr,send,recv,local):
+class Chain:
+    def __init__(self,net,k,own,up_in,down_in,up_out,down_out):
+        self.net,self.k,self.own=net,k,own
+        self.up_in,self.down_in,self.up_out,self.down_out=up_in,down_in,up_out,down_out
+        self.z,self.n=lax.axis_index("z"),lax.axis_size("z")
+    def copy(self,up,src):
+        k=self.k+(0 if up else 1)
+        return pltpu.make_async_remote_copy(src_ref=src,dst_ref=self.up_in if up else self.down_in,
+            send_sem=self.net.send.at[k],recv_sem=self.net.recv.at[k],
+            device_id={"z":self.z+1 if up else self.z-1},device_id_type=MESH)
+    def hop(self,h):
+        for up in (True,False):
+            here=self.z==(h if up else self.n-1-h)
+            inn,out=(self.up_in,self.up_out) if up else (self.down_in,self.down_out)
+            @pl.when(here)
+            def _():
+                if h==0:
+                    self.copy(up,self.own).start()
+                else:
+                    self.copy(up,inn).wait_recv()
+                    out[...]=(self.own[...].astype(F32)+inn[...].astype(F32)).astype(out.dtype)
+                    self.copy(up,out).start()
+    def total(self):
+        first,final=self.z==0,self.z==self.n-1
+        @pl.when(first)
+        def _():
+            self.copy(False,self.down_in).wait_recv()
+            self.copy(True,self.own).wait_send()
+            self.own[...]=(self.own[...].astype(F32)+self.down_in[...].astype(F32)).astype(self.own.dtype)
+        @pl.when(final)
+        def _():
+            self.copy(True,self.up_in).wait_recv()
+            self.copy(False,self.own).wait_send()
+            self.own[...]=(self.own[...].astype(F32)+self.up_in[...].astype(F32)).astype(self.own.dtype)
+        @pl.when(jnp.logical_not(first|final))
+        def _():
+            self.copy(True,self.up_out).wait_send()
+            self.copy(False,self.down_out).wait_send()
+            self.own[...]=(self.own[...].astype(F32)+self.up_in[...].astype(F32)+self.down_in[...].astype(F32)).astype(self.own.dtype)
+
+def meet_all(net,who):
+    z,n=lax.axis_index("z"),lax.axis_size("z")
+    barrier=pltpu.get_barrier_semaphore()
+    for t in who:
+        pl.semaphore_signal(barrier,inc=1,device_id=net.to[t],device_id_type=MESH)
+    @pl.when(z>0)
+    def _(): pl.semaphore_signal(barrier,inc=1,device_id={"z":z-1},device_id_type=MESH)
+    @pl.when(z<n-1)
+    def _(): pl.semaphore_signal(barrier,inc=1,device_id={"z":z+1},device_id_type=MESH)
+    ends=(z==0)|(z==n-1)
+    @pl.when(ends)
+    def _(): pl.semaphore_wait(barrier,len(who)+1)
+    @pl.when(jnp.logical_not(ends))
+    def _(): pl.semaphore_wait(barrier,len(who)+2)
+
+SEG=3
+def last_kernel(gq_ref,heads_ref,normed_ref,hidden_ref,gmid_ref,gain_ref,block_ref,long_ref,wskip_ref,small_ref,
+                gin_out,gsk_out,small_out,gqkv_out,gskip_out,
+                big,part,rx,ry,dx,dy,gw,gwr,gsr,qz,fq,sdx,sdy,srx,sry,own,sz,fs,sm,sin,smz,send,recv,local):
     x,y,c,w,wx,wy,wd=place()
     tokens,d=block_ref.shape
-    tc=tokens//4; kr=d//4; kh=kr//2; sr=d//2; sh=sr//2
+    tc=tokens//4; kr=d//4; kh=kr//2; sr=d//2; sh=sr//2; sq=sh//2
     mul=pl.multiple_of
     net=Links(send,recv)
     load=pltpu.make_async_copy(normed_ref,big,local.at[0])
     load.start()
-    net.meet("XYC")
+    meet_all(net,"XYDC")
     def tok(i): return pl.ds(i*tc,tc)
+    def pr(s,i): return pl.ds(s*tokens+i*tc,tc)
     def partial(b,i):
         return nt(gq_ref[pl.ds(mul(b*tokens+i*tc,16),tc),:],heads_ref[...])
     for i,t,dst,k in ((0,"X",dx,0),(2,"Y",dy,2),(1,"X",dx,1),(3,"Y",dy,3)):
-        part[2,tok(i),:]=partial(wd,i).astype(BF)
-        net.start(k,t,part.at[2,tok(i)],dst.at[tok(i%2)])
+        part[pr(2,i),:]=partial(wd,i).astype(BF)
+        net.start(k,t,part.at[pr(2,i)],dst.at[tok(i%2)])
     for i,t,b,dst,k in ((0,"X",wx,rx,4),(2,"Y",wy,ry,10),(1,"X",wx,rx,5),(3,"Y",wy,ry,11)):
         s=0 if t=="X" else 1
-        part[s,tok(i),:]=partial(b,i).astype(BF)
-        net.start(k,t,part.at[s,tok(i)],dst.at[tok(i)])
-    for i,t,b,dst,k,src,k2,t2 in ((2,"X",wx,rx,6,dy,2,"Y"),(0,"Y",wy,ry,8,dx,0,"X"),(3,"X",wx,rx,7,dy,3,"Y"),(1,"Y",wy,ry,9,dx,1,"X")):
+        part[pr(s,i),:]=partial(b,i).astype(BF)
+        net.start(k,t,part.at[pr(s,i)],dst.at[tok(i)])
+    @pl.loop(0,4)
+    def _(i):
+        r=pl.ds(mul(i*tc,16),tc)
+        part[pl.ds(mul(3*tokens+i*tc,16),tc),:]=nt(gq_ref[pl.ds(mul(w*tokens+i*tc,16),tc),:],heads_ref[...]).astype(BF)
+    load.wait()
+    cc=d//3
+    def weight_grad(k):
+        cr=pl.ds(k*cc,cc)
+        gw[cr,:]=tn(big[:,cr],gq_ref[...]).astype(BF)
+    def relay(i,t,b,dst,k,src,k2,t2):
         s=0 if t=="X" else 1
         mine=partial(b,i)
         net.got(k2,t2,src.at[tok(i%2)])
-        part[s,tok(i),:]=(mine+src[tok(i%2),:].astype(F32)).astype(BF)
-        net.start(k,t,part.at[s,tok(i)],dst.at[tok(i)])
-    @pl.loop(0,4)
-    def _(i):
-        r=pl.ds(mul(i*tc,16),tc)
-        gin_ref[r,:]=nt(gq_ref[pl.ds(mul(w*tokens+i*tc,16),tc),:],heads_ref[...])
-    load.wait()
-    cc=d//3
-    for k in range(3):
-        cr=pl.ds(k*cc,cc)
-        gw[cr,:]=tn(big[:,cr],gq_ref[...]).astype(BF)
+        part[pr(s,i),:]=(mine+src[tok(i%2),:].astype(F32)).astype(BF)
+        net.start(k,t,part.at[pr(s,i)],dst.at[tok(i)])
+    weight_grad(0)
+    relay(2,"X",wx,rx,6,dy,2,"Y")
+    relay(0,"Y",wy,ry,8,dx,0,"X")
+    weight_grad(1)
+    weight_grad(2)
     def rows(b,core): return pl.ds(mul(b*kr+core*kh,16),kh)
     for b in range(4):
         net.start(12+b,"C",gw.at[rows(b,1-c)],gwr.at[pl.ds(b*kh,kh)])
-    outs=[]
+    relay(3,"X",wx,rx,7,dy,3,"Y")
+    relay(1,"Y",wy,ry,9,dx,1,"X")
     for b in range(4):
         r=pl.ds(b*kh,kh)
         net.got(12+b,"C",gwr.at[r])
         gwr[r,:]=(gwr[r,:].astype(F32)+gw[rows(b,c),:].astype(F32)).astype(BF)
-    copy=pltpu.make_async_copy(gwr,gqkv_out,local.at[1]); copy.start(); outs.append(copy)
-    small_ref[...]=jnp.zeros_like(small_ref)
+    halves=[pl.ds(i*2*kh,2*kh) for i in range(2)]
+    chains=[Chain(net,40+2*i,gwr.at[r],*[qz.at[j,r] for j in range(4)]) for i,r in enumerate(halves)]
+    for chain in chains: chain.hop(0)
     gain=gain_ref[...]
+    sm[...]=jnp.zeros_like(sm)
+    for h in range(1,lax.axis_size("z")-2):
+        for chain in chains: chain.hop(h)
     for i in (0,2,1,3):
         r=tok(i)
         net.got(4+i,"X",rx.at[r])
         net.got(8+i,"Y",ry.at[r])
-        gf=gin_ref[r,:]+rx[r,:].astype(F32)+ry[r,:].astype(F32)
+        gf=part[pr(3,i),:].astype(F32)+rx[r,:].astype(F32)+ry[r,:].astype(F32)
         h=hidden_ref[r,:]
         cen=h-jnp.mean(h,axis=1,keepdims=True)
         inv=lax.rsqrt(jnp.mean(cen*cen,axis=1,keepdims=True)+1e-5)
         xhat=cen*inv
-        small_ref[0:1,:]+=jnp.sum(gf*xhat,axis=0,keepdims=True)
-        small_ref[1:2,:]+=jnp.sum(gf,axis=0,keepdims=True)
+        sm[0:1,:]+=jnp.sum(gf*xhat,axis=0,keepdims=True)
+        sm[1:2,:]+=jnp.sum(gf,axis=0,keepdims=True)
         e=gf*gain
         back=e-jnp.mean(e,axis=1,keepdims=True)-xhat*jnp.mean(e*xhat,axis=1,keepdims=True)
-        gh=(gmid_ref[r,:]+back*inv).astype(BF)
-        big[pl.ds(2*d+i*tc,tc),:]=gh
-        gin_ref[r,:]=nt(gh,wskip_ref[:d,:])
-        gsk_ref[r,:]=nt(gh,wskip_ref[d:,:])
+        big[pl.ds(2*d+i*tc,tc),:]=(gmid_ref[r,:]+back*inv).astype(BF)
+    sm[2:4,:]=small_ref[0:2,:]
     for k in range(6):
         src=block_ref if k<3 else long_ref
         big[pl.ds(k*cc,cc),:]=tn(src[:,(k%3)*cc:(k%3+1)*cc],big[2*d:2*d+tokens,:]).astype(BF)
     def srows(b,core): return pl.ds(mul(b*sr+core*sh,16),sh)
     for b in range(4):
         net.start(16+b,"C",big.at[srows(b,1-c)],gsr.at[pl.ds(b*sh,sh)])
+    net.start(20,"C",sm,sin.at[0])
+    for copy in net.sent[:16]: copy.wait_send()
+    net.sent=net.sent[16:]
+    wload=pltpu.make_async_copy(wskip_ref,part.at[pl.ds(0,2*d)],local.at[1])
+    wload.start()
+    for chain in chains: chain.hop(lax.axis_size("z")-2)
     for b in range(4):
         r=pl.ds(b*sh,sh)
         net.got(16+b,"C",gsr.at[r])
         gsr[r,:]=(gsr[r,:].astype(F32)+big[srows(b,c),:].astype(F32)).astype(BF)
-    copy=pltpu.make_async_copy(gsr,gskip_out,local.at[2]); copy.start(); outs.append(copy)
+    def quarter(b,i): return pl.ds(mul(b*sh+i*sq,16),sq)
+    top,low=pl.ds(0,sq),pl.ds(sq,sq)
+    net.start(21,"X",gsr.at[quarter(wd,0)],sdx)
+    net.start(22,"Y",gsr.at[quarter(wd,1)],sdy)
+    net.start(23,"X",gsr.at[quarter(wx,0)],srx.at[top])
+    net.start(24,"Y",gsr.at[quarter(wy,1)],sry.at[low])
+    net.got(20,"C",sin.at[0])
+    smz[6]=sm[...]+sin[0]
+    net.start(27,"X",smz.at[6],sin.at[1])
+    for chain in chains: chain.total()
+    def qrows(b): return pl.ds(mul(b*kh,16),kh)
+    for j,(t,b) in enumerate((("X",wx),("Y",wy),("D",wd))):
+        net.start(29+j,t,gwr.at[qrows(b)],fq.at[w,c])
+    fq[w,c]=gwr[qrows(w),:]
+    wload.wait()
+    @pl.loop(0,4)
+    def _(i):
+        r=pl.ds(mul(i*tc,16),tc)
+        gh=big[pl.ds(mul(2*d+i*tc,16),tc),:]
+        rx[r,:]=nt(gh,part[:d,:]).astype(BF)
+        ry[r,:]=nt(gh,part[d:2*d,:]).astype(BF)
+    outs=[]
+    def put(k,src,dst):
+        copy=pltpu.make_async_copy(src,dst,local.at[k]); copy.start(); outs.append(copy)
+    put(2,rx,gin_out); put(3,ry,gsk_out)
+    net.got(21,"X",sdx)
+    gsr[quarter(wy,0),:]=(gsr[quarter(wy,0),:].astype(F32)+sdx[...].astype(F32)).astype(BF)
+    net.start(25,"Y",gsr.at[quarter(wy,0)],sry.at[top])
+    net.got(22,"Y",sdy)
+    gsr[quarter(wx,1),:]=(gsr[quarter(wx,1),:].astype(F32)+sdy[...].astype(F32)).astype(BF)
+    net.start(26,"X",gsr.at[quarter(wx,1)],srx.at[low])
+    net.got(27,"X",sin.at[1])
+    smz[0]=smz[6]+sin[1]
+    net.start(28,"Y",smz.at[0],sin.at[2])
+    for j,(t,b) in enumerate((("X",wx),("Y",wy),("D",wd))):
+        net.got(29+j,t,fq.at[b,c])
+    for b in range(4):
+        net.start(32+b,"C",fq.at[b,c],fq.at[b,c])
+    net.got(28,"Y",sin.at[2])
+    smz[1]=smz[0]+sin[2]
+    net.got(23,"X",srx.at[top]); net.got(25,"Y",sry.at[top])
+    net.got(24,"Y",sry.at[low]); net.got(26,"X",srx.at[low])
+    own[...]=(gsr[pl.ds(mul(w*sh,16),sh),:].astype(F32)+srx[...].astype(F32)+sry[...].astype(F32)).astype(BF)
+    seg=sh//SEG
+    chains=[Chain(net,44,smz.at[1],smz.at[2],smz.at[3],smz.at[4],smz.at[5])]
+    for i in range(SEG):
+        r=pl.ds(i*seg,seg)
+        chains.append(Chain(net,46+2*i,own.at[r],*[sz.at[j,r] for j in range(4)]))
+    for h in range(lax.axis_size("z")-1):
+        for chain in chains: chain.hop(h)
+    for chain in chains: chain.total()
+    net.start(36,"C",own,fs)
+    for b in range(4): net.got(32+b,"C",fq.at[b,1-c])
+    put(4,fq,gqkv_out); put(5,smz.at[1],small_out); put(6,own,gskip_out.at[c])
+    net.got(36,"C",fs)
+    put(7,fs,gskip_out.at[1-c])
     for copy in outs: copy.wait()
     net.finish()
 
-def last(gq,heads,normed,hidden,gmid,gain,block,long,wskip):
+def last(gq,heads,normed,hidden,gmid,gain,block,long,wskip,small):
     tokens,d=block.shape; S=jax.ShapeDtypeStruct; hd3=gq.shape[1]
     V=pltpu.VMEM
     return pl.pallas_call(last_kernel,
-        out_shape=(S((tokens,d),F32),S((tokens,d),F32),S((8,d),F32),S((d//2,hd3),BF),S((d,d),BF)),
-        in_specs=[VM,VM,ANY]+[VM]*6,out_specs=(VM,VM,VM,ANY,ANY),
-        scratch_shapes=[V((4*tokens,d),BF),V((3,tokens,d),BF),V((tokens,d),BF),V((tokens,d),BF),V((tokens//2,d),BF),V((tokens//2,d),BF),
-            V((d,hd3),BF),V((d//2,hd3),BF),V((d,d),BF),
-            pltpu.SemaphoreType.DMA((20,)),pltpu.SemaphoreType.DMA((20,)),pltpu.SemaphoreType.DMA((3,))],
+        out_shape=(S((tokens,d),BF),S((tokens,d),BF),S((8,d),F32),S((4,2,d//8,hd3),BF),S((2,d//4,d),BF)),
+        in_specs=[VM,VM,ANY]+[VM]*5+[ANY,VM],out_specs=(ANY,)*5,
+        scratch_shapes=[V((4*tokens,d),BF),V((4*tokens,d),BF),V((tokens,d),BF),V((tokens,d),BF),V((tokens//2,d),BF),V((tokens//2,d),BF),
+            V((d,hd3),BF),V((d//2,hd3),BF),V((d,d),BF),V((4,d//2,hd3),BF),V((4,2,d//8,hd3),BF),
+            V((d//8,d),BF),V((d//8,d),BF),V((d//4,d),BF),V((d//4,d),BF),V((d//4,d),BF),V((4,d//4,d),BF),V((d//4,d),BF),
+            V((8,d),F32),V((3,8,d),F32),V((7,8,d),F32),
+            pltpu.SemaphoreType.DMA((52,)),pltpu.SemaphoreType.DMA((52,)),pltpu.SemaphoreType.DMA((8,))],
         compiler_params=pltpu.CompilerParams(vmem_limit_bytes=63*2**20,collective_id=1,has_side_effects=True),
         cost_estimate=pl.CostEstimate(flops=2*tokens*d*d*10,bytes_accessed=60*2**20,transcendentals=0))(
-        gq,heads,normed,hidden,gmid,gain,block,long,wskip)
+        gq,heads,normed,hidden,gmid,gain,block,long,wskip,small)
+
+def assemble_kernel(gin_ref,gsk_ref,skip_ref,gq_ref,um_ref,uo_ref,dm_ref,do_ref,om_ref,oo_ref,
+                    gin_out,gsk_out,skip_out,qkv_out,up_out,down_out,out_out,
+                    s0,s1,s2,s3,s4,s5,s6,local):
+    first=lax.axis_index("core")==0
+    copies=[]
+    def put(src,dst):
+        copy=pltpu.make_async_copy(src,dst,local.at[len(copies)]); copy.start(); copies.append(copy)
+    def chunks(n,body,size=144):
+        @pl.loop(0,n//size)
+        def _(i): body(pl.ds(pl.multiple_of(i*size,16),size))
+    def wide(dst,src):
+        def body(r): dst[r,:]=src[r,:].astype(F32)
+        chunks(dst.shape[0],body,208 if dst.shape[0]%208==0 else 144)
+    wide(s0,gin_ref); put(s0,gin_out)
+    wide(s1,gsk_ref); put(s1,gsk_out)
+    def pair(dst,mine,other):
+        h=mine.shape[0]
+        a=mine.shape[0]
+        def body(r):
+            m,o=mine[r,:].astype(F32),other[r,:].astype(F32)
+            dst[0,r,:]=jnp.where(first,m,o)
+            dst[1,r,:]=jnp.where(first,o,m)
+        chunks(h,body)
+    pair(s5,dm_ref,do_ref); put(s5,down_out)
+    pair(s6,om_ref,oo_ref); put(s6,out_out)
+    fb=um_ref.shape[1]//4
+    def up(r):
+        m,o=um_ref[r,:].astype(F32),uo_ref[r,:].astype(F32)
+        a,b=jnp.where(first,m,o),jnp.where(first,o,m)
+        s4[r,:]=jnp.concatenate([v[:,p*fb:(p+1)*fb] for p in range(4) for v in (a,b)],axis=1)
+    chunks(s4.shape[0],up,48); put(s4,up_out)
+    def skip(r): s2[r,:]=skip_ref[r,:].astype(F32)
+    chunks(s2.shape[0],skip); put(s2,skip_out)
+    hd=gq_ref.shape[3]//3; kh=gq_ref.shape[2]
+    for core in range(2):
+        for i in range(kh//48):
+            r=pl.ds(i*48,48)
+            s3[pl.ds(core*kh+i*48,48),:]=jnp.concatenate([gq_ref[p,core,r,s*hd:(s+1)*hd].astype(F32) for s in range(3) for p in range(4)],axis=1)
+    put(s3,qkv_out)
+    for copy in copies: copy.wait()
+
+def assemble(gin,gsk,skip,gq,um,uo,dm,do,om,oo):
+    S=lambda *s: jax.ShapeDtypeStruct(s,F32)
+    tokens,d=gin.shape
+    shapes=(S(tokens,d),S(tokens,d),S(*skip.shape),S(d//4,3*d),S(d//4,2*um.shape[1]),S(2,*dm.shape),S(2,*om.shape))
+    return pl.pallas_call(assemble_kernel,out_shape=shapes,in_specs=[VM]*10,out_specs=(ANY,)*7,
+        scratch_shapes=[pltpu.VMEM(s.shape,F32) for s in shapes]+[pltpu.SemaphoreType.DMA((7,))],
+        compiler_params=pltpu.CompilerParams(vmem_limit_bytes=60*2**20),
+        cost_estimate=pl.CostEstimate(flops=0,bytes_accessed=40*2**20,transcendentals=0))(
+        gin,gsk,skip,gq,um,uo,dm,do,om,oo)
 
 from jax.sharding import Mesh, PartitionSpec as P
 WIDE=("y","x"); ROWS=("z","core")
@@ -578,9 +757,13 @@
     grad_qkv,early=lax.optimization_barrier((grad_qkv,early))
     early=lax.psum(early,"z")
     if near:
-        gin,gsk,small1,gqkv,gskip=last(grad_qkv,w_heads,normed_all,hidden,gmid,gain1,block_input[0],long_skip[0],w_skip)
-        gqkv=gqkv.reshape(nw,-1,3*hd)
-        gskip=lax.psum_scatter(gskip,WIDE,scatter_dimension=0,tiled=True)
+        gin,gsk,smalls,gqkv,gskip=last(grad_qkv,w_heads,normed_all,hidden,gmid,gain1,block_input[0],long_skip[0],w_skip,small)
+        gskip,early=lax.optimization_barrier((gskip,early))
+        others=swap_cores(early)
+        gin,gsk,skip_share,qkv_share,up_share,down_share,out_share=assemble(gin,gsk,gskip.reshape(-1,d),gqkv,
+            early[0],others[0],early[1],others[1],early[2],others[2])
+        down_share,out_share=down_share.reshape(-1,d),out_share.reshape(-1,d)
+        smalls=lax.dynamic_slice_in_dim(smalls[:4],(2*lax.axis_index("y")+lax.axis_index("x"))*(d//nw),d//nw,axis=1).T
     else:
         part_first=nt(grad_qkv,w_heads).astype(BF)
         grad_first=lax.psum_scatter(part_first,WIDE,scatter_dimension=0,tiled=True).astype(F32)
@@ -593,16 +776,16 @@
         grad_joined=nt(grad_hidden,w_skip)
         gin,gsk=grad_joined[:,:d],grad_joined[:,d:]
         small1=jnp.stack([jnp.sum(grad_first*xhat1,axis=0),jnp.sum(grad_first,axis=0)])
-    gqkv,gskip,early=lax.optimization_barrier((gqkv,gskip,early))
-    gqkv,gskip=lax.psum((gqkv,gskip),"z")
-    up_share=both_cores(early[0].reshape(d//nw,nw,fb),2).reshape(d//nw,ff)
-    down_share=both_cores(early[1],0).reshape(ff//nw,d)
-    out_share=both_cores(early[2],0).reshape(d//nw,d)
-    skip_share=both_cores(gskip,0).reshape(2*d//nw,d)
-    gqkv=lax.all_to_all(gqkv,WIDE,0,0).reshape(nw,-1,3,hd).transpose(1,2,0,3)
-    qkv_share=both_cores(gqkv,0).reshape(d//nw,-1)
-    smalls=jnp.stack([small1[0],small1[1],small[0],small[1]],axis=1)
-    smalls=lax.psum(lax.psum_scatter(smalls.astype(BF),WIDE,scatter_dimension=0,tiled=True),ROWS).astype(F32)
+        gqkv,gskip,early=lax.optimization_barrier((gqkv,gskip,early))
+        gqkv,gskip=lax.psum((gqkv,gskip),"z")
+        up_share=both_cores(early[0].reshape(d//nw,nw,fb),2).reshape(d//nw,ff)
+        down_share=both_cores(early[1],0).reshape(ff//nw,d)
+        out_share=both_cores(early[2],0).reshape(d//nw,d)
+        skip_share=both_cores(gskip,0).reshape(2*d//nw,d)
+        gqkv=lax.all_to_all(gqkv,WIDE,0,0).reshape(nw,-1,3,hd).transpose(1,2,0,3)
+        qkv_share=both_cores(gqkv,0).reshape(d//nw,-1)
+        smalls=jnp.stack([small1[0],small1[1],small[0],small[1]],axis=1)
+        smalls=lax.psum(lax.psum_scatter(smalls.astype(BF),WIDE,scatter_dimension=0,tiled=True),ROWS).astype(F32)
     return (lay[None],gin[None],gsk[None],skip_share,smalls[:,0],smalls[:,1],qkv_share,out_share,
             smalls[:,2],smalls[:,3],up_share,down_share)
 

time: 947 us -> 853 us (0.901)
  waiting for transfers between devices: 308 us -> 152 us
  Pallas kernels: 428 us -> 562 us
  local copies, waits for them, and re-layouts: 88.1 us -> 48.7 us
  blocking collectives: 57.8 us -> 42.3 us
  other arithmetic: 30.3 us -> 16.1 us
    pallas_call x1 -> x2, Pallas kernels: 95.3 us -> 230 us  [the longest x1 216 us: last(): pl.pallas_call(last_kernel, out_shape=(S((tokens, d), BF), S((tokens, d),...]
    psum x1 -> x0, waiting for transfers between devices: 67.8 us -> none  [on_device(): gqkv, gskip = lax.psum((gqkv, gskip), 'z')]
    reduce_scatter x1 -> x0, waiting for transfers between devices: 42.2 us -> none  [on_device(): gskip = lax.psum_scatter(gskip, WIDE, scatter_dimension=0, tiled=True)]
    unnamed x11 -> x7, waiting for transfers between devices: 26.9 us -> 0.11 us
    convert_element_type x4 -> x0, local copies, waits for them, and re-layouts: 26.8 us -> none  [both_cores(): return place_halves(mine, swap_cores(mine), core, axis).astype(F32)]
    psum x1, waiting for transfers between devices: 22.4 us -> 0.02 us  [on_device(): early = lax.psum(early, 'z')]
    psum x1 -> x0, blocking collectives: 15.9 us -> none  [on_device(): lax.psum(lax.psum_scatter(smalls.astype(BF), WIDE, scatter_dimension=0, t...]
    ppermute x10 -> x8, waiting for transfers between devices: 17 us -> 20.3 us  [swap_cores(): return lax.ppermute(values, 'core', SWAP)]
  transfers between devices with their start and end apart: 22 -> 16, of which waited for: 10 -> 7; matrix products, arithmetic and copies ran while one was open for 10% -> 7% of each run, Pallas kernels for 23% -> 40%
where the time goes in v3:
time: 853 us; the launch traced here: 843 us
  Pallas kernels  562 us (66%)
  waiting for transfers between devices  152 us (18%)
  local copies, waits for them, and re-layouts  48.7 us (6%)
  blocking collectives  42.3 us (5%)
  other arithmetic  16.1 us (2%)
  between operations  14.7 us (2%)
    pallas_call x1, Pallas kernels, last(): pl.pallas_call(last_kernel, out_shape=(S((tokens, d), BF), S((tokens, d),...  216 us
    pallas_call x1, Pallas kernels, first(): pl.pallas_call(first_kernel, out_shape=(S((tokens, d), F32), S((4 * token...  109 us
    pallas_call x1, Pallas kernels, mlp(): pl.pallas_call(functools.partial(mlp_kernel, tile), out_shape=(S((tokens,...  104 us
    all_gather x3, waiting for transfers between devices, on_device(): gather = lambda v: lax.all_gather(v, WIDE, axis=0, tiled=True)  75.9 us
    pallas_call x1, Pallas kernels, attend_back(): pl.pallas_call(functools.partial(attend_back_kernel, heads), out_shape=ja...  75.2 us
    pallas_call x1, Pallas kernels, attend(): pl.pallas_call(functools.partial(attend_kernel, heads), out_shape=(jax.Sh...  43.5 us
    all_to_all x1, blocking collectives, on_device(): grad_heads = lax.all_to_all(gatt, WIDE, 0, 0).reshape(nw * tokens, hd)  42.3 us
    all_to_all x1, waiting for transfers between devices, on_device(): att = lax.all_to_all(att.reshape(nw, tokens, hd), WIDE, 0, 0)  29.6 us
  transfers between devices with their start and end apart: 16, of which 7 were waited for; matrix products, arithmetic and copies ran while one was open for 7% of the time, Pallas kernels for 40%

profile of v3, /device:TPU:0, one launch (start us, length us, event | category | flops | bytes accessed | tf_op | source)
XLA Modules:
  0.0 843.0 jit_solution(897590229394151973)
XLA Ops:
  7.2 0.0 all-gather.9.cloned.1.call-start
  7.2 0.7 stack.19
  7.9 0.7 stack.20
  8.6 0.7 stack.21
  9.3 0.7 stack.22
  10.0 0.6 convert_element_type.33.vec_ref
  10.6 109.2 %shard_map.220 = (f32[832,1152]{1,0:T(8,128)}, bf16[3328,1152]{1,0:T(8,128)(2,1)}, bf16[3328,864]{1,0:T(8,128)(2,1)}, bf16[1152,864]{1,0:T(8,128)(2,1)}, bf16[23...) custom-call(bf16[832,1152]{1,0:T(8,128)(2,1)} %bitcast.35, bf16[832,1152]{1,0:T(8,128)(2,1)} %bitcast.37, ...), custom_call_target="tpu_custom_call" | custom-call | flops 11041505280 | bytes 41943040 | tf_op jit(solution)/shard_map/pallas_call | solution.py:412
  119.8 1.2 constant_dynamic-slice_fusion.2
  121.0 0.0 all-gather.9.cloned.1.call-update
  121.0 0.3 all-gather.5.cloned.1.call-start
  121.3 7.3 reshape.64
  128.5 10.8 %dynamic-slice_reduce_fusion = bf16[288,4,576]{2,1,0:T(4,128)(2,1)} fusion(bf16[288,4,2,576]{3,2,1,0:T(2,128)(2,1)S(1)} %reshape.64, s32[]{:T(128)S(6)} %select_n.14), kind=kLoop, calls=%fused_computation.2 | loop fusion | bytes 2654212 | tf_op jit(solution)/shard_map/jit(dynamic_index_in_dim)/dynamic_slice | solution.py:699
  139.4 4.2 reshape.65
  143.6 0.0 all-gather.5.cloned.1.call-update
  143.6 0.0 all-gather.7.cloned.1.call-start
  143.7 43.5 %shard_map.221 = (bf16[3328,288]{1,0:T(8,128)(2,1)}, f32[12,12,384]{2,1,0:T(8,128)}) custom-call(s32[1,12]{1,0:T(1,128)} %len_ref.3, bf16[3328,864]{1,0:T(8,128)(2,1)} %get-tuple-element.58.qkv_ref), custom_call_target="tpu_custom_call" | custom-call | flops 12759072768 | bytes 12582912 | tf_op jit(solution)/shard_map/pallas_call | solution.py:131
  187.2 60.3 %all-gather.5.cloned.1.call-done.upo_ref = bf16[1152,2304]{1,0:T(8,128)(2,1)} async-done(((bf16[288,2304]{1,0:T(8,128)(2,1)}), bf16[1152,2304]{1,0:T(8,128)(2,1)}) %all-gather.5.cloned.1.call-update) | async-done | bytes 5308432 | tf_op jit(solution)/shard_map/all_gather | solution.py:718
  247.5 0.5 collective-permute-start.1
  248.0 0.0 all-gather.7.cloned.1.call-update
  248.0 4.3 copy.29
  252.3 3.6 all-to-all-start
  255.9 0.0 reduce-scatter.10.cloned.1.call-start
  256.0 1.0 slice_reduce_fusion
  257.0 0.7 slice.36.shift_ref
  257.6 0.7 slice.34.gain_ref
  258.3 29.6 %all-to-all-done = bf16[4,832,288]{1,2,0:T(8,128)(2,1)S(1)} async-done(((bf16[4,832,288]{1,2,0:T(8,128)(2,1)}), bf16[4,832,288]{1,2,0:T(8,128)(2,1)S(1)}, u32[]{:S(2)}, u32[]{:S(2)}) %all-to-all-start) | async-done | bytes 1916960 | tf_op jit(solution)/shard_map/all_to_all | solution.py:743
  288.0 2.7 copy.30.att_ref
  290.7 15.6 %all-gather.7.cloned.1.call-done.outw_ref = bf16[1152,1152]{1,0:T(8,128)(2,1)} async-done(((bf16[288,1152]{1,0:T(8,128)(2,1)}), bf16[1152,1152]{1,0:T(8,128)(2,1)}) %all-gather.7.cloned.1.call-update) | async-done | bytes 2654224 | tf_op jit(solution)/shard_map/all_gather | solution.py:718
  306.3 104.4 %shard_map.222 = (f32[832,1152]{1,0:T(8,128)}, f32[832,1152]{1,0:T(8,128)}, bf16[4,832,288]{2,1,0:T(8,128)(2,1)}, bf16[1152,1152]{1,0:T(8,128)(2,1)}, f32[8,1152...) custom-call(f32[832,1152]{1,0:T(8,128)} %get-tuple-element.56.hidden, ...), custom_call_target="tpu_custom_call" | custom-call | flops 59624128512 | bytes 62914560 | tf_op jit(solution)/shard_map/pallas_call | solution.py:266
  410.7 0.1 collective-permute-start.2
  410.8 1.9 constant_dynamic-slice_fusion.1
  412.7 0.5 collective-permute-start.4
  413.3 8.1 collective-permute-done.4
  421.4 1.5 fusion
  422.9 0.0 reduce-scatter.10.cloned.1.call-update
  423.0 0.0 reduce-scatter.6.cloned.1.call-start
  423.0 7.8 add_convert_fusion.1
  430.8 0.0 reduce-scatter.6.cloned.1.call-update
  430.8 0.0 reduce-scatter.8.cloned.1.call-start
  430.9 0.2 collective-permute-start.3
  431.1 8.8 %collective-permute-done.3 = bf16[2304,1152]{1,0:T(8,128)(2,1)S(1)} collective-permute-done((bf16[2304,1152]{1,0:T(8,128)(2,1)}, bf16[2304,1152]{1,0:T(8,128)(2,1)S(1)}, u32[]{:S(2)}, u32[]{:S(2)}) %collective-permute-start.3) | collective-permute-done | bytes 5308448 | tf_op jit(solution)/shard_map/ppermute | solution.py:696
  439.9 6.3 add_convert_fusion
  446.2 0.0 reduce-scatter.8.cloned.1.call-update
  446.2 0.0 all-reduce.4.cloned.1.call-start
  446.2 3.1 copy.31
  449.3 42.3 %all_to_all.10 = bf16[4,832,288]{1,2,0:T(8,128)(2,1)} all-to-all(bf16[4,832,288]{1,2,0:T(8,128)(2,1)S(1)} %copy.31), channel_id=1, replica_groups=mesh['z'=4,'core'=2,'y'=2,'x'=2] {'y','x'}, dimensions={0} | all-to-all | bytes 3833856 | tf_op jit(solution)/shard_map/all_to_all | solution.py:745
  491.6 4.3 copy.32
  495.9 75.2 %shard_map.223.gq_ref = bf16[3328,864]{1,0:T(8,128)(2,1)} custom-call(s32[1,12]{1,0:T(1,128)} %len_ref.3, bf16[3328,864]{1,0:T(8,128)(2,1)} %get-tuple-element.58.qkv_ref, bf16[3328,288]{1,0:T(8,128)(2,1)} %bitcast.24, f32[12,12,384]{2,1,0:T(8,128)} %get-tuple-element.69.lse_ref), custom_call_target="tpu_custom_call" | custom-call | flops 31897681920 | bytes 20971520 | tf_op jit(solution)/shard_map/pallas_call | solution.py:139
  571.2 25.9 %reduce-scatter.8.cloned.1.call-done = bf16[576,1152]{1,0:T(8,128)(2,1)} async-done(((bf16[2304,1152]{1,0:T(8,128)(2,1)}), bf16[576,1152]{1,0:T(8,128)(2,1)}) %reduce-scatter.8.cloned.1.call-update) | async-done | bytes 1327120 | tf_op jit(solution)/shard_map/reduce_scatter | solution.py:749
  597.1 0.0 all-reduce.4.cloned.1.call-update
  597.1 0.7 slice.38.gain_ref
  597.8 215.8 %shard_map.224 = (bf16[832,1152]{1,0:T(8,128)(2,1)}, bf16[832,1152]{1,0:T(8,128)(2,1)}, f32[8,1152]{1,0:T(8,128)}, bf16[4,2,144,864]{3,2,1,0:T(8,128)(2,1)}, bf16[2,288,1152]{2,1,0:T(8,128)(2,1)}) custom-call(bf16[3328,864]{1,0:T(8,128)(2,1)} %shard_map.223.gq_ref, bf16[1152,864]{1,0:T(8,128)(2,1)} %get-tuple-element.76.heads_ref, ...), custom_call_target="tpu_custom_call" | custom-call | flops 22083010560 | bytes 62914560 | tf_op jit(solution)/shard_map/pallas_call | solution.py:628
  813.6 0.0 all-reduce.4.cloned.1.call-done
  813.6 1.3 collective-permute-start.5
  814.9 0.1 collective-permute-start.6
  815.0 0.4 collective-permute-start.7
  815.4 0.8 slice.39
  816.2 0.1 dynamic-slice_bitcast_fusion
  816.2 0.6 slice_reduce_fusion.3
  816.9 3.3 collective-permute-done.7.oo_ref
  820.2 0.7 copy-done.3
  820.9 0.5 copy-done
  821.4 0.4 copy-done.1
  821.8 13.9 %shard_map.225 = (f32[832,1152]{1,0:T(8,128)}, f32[832,1152]{1,0:T(8,128)}, f32[576,1152]{1,0:T(8,128)}, f32[288,3456]{1,0:T(8,128)}, f32[288,4608]{1,0:T(8,128)...) custom-call(bf16[832,1152]{1,0:T(8,128)(2,1)} %get-tuple-element.81.gin_ref, ...), custom_call_target="tpu_custom_call" | custom-call | bytes 41943040 | tf_op jit(solution)/shard_map/pallas_call | solution.py:685
  (15 shorter events, 0.1 us)
Async XLA Ops:
  7.2 180.0 %all-gather.9.cloned.1.call-start = ((), (), s32[]{:S(2)}) async-start(), calls=%async_computation.9 | async-start | bytes 6635520 | tf_op jit(solution)/shard_map/all_gather | solution.py:718
  10.6 109.2 %copy-start.2 = (bf16[1152,1152]{1,0:T(8,128)(2,1)S(1)}, bf16[1152,1152]{1,0:T(8,128)(2,1)}, u32[]{:S(2)}) copy-start(bf16[1152,1152]{1,0:T(8,128)(2,1)} %param.25) | copy-start | bytes 7962628
  121.0 126.5 %all-gather.5.cloned.1.call-start = ((), (), s32[]{:S(2)}) async-start(), calls=%async_computation.5 | async-start | bytes 6635520 | tf_op jit(solution)/shard_map/all_gather | solution.py:718
  143.6 162.6 %all-gather.7.cloned.1.call-start = ((), (), s32[]{:S(2)}) async-start(), calls=%async_computation.6 | async-start | bytes 3317760 | tf_op jit(solution)/shard_map/all_gather | solution.py:718
  247.5 58.8 %collective-permute-start = (bf16[1152,2304]{1,0:T(8,128)(2,1)}, bf16[1152,2304]{1,0:T(8,128)(2,1)}, u32[]{:S(2)}, u32[]{:S(2)}) collective-permute-start(bf16[1152,2304]{1,0:T(8,128)(2,1)} %all-gather.5.cloned.1.call-done.upo_ref), channel_id=1, source_target_pairs={{0,4},{4,0},{1,5},{5,1},{2,6},{6,2},{3,7},{7,3},{8,12},{12,8},{9,1... | collective-permute-start | bytes 15925256 | tf_op jit(solution)/shard_map/ppermute | solution.py:696
  247.5 58.8 %collective-permute-start.1 = (bf16[2304,1152]{1,0:T(8,128)(2,1)}, bf16[2304,1152]{1,0:T(8,128)(2,1)}, u32[]{:S(2)}, u32[]{:S(2)}) collective-permute-start(bf16[2304,1152]{1,0:T(8,128)(2,1)} %bitcast.29), channel_id=1, source_target_pairs={{0,4},{4,0},{1,5},{5,1},{2,6},{6,2},{3,7},{7,3},{8,12},{12,8},{9,1... | collective-permute-start | bytes 15925256 | tf_op jit(solution)/shard_map/ppermute | solution.py:696
  252.3 35.6 %all-to-all-start = ((bf16[4,832,288]{1,2,0:T(8,128)(2,1)}), bf16[4,832,288]{1,2,0:T(8,128)(2,1)S(1)}, u32[]{:S(2)}, u32[]{:S(2)}) async-start(bf16[4,832,288]{1,2,0:T(8,128)(2,1)} %copy.29), calls=%async_computation | async-start | bytes 4128768 | tf_op jit(solution)/shard_map/all_to_all | solution.py:743
  255.9 315.2 %reduce-scatter.10.cloned.1.call-start = ((), (), s32[]{:S(2)}) async-start(), calls=%async_computation.10 | async-start | bytes 1658880
  410.7 12.3 %collective-permute-start.2 = (bf16[1152,2304]{1,0:T(8,128)(2,1)}, bf16[1152,2304]{1,0:T(8,128)(2,1)}, u32[]{:S(2)}, u32[]{:S(2)}) collective-permute-start(bf16[1152,2304]{1,0:T(8,128)(2,1)} %get-tuple-element.71), channel_id=1, source_target_pairs={{0,4},{4,0},{1,5},{5,1},{2,6},{6,2},{3,7},{7,3},{8,12},{12,8},{9,1... | collective-permute-start | bytes 15925256 | tf_op jit(solution)/shard_map/ppermute | solution.py:696
  412.7 8.7 %collective-permute-start.4 = (bf16[576,1152]{1,0:T(8,128)(2,1)S(1)}, bf16[576,1152]{1,0:T(8,128)(2,1)S(1)}, u32[]{:S(2)}, u32[]{:S(2)}) collective-permute-start(bf16[576,1152]{1,0:T(8,128)(2,1)S(1)} %bitcast.25), channel_id=1, source_target_pairs={{0,4},{4,0},{1,5},{5,1},{2,6},{6,2},{3,7},{7,3},{8,12},{12,8},{9,1... | collective-permute-start | bytes 3981320 | tf_op jit(solution)/shard_map/ppermute | solution.py:696
  423.0 148.2 %reduce-scatter.6.cloned.1.call-start = ((), (), s32[]{:S(2)}) async-start(), calls=%async_computation.7 | async-start | bytes 6635520 | tf_op jit(solution)/shard_map/reduce_scatter | solution.py:749
  430.8 166.3 %reduce-scatter.8.cloned.1.call-start = ((), (), s32[]{:S(2)}) async-start(), calls=%async_computation.8 | async-start | bytes 6635520 | tf_op jit(solution)/shard_map/reduce_scatter | solution.py:749
  430.9 9.0 %collective-permute-start.3 = (bf16[2304,1152]{1,0:T(8,128)(2,1)}, bf16[2304,1152]{1,0:T(8,128)(2,1)S(1)}, u32[]{:S(2)}, u32[]{:S(2)}) collective-permute-start(bf16[2304,1152]{1,0:T(8,128)(2,1)} %get-tuple-element.73), channel_id=1, source_target_pairs={{0,4},{4,0},{1,5},{5,1},{2,6},{6,2},{3,7},{7,3},{8,12},{12,8},{9,1... | collective-permute-start | bytes 15925256 | tf_op jit(solution)/shard_map/ppermute | solution.py:696
  446.2 367.4 %all-reduce.4.cloned.1.call-start = ((), (), s32[]{:S(2)}) async-start(), calls=%async_computation.11 | async-start | bytes 5971968 | tf_op jit(solution)/shard_map/psum | solution.py:758
  813.6 6.5 collective-permute-start.5
  814.9 5.3 collective-permute-start.6
  815.0 5.2 collective-permute-start.7
  820.2 0.7 copy-start.3
  820.2 1.2 copy-start
  820.2 1.6 copy-start.1
Sparse Core Ops, SparseCore 0:
  121.1 61.9 all-gather.8
  185.5 61.9 all-gather.4
  249.4 56.8 all-gather.6
  423.1 29.7 reduce-scatter.9
  456.6 74.7 reduce-scatter.5
  535.1 61.9 reduce-scatter.7
  599.9 158.4 all-reduce.3

commit v4 on v3

--- a/solution.py
+++ b/solution.py
@@ -637,9 +637,252 @@
         cost_estimate=pl.CostEstimate(flops=2*tokens*d*d*10,bytes_accessed=60*2**20,transcendentals=0))(
         gq,heads,normed,hidden,gmid,gain,block,long,wskip,small)
 
-def assemble_kernel(gin_ref,gsk_ref,skip_ref,gq_ref,um_ref,uo_ref,dm_ref,do_ref,om_ref,oo_ref,
-                    gin_out,gsk_out,skip_out,qkv_out,up_out,down_out,out_out,
-                    s0,s1,s2,s3,s4,s5,s6,local):
+SPLIT=((0,640),(640,512))
+def middle_kernel(hidden_ref,att_ref,g_ref,gain_ref,shift_ref,outw_ref,outx_ref,outy_ref,upw_ref,upx_ref,upy_ref,dnw_ref,
+                  lay_out,gmid_ref,gh_out,gow_out,small_ref,gup_out,gdn_out,uland,dland,
+                  att_in,att_s,outw_s,n2_s,xhat_s,rstd_s,lay_s,act_s,gu_s,upb,dnb,gub,gdb,land_u,land_d,
+                  send,recv,csend,crecv,fetch_sem,flush_sem,local):
+    x,y,c,w,wx,wy,wd=place()
+    tokens,d=hidden_ref.shape
+    cols=att_ref.shape[1]
+    kr=d//4; kh=kr//2; dh=d//2; dq=dh//2
+    tc=tokens//4; th=tokens//2
+    mul=pl.multiple_of
+    net=Links(send,recv)
+    left=[]
+    def start(k,t,src,dst,view):
+        pltpu.make_async_remote_copy(src_ref=src,dst_ref=dst,send_sem=send.at[k],recv_sem=recv.at[k],
+                                     device_id=net.to[t],device_id_type=MESH).start()
+        left.append((k,t,view))
+    def blk(b): return pl.ds(mul(b*d,128),d)
+    def urow(b,core): return pl.ds(mul(b*kr+core*kh,16),kh)
+    def drow(b,core,p): return pl.ds(mul(b*d+core*dh+p*dq,16),dq)
+    def trow(b): return pl.ds(mul(b*tokens,16),tokens)
+    uview=uland.at[pl.ds(0,kh),pl.ds(0,d)]
+    dview=dland.at[pl.ds(0,dq)]
+    net.meet("XYDC")
+    for j,(t,b) in enumerate((("X",wx),("Y",wy),("D",wd))):
+        start(j,t,att_ref.at[trow(b)],att_in.at[w],att_in.at[0])
+    own_att=pltpu.make_async_copy(att_ref.at[trow(w)],att_in.at[w],local.at[0])
+    own_att.start()
+    cut=kh//32*16+16
+    def orow(b,core,lo,n): return pl.ds(mul(b*kr+core*kh+lo,16),n)
+    start(3,"Y",outx_ref.at[pl.ds(0,cut)],outw_s.at[orow(wx,c,0,cut)],outw_s.at[pl.ds(0,cut)])
+    start(4,"X",outy_ref.at[pl.ds(cut,kh-cut)],outw_s.at[orow(wy,c,cut,kh-cut)],outw_s.at[pl.ds(0,kh-cut)])
+    start(5,"C",outx_ref,outw_s.at[urow(wx,c)],outw_s.at[pl.ds(0,kh)])
+    start(6,"C",outy_ref,outw_s.at[urow(wy,c)],outw_s.at[pl.ds(0,kh)])
+    start(7,"Y",upx_ref.at[:,blk(wy)],uland.at[urow(wx,c),blk(wy)],uview)
+    start(8,"X",upy_ref.at[:,blk(w)],uland.at[urow(wy,c),blk(w)],uview)
+    order=(w,wx,wy,wd)
+    def up_core(i):
+        start(11+2*i,"C",upx_ref.at[:,blk(order[i])],uland.at[urow(wx,c),blk(order[i])],uview)
+        start(12+2*i,"C",upy_ref.at[:,blk(order[i])],uland.at[urow(wy,c),blk(order[i])],uview)
+    up_core(0)
+    outw_s[pl.ds(mul(w*kr,16),kr),:]=outw_ref[...]
+    outw_s[urow(wx,c),:]=outx_ref[...]
+    outw_s[urow(wy,c),:]=outy_ref[...]
+
+    diag_id=(7,8,10,9)
+    def diag_from(i): return "Y" if i in (0,3) else "X"
+    def up_relay(i):
+        view=uland.at[urow(wd,c),blk(order[i])]
+        net.got(diag_id[i],diag_from(i),view)
+        start(19+i,"C",view,view,uview)
+    def up_sources(i):
+        b=order[i]
+        net.got(11+2*i,"C",uland.at[urow(wx,1-c),blk(b)])
+        net.got(12+2*i,"C",uland.at[urow(wy,1-c),blk(b)])
+        net.got(19+i,"C",uland.at[urow(wd,1-c),blk(b)])
+        return [(upw_ref.at[:,blk(b)],pl.ds(mul(w*kr,16),kr)),(upx_ref.at[:,blk(b)],urow(wx,c)),(upy_ref.at[:,blk(b)],urow(wy,c)),
+                (uland.at[urow(wx,1-c),blk(b)],urow(wx,1-c)),(uland.at[urow(wy,1-c),blk(b)],urow(wy,1-c)),
+                (uland.at[pl.ds(mul(wd*kr,16),kr),blk(b)],pl.ds(mul(wd*kr,16),kr))]
+    def fetch(i):
+        slot=i%2
+        for j,(src,rows) in enumerate(up_sources(i)):
+            pltpu.make_async_copy(src,upb.at[slot,rows],fetch_sem.at[slot,j]).start()
+        src=dnw_ref if i==0 else dland.at[pl.ds(mul(order[i]*d,16),d)]
+        pltpu.make_async_copy(src,dnb.at[slot],fetch_sem.at[slot,6]).start()
+    def fetched(slot):
+        for j,n in enumerate((kr,kh,kh,kh,kh,kr)):
+            view=upb.at[slot,pl.ds(0,n)]
+            pltpu.make_async_copy(view,view,fetch_sem.at[slot,j]).wait()
+        pltpu.make_async_copy(dnb.at[slot],dnb.at[slot],fetch_sem.at[slot,6]).wait()
+    def down_relay(k,t,b,p,onward):
+        r=drow(b,c,p)
+        net.got(k,t,dland.at[r])
+        for k2,t2 in onward: start(k2,t2,dland.at[r],dland.at[r],dview)
+    def down_core(k,b,p): net.got(k,"C",dland.at[drow(b,1-c,p)])
+
+    for j,(t,b) in enumerate((("X",wx),("Y",wy),("D",wd))):
+        net.got(j,t,att_in.at[b])
+    start(9,"Y",upx_ref.at[:,blk(wx)],uland.at[urow(wx,c),blk(wx)],uview)
+    start(10,"X",upy_ref.at[:,blk(wd)],uland.at[urow(wy,c),blk(wd)],uview)
+    def dmine(p): return dnw_ref.at[pl.ds(mul(c*dh+p*dq,16),dq)]
+    start(23,"X",dmine(0),dland.at[drow(w,c,0)],dview)
+    start(25,"Y",dmine(1),dland.at[drow(w,c,1)],dview)
+    start(24,"X",dmine(1),dland.at[drow(w,c,1)],dview)
+    start(26,"Y",dmine(0),dland.at[drow(w,c,0)],dview)
+    net.got(3,"Y",outw_s.at[orow(wd,c,0,cut)])
+    net.got(4,"X",outw_s.at[orow(wd,c,cut,kh-cut)])
+    start(35,"C",outw_s.at[urow(wd,c)],outw_s.at[urow(wd,c)],outw_s.at[pl.ds(0,kh)])
+    up_relay(0)
+    for i in (1,2,3): up_core(i)
+    net.got(5,"C",outw_s.at[urow(wx,1-c)]); net.got(6,"C",outw_s.at[urow(wy,1-c)])
+    net.got(35,"C",outw_s.at[urow(wd,1-c)])
+    own_att.wait()
+    fetch(0)
+    gain=gain_ref[...]; shift=shift_ref[...]
+    @pl.loop(0,4)
+    def _(i):
+        r=pl.ds(mul(i*tc,16),tc)
+        joined=jnp.concatenate([att_in[p,r,:] for p in range(4)],axis=1)
+        att_s[r,:]=joined
+        mid=hidden_ref[r,:]+nn(joined,outw_s[...])
+        lay_s[r,:]=mid
+        cen=mid-jnp.mean(mid,axis=1,keepdims=True)
+        inv=lax.rsqrt(jnp.mean(cen*cen,axis=1,keepdims=True)+1e-5)
+        xhat=cen*inv
+        xhat_s[r,:]=xhat
+        rstd_s[r,:]=jnp.broadcast_to(inv,(tc,128))
+        n2_s[r,:]=(xhat*gain+shift).astype(BF)
+        gmid_ref[r,:]=jnp.zeros((tc,d),F32)
+
+    def pieces(slot):
+        out=[(gub,pl.ds(mul(p*kr+(1-c)*kh,16),kh),land_u.at[slot,pl.ds(p*kh,kh)]) for p in range(4)]
+        return out+[(gdb,pl.ds(mul((1-c)*dh,16),dh),land_d.at[slot])]
+    def exchange(slot,act):
+        for j,(ref,r,dst) in enumerate(pieces(slot)):
+            act(pltpu.make_async_remote_copy(src_ref=ref.at[r],dst_ref=dst,send_sem=csend.at[slot,j],recv_sem=crecv.at[slot,j],
+                                             device_id=net.to["C"],device_id_type=MESH))
+    def flush(b,act):
+        for p in range(4):
+            act(pltpu.make_async_copy(gub.at[pl.ds(mul(p*kr+c*kh,16),kh)],gup_out.at[pl.ds(p*kh,kh),blk(b)],flush_sem.at[p]))
+        act(pltpu.make_async_copy(gdb.at[pl.ds(mul(c*dh,16),dh)],gdn_out.at[pl.ds(mul(b*dh,16),dh)],flush_sem.at[4]))
+    go=lambda copy: copy.start()
+    def finalize(i):
+        slot=lax.rem(i,2)
+        exchange(slot,lambda copy: copy.wait())
+        for p in range(4):
+            r=pl.ds(mul(p*kr+c*kh,16),kh)
+            gub[r,:]=(gub[r,:].astype(F32)+land_u[slot,pl.ds(p*kh,kh),:].astype(F32)).astype(BF)
+        for p in range(2):
+            r=pl.ds(mul(c*dh+p*dq,16),dq)
+            gdb[r,:]=(gdb[r,:].astype(F32)+land_d[slot,pl.ds(p*dq,dq),:].astype(F32)).astype(BF)
+    def block_of(i):
+        return 2*lax.rem(y+i//2,2)+lax.rem(x+lax.rem(i,2),2)
+
+    @pl.loop(0,4)
+    def _(i):
+        slot=lax.rem(i,2)
+        fetched(slot)
+        @pl.loop(0,2)
+        def _(t):
+            r=pl.ds(mul(t*th,16),th)
+            for lo,n in SPLIT:
+                f=pl.ds(lo,n)
+                u=nn(n2_s[r,:],upb[slot,:,f])
+                a,dg=gelu_parts(u)
+                act_s[r,f]=a.astype(BF)
+                gu_s[r,f]=(nt(g_ref[r,:],dnb[slot,f,:])*dg).astype(BF)
+        @pl.when(i>=1)
+        def _():
+            finalize(i-1)
+            flush(block_of(i-1),go)
+        @pl.when(i==0)
+        def _():
+            for j in (1,2,3): up_relay(j)
+        @pl.loop(0,2)
+        def _(t):
+            r=pl.ds(mul(t*th,16),th)
+            for lo,n in SPLIT:
+                f=pl.ds(lo,n)
+                lay_s[r,f]+=nn(act_s[r,:],dnb[slot,:,f])
+                gmid_ref[r,f]+=nt(gu_s[r,:],upb[slot,f,:])
+        @pl.when(i==0)
+        def _():
+            down_relay(23,"X",wx,0,((27,"Y"),(29,"C")))
+            down_relay(25,"Y",wy,1,((28,"X"),(30,"C")))
+            down_relay(24,"X",wx,1,((31,"C"),))
+            down_core(29,wx,0); down_core(31,wx,1)
+            fetch(1)
+        @pl.when(i==1)
+        def _():
+            down_relay(26,"Y",wy,0,((32,"C"),))
+            down_core(30,wy,1); down_core(32,wy,0)
+            down_relay(27,"Y",wd,0,((33,"C"),))
+            down_relay(28,"X",wd,1,((34,"C"),))
+            fetch(2)
+        @pl.when(i==2)
+        def _():
+            down_core(33,wd,0); down_core(34,wd,1)
+            fetch(3)
+        @pl.when(i>=1)
+        def _(): flush(block_of(i-1),lambda copy: copy.wait())
+        for lo,n in SPLIT:
+            f=pl.ds(lo,n)
+            gdb[f,:]=tn(act_s[:,f],g_ref[...]).astype(BF)
+            gub[f,:]=tn(n2_s[:,f],gu_s[...]).astype(BF)
+        exchange(slot,go)
+    act_s[...]=lay_s[...].astype(BF)
+    lay_copy=pltpu.make_async_copy(act_s,lay_out,local.at[1])
+    lay_copy.start()
+    small_ref[...]=jnp.zeros_like(small_ref)
+    for i in range(4):
+        r=pl.ds(i*tc,tc)
+        gs=gmid_ref[r,:]; xhat=xhat_s[r,:]
+        small_ref[0:1,:]+=jnp.sum(gs*xhat,axis=0,keepdims=True)
+        small_ref[1:2,:]+=jnp.sum(gs,axis=0,keepdims=True)
+        e=gs*gain
+        back=e-jnp.mean(e,axis=1,keepdims=True)-xhat*jnp.mean(e*xhat,axis=1,keepdims=True)
+        gm=g_ref[r,:].astype(F32)+back*rstd_s[r,0:1]
+        gmid_ref[r,:]=gm
+        low=gm.astype(BF)
+        n2_s[r,:]=low
+        ga=nt(low,outw_s[...]).astype(BF)
+        for p in range(4): att_in[p,r,:]=ga[:,p*cols:(p+1)*cols]
+        for j,(t,b) in enumerate((("X",wx),("Y",wy),("D",wd))):
+            start(36+3*i+j,t,att_in.at[b,r],gh_out.at[w,r],gh_out.at[0,pl.ds(0,tc)])
+    own_grad=pltpu.make_async_copy(att_in.at[w],gh_out.at[w],local.at[2])
+    own_grad.start()
+    finalize(3)
+    flush(wd,go)
+    flush(wd,lambda copy: copy.wait())
+    for lo,n in SPLIT:
+        f=pl.ds(lo,n)
+        gub[f,:]=tn(att_s[:,f],n2_s[...]).astype(BF)
+    for p in range(4):
+        start(48+p,"C",gub.at[pl.ds(mul(p*kr+(1-c)*kh,16),kh)],land_u.at[0,pl.ds(p*kh,kh)],land_u.at[0,pl.ds(0,kh)])
+    for p in range(4):
+        net.got(48+p,"C",land_u.at[0,pl.ds(p*kh,kh)])
+        r=pl.ds(mul(p*kr+c*kh,16),kh)
+        land_u[1,pl.ds(p*kh,kh),:]=(gub[r,:].astype(F32)+land_u[0,pl.ds(p*kh,kh),:].astype(F32)).astype(BF)
+    out_copy=pltpu.make_async_copy(land_u.at[1],gow_out,local.at[3])
+    out_copy.start()
+    for i in range(4):
+        for j,(t,b) in enumerate((("X",wx),("Y",wy),("D",wd))):
+            net.got(36+3*i+j,t,gh_out.at[b,pl.ds(i*tc,tc)])
+    for copy in (lay_copy,own_grad,out_copy): copy.wait()
+    for k,t,view in left:
+        pltpu.make_async_remote_copy(src_ref=view,dst_ref=view,send_sem=send.at[k],recv_sem=recv.at[k],
+                                     device_id=net.to[t],device_id_type=MESH).wait_send()
+
+def middle(hidden,att,g,gain,shift,outw,outx,outy,upw,upx,upy,dnw):
+    tokens,d=hidden.shape; cols=att.shape[1]; ff=upw.shape[1]
+    S=jax.ShapeDtypeStruct; V=pltpu.VMEM; D=pltpu.SemaphoreType.DMA
+    return pl.pallas_call(middle_kernel,
+        out_shape=(S((tokens,d),BF),S((tokens,d),F32),S((4,tokens,cols),BF),S((d//2,d),BF),S((8,d),F32),S((d//2,ff),BF),S((ff//2,d),BF),
+                   S((d,ff),BF),S((ff,d),BF)),
+        in_specs=[VM,ANY]+[VM]*6+[ANY]*4,out_specs=(ANY,VM,ANY,ANY,VM)+(ANY,)*4,
+        scratch_shapes=[V((4,tokens,cols),BF),V((tokens,d),BF),V((d,d),BF),V((tokens,d),BF),V((tokens,d),F32),V((tokens,128),F32),
+            V((tokens,d),F32),V((tokens,d),BF),V((tokens,d),BF),V((2,d,d),BF),V((2,d,d),BF),V((d,d),BF),V((d,d),BF),
+            V((2,d//2,d),BF),V((2,d//2,d),BF),D((52,)),D((52,)),D((2,5)),D((2,5)),D((2,7)),D((5,)),D((4,))],
+        compiler_params=pltpu.CompilerParams(vmem_limit_bytes=63*2**20,collective_id=2,has_side_effects=True),
+        cost_estimate=pl.CostEstimate(flops=2*tokens*d*(ff*6+d*3),bytes_accessed=60*2**20,transcendentals=tokens*ff*2))(
+        hidden,att,g,gain,shift,outw,outx,outy,upw,upx,upy,dnw)
+
+def assemble_kernel(lay_ref,gin_ref,gsk_ref,skip_ref,gq_ref,um_ref,uo_ref,dm_ref,do_ref,om_ref,oo_ref,
+                    lay_out,gin_out,gsk_out,skip_out,qkv_out,up_out,down_out,out_out,
+                    s0,s1,s2,s3,s4,s5,s6,s7,local):
     first=lax.axis_index("core")==0
     copies=[]
     def put(src,dst):
@@ -650,24 +893,19 @@
     def wide(dst,src):
         def body(r): dst[r,:]=src[r,:].astype(F32)
         chunks(dst.shape[0],body,208 if dst.shape[0]%208==0 else 144)
+    wide(s7,lay_ref); put(s7,lay_out)
     wide(s0,gin_ref); put(s0,gin_out)
     wide(s1,gsk_ref); put(s1,gsk_out)
-    def pair(dst,mine,other):
+    def pair(dst,mine,other,size=144):
         h=mine.shape[0]
-        a=mine.shape[0]
         def body(r):
             m,o=mine[r,:].astype(F32),other[r,:].astype(F32)
             dst[0,r,:]=jnp.where(first,m,o)
             dst[1,r,:]=jnp.where(first,o,m)
-        chunks(h,body)
+        chunks(h,body,size)
     pair(s5,dm_ref,do_ref); put(s5,down_out)
     pair(s6,om_ref,oo_ref); put(s6,out_out)
-    fb=um_ref.shape[1]//4
-    def up(r):
-        m,o=um_ref[r,:].astype(F32),uo_ref[r,:].astype(F32)
-        a,b=jnp.where(first,m,o),jnp.where(first,o,m)
-        s4[r,:]=jnp.concatenate([v[:,p*fb:(p+1)*fb] for p in range(4) for v in (a,b)],axis=1)
-    chunks(s4.shape[0],up,48); put(s4,up_out)
+    pair(s4,um_ref,uo_ref,48); put(s4,up_out)
     def skip(r): s2[r,:]=skip_ref[r,:].astype(F32)
     chunks(s2.shape[0],skip); put(s2,skip_out)
     hd=gq_ref.shape[3]//3; kh=gq_ref.shape[2]
@@ -678,15 +916,15 @@
     put(s3,qkv_out)
     for copy in copies: copy.wait()
 
-def assemble(gin,gsk,skip,gq,um,uo,dm,do,om,oo):
+def assemble(lay,gin,gsk,skip,gq,um,uo,dm,do,om,oo):
     S=lambda *s: jax.ShapeDtypeStruct(s,F32)
     tokens,d=gin.shape
-    shapes=(S(tokens,d),S(tokens,d),S(*skip.shape),S(d//4,3*d),S(d//4,2*um.shape[1]),S(2,*dm.shape),S(2,*om.shape))
-    return pl.pallas_call(assemble_kernel,out_shape=shapes,in_specs=[VM]*10,out_specs=(ANY,)*7,
-        scratch_shapes=[pltpu.VMEM(s.shape,F32) for s in shapes]+[pltpu.SemaphoreType.DMA((7,))],
+    shapes=(S(tokens,d),S(tokens,d),S(*skip.shape),S(d//4,3*d),S(2,*um.shape),S(2,*dm.shape),S(2,*om.shape))
+    return pl.pallas_call(assemble_kernel,out_shape=(shapes[0],)+shapes,in_specs=[VM]*11,out_specs=(ANY,)*8,
+        scratch_shapes=[pltpu.VMEM(s.shape,F32) for s in shapes+shapes[:1]]+[pltpu.SemaphoreType.DMA((8,))],
         compiler_params=pltpu.CompilerParams(vmem_limit_bytes=60*2**20),
         cost_estimate=pl.CostEstimate(flops=0,bytes_accessed=40*2**20,transcendentals=0))(
-        gin,gsk,skip,gq,um,uo,dm,do,om,oo)
+        lay,gin,gsk,skip,gq,um,uo,dm,do,om,oo)
 
 from jax.sharding import Mesh, PartitionSpec as P
 WIDE=("y","x"); ROWS=("z","core")
@@ -722,7 +960,10 @@
         hidden,normed_all,qkv,w_heads,w_skip,vecs=first(block_input[0],long_skip[0],skip_weight,qkv_weight,vecs)
         vec=vecs.transpose(1,0,2).reshape(8,d)
         gain1,shift1,gain2,shift2=[vec[i:i+1] for i in range(4)]
-        qkv,up_weight,down_weight,out_weight=lax.optimization_barrier((qkv,up_weight,down_weight,out_weight))
+        half=lambda v: lax.dynamic_slice_in_dim(v,core*(v.shape[0]//2),v.shape[0]//2)
+        qkv,up_half,out_half=lax.optimization_barrier((qkv,half(up_weight),half(out_weight)))
+        up_x,out_x=lax.ppermute((up_half,out_half),"x",SWAP)
+        up_y,out_y=lax.ppermute((up_half,out_half),"y",SWAP)
     else:
         vec=gather(vecs.astype(BF).T).T.astype(F32)
         gain1,shift1,gain2,shift2=[vec[i:i+1] for i in range(4)]
@@ -734,15 +975,19 @@
         xhat1,inv1=norm(hidden)
         normed_all=gather((xhat1*gain1+shift1).astype(BF))
         qkv=dot(normed_all,w_heads).astype(BF)
-    w_out=gather(out_weight)
-    up_mine=gather(pick(up_weight.reshape(d//nw,nw,2,fb),core,2).reshape(d//nw,nw*fb))
-    down_mine=gather(pick(down_weight.reshape(2,fb,d),core,0))
     att,lse=attend(item_lengths,qkv,heads)
-    att,up_mine,down_mine=lax.optimization_barrier((att,up_mine,down_mine))
-    up_other,down_other=swap_cores(up_mine),swap_cores(down_mine)
-    att=lax.all_to_all(att.reshape(nw,tokens,hd),WIDE,0,0)
-    lay,gmid,gatt,gow,small,gupo,guph,gdno,gdnh=mlp(hidden,att,w_out,gain2,shift2,output_grad[0],up_mine,up_other,down_mine,down_other)
-    grad_heads=lax.all_to_all(gatt,WIDE,0,0).reshape(nw*tokens,hd)
+    if near:
+        lay,gmid,gatt,gow,small,gup,gdn,_,_=middle(hidden,att,output_grad[0],gain2,shift2,out_weight,out_x,out_y,
+            up_weight,up_x,up_y,down_weight)
+    else:
+        w_out=gather(out_weight)
+        up_mine=gather(pick(up_weight.reshape(d//nw,nw,2,fb),core,2).reshape(d//nw,nw*fb))
+        down_mine=gather(pick(down_weight.reshape(2,fb,d),core,0))
+        up_other,down_other=swap_cores(up_mine),swap_cores(down_mine)
+        att=lax.all_to_all(att.reshape(nw,tokens,hd),WIDE,0,0)
+        lay,gmid,gatt,gow,small,gupo,guph,gdno,gdnh=mlp(hidden,att,w_out,gain2,shift2,output_grad[0],up_mine,up_other,down_mine,down_other)
+        gatt=lax.all_to_all(gatt,WIDE,0,0)
+    grad_heads=gatt.reshape(nw*tokens,hd)
 
     def scatter(mine,other):
         both=(mine.astype(F32)+swap_cores(other).astype(F32)).astype(BF)
@@ -752,7 +997,10 @@
     def by_rows(grad):
         cut=grad.reshape(nw,2,-1,grad.shape[1])
         return scatter(pick(cut,core,1).reshape(-1,grad.shape[1]),pick(cut,1-core,1).reshape(-1,grad.shape[1]))
-    early=scatter(gupo,guph),scatter(gdno,gdnh),by_rows(gow)
+    if near:
+        early=tuple(lax.psum_scatter(v,WIDE,scatter_dimension=0,tiled=True) for v in (gup,gdn,gow))
+    else:
+        early=scatter(gupo,guph),scatter(gdno,gdnh),by_rows(gow)
     grad_qkv=attend_back(item_lengths,qkv,grad_heads,lse,heads)
     grad_qkv,early=lax.optimization_barrier((grad_qkv,early))
     early=lax.psum(early,"z")
@@ -760,9 +1008,9 @@
         gin,gsk,smalls,gqkv,gskip=last(grad_qkv,w_heads,normed_all,hidden,gmid,gain1,block_input[0],long_skip[0],w_skip,small)
         gskip,early=lax.optimization_barrier((gskip,early))
         others=swap_cores(early)
-        gin,gsk,skip_share,qkv_share,up_share,down_share,out_share=assemble(gin,gsk,gskip.reshape(-1,d),gqkv,
+        lay,gin,gsk,skip_share,qkv_share,up_share,down_share,out_share=assemble(lay,gin,gsk,gskip.reshape(-1,d),gqkv,
             early[0],others[0],early[1],others[1],early[2],others[2])
-        down_share,out_share=down_share.reshape(-1,d),out_share.reshape(-1,d)
+        up_share,down_share,out_share=up_share.reshape(-1,ff),down_share.reshape(-1,d),out_share.reshape(-1,d)
         smalls=lax.dynamic_slice_in_dim(smalls[:4],(2*lax.axis_index("y")+lax.axis_index("x"))*(d//nw),d//nw,axis=1).T
     else:
         part_first=nt(grad_qkv,w_heads).astype(BF)

time: 853 us -> 780 us (0.914)
  the two profiles are of different devices: /device:TPU:0 before, /device:TPU:25 now
where the time goes in v4:
time: 780 us; the launch traced here: 765 us
  Pallas kernels  636 us (82%)
  waiting for transfers between devices  98.2 us (13%)
  between operations  14.1 us (2%)
  local copies, waits for them, and re-layouts  12 us (2%)
    pallas_call x1, Pallas kernels, last(): pl.pallas_call(last_kernel, out_shape=(S((tokens, d), BF), S((tokens, d),...  219 us
    pallas_call x1, Pallas kernels, middle(): pl.pallas_call(middle_kernel, out_shape=(S((tokens, d), BF), S((tokens, d...  186 us
    pallas_call x1, Pallas kernels, first(): pl.pallas_call(first_kernel, out_shape=(S((tokens, d), F32), S((4 * token...  108 us
    reduce_scatter x2, waiting for transfers between devices, on_device(): lax.psum_scatter(v, WIDE, scatter_dimension=0, tiled=True)  93.2 us
    pallas_call x1, Pallas kernels, attend_back(): pl.pallas_call(functools.partial(attend_back_kernel, heads), out_shape=ja...  67.5 us
    pallas_call x1, Pallas kernels, attend(): pl.pallas_call(functools.partial(attend_kernel, heads), out_shape=(jax.Sh...  39.6 us
  transfers between devices with their start and end apart: 11, of which 3 were waited for; matrix products, arithmetic and copies ran while one was open for 1% of the time, Pallas kernels for 43%

profile of v4, /device:TPU:25, one launch (start us, length us, event | category | flops | bytes accessed | tf_op | source)
XLA Modules:
  0.0 764.9 jit_solution(15649123711608911084)
XLA Ops:
  7.2 0.0 reduce-scatter.10.cloned.1.call-start
  7.2 0.7 stack.19
  7.9 0.7 stack.20
  8.6 0.7 stack.21
  9.3 0.7 stack.22
  10.0 0.6 convert_element_type.3.vec_ref
  10.6 1.0 constant_dynamic-slice_fusion
  11.6 1.4 constant_dynamic-slice_fusion.1
  13.0 107.8 %shard_map.220 = (f32[832,1152]{1,0:T(8,128)}, bf16[3328,1152]{1,0:T(8,128)(2,1)}, bf16[3328,864]{1,0:T(8,128)(2,1)}, bf16[1152,864]{1,0:T(8,128)(2,1)}, bf16[23...) custom-call(bf16[832,1152]{1,0:T(8,128)(2,1)} %bitcast.23, bf16[832,1152]{1,0:T(8,128)(2,1)} %bitcast.25, ...), custom_call_target="tpu_custom_call" | custom-call | flops 11041505280 | bytes 41943040 | tf_op jit(solution)/shard_map/pallas_call | solution.py:412
  120.9 0.9 collective-permute-start.3
  121.7 0.5 collective-permute-start.2
  122.3 0.6 collective-permute-start.1
  122.9 1.0 collective-permute-start
  123.9 39.6 %shard_map.221 = (bf16[3328,288]{1,0:T(8,128)(2,1)}, f32[12,12,384]{2,1,0:T(8,128)}) custom-call(s32[1,12]{1,0:T(1,128)} %len_ref.3, bf16[3328,864]{1,0:T(8,128)(2,1)} %get-tuple-element.53.qkv_ref), custom_call_target="tpu_custom_call" | custom-call | flops 12759072768 | bytes 12582912 | tf_op jit(solution)/shard_map/pallas_call | solution.py:131
  163.5 1.0 slice_reduce_fusion
  164.4 0.7 slice.36.shift_ref
  165.1 0.7 slice.34.gain_ref
  165.8 0.0 collective-permute-done.1.outy_ref
  165.8 0.0 copy-start.3
  165.8 0.0 collective-permute-done.outx_ref
  165.8 0.0 copy-start.4
  165.8 0.0 collective-permute-done.3.upy_ref
  165.8 0.0 collective-permute-done.2.upx_ref
  165.8 0.7 copy-done.3
  166.5 0.1 copy-done.4
  166.6 186.4 %shard_map.222 = (bf16[832,1152]{1,0:T(8,128)(2,1)}, f32[832,1152]{1,0:T(8,128)}, bf16[4,832,288]{2,1,0:T(8,128)(2,1)}, bf16[576,1152]{1,0:T(8,128)(2,1)}, f32[8...) custom-call(f32[832,1152]{1,0:T(8,128)} %get-tuple-element.51.hidden, ...), custom_call_target="tpu_custom_call" | custom-call | flops 59624128512 | bytes 62914560 | tf_op jit(solution)/shard_map/pallas_call | solution.py:872
  353.0 0.0 reduce-scatter.10.cloned.1.call-update
  353.0 0.0 reduce-scatter.6.cloned.1.call-start
  353.1 0.7 reduce-scatter.6.cloned.1.call-update
  353.8 0.0 reduce-scatter.8.cloned.1.call-start
  353.8 0.7 reduce-scatter.8.cloned.1.call-update
  354.5 0.0 all-reduce.4.cloned.1.call-start
  354.6 67.5 %shard_map.223.gq_ref = bf16[3328,864]{1,0:T(8,128)(2,1)} custom-call(s32[1,12]{1,0:T(1,128)} %len_ref.3, bf16[3328,864]{1,0:T(8,128)(2,1)} %get-tuple-element.53.qkv_ref, bf16[3328,288]{1,0:T(8,128)(2,1)} %bitcast.28, f32[12,12,384]{2,1,0:T(8,128)} %get-tuple-element.60.lse_ref), custom_call_target="tpu_custom_call" | custom-call | flops 31897681920 | bytes 20971520 | tf_op jit(solution)/shard_map/pallas_call | solution.py:139
  422.1 0.0 reduce-scatter.10.cloned.1.call-done
  422.1 27.9 %reduce-scatter.6.cloned.1.call-done = bf16[144,4608]{1,0:T(8,128)(2,1)} async-done(((bf16[576,4608]{1,0:T(8,128)(2,1)}), bf16[144,4608]{1,0:T(8,128)(2,1)}) %reduce-scatter.6.cloned.1.call-update) | async-done | bytes 1327120 | tf_op jit(solution)/shard_map/reduce_scatter | solution.py:1001
  450.0 65.3 %reduce-scatter.8.cloned.1.call-done = bf16[576,1152]{1,0:T(8,128)(2,1)} async-done(((bf16[2304,1152]{1,0:T(8,128)(2,1)}), bf16[576,1152]{1,0:T(8,128)(2,1)}) %reduce-scatter.8.cloned.1.call-update) | async-done | bytes 1327120 | tf_op jit(solution)/shard_map/reduce_scatter | solution.py:1001
  515.3 0.0 all-reduce.4.cloned.1.call-update
  515.3 0.7 slice.38.gain_ref
  516.0 219.2 %shard_map.224 = (bf16[832,1152]{1,0:T(8,128)(2,1)}, bf16[832,1152]{1,0:T(8,128)(2,1)}, f32[8,1152]{1,0:T(8,128)}, bf16[4,2,144,864]{3,2,1,0:T(8,128)(2,1)}, bf16[2,288,1152]{2,1,0:T(8,128)(2,1)}) custom-call(bf16[3328,864]{1,0:T(8,128)(2,1)} %shard_map.223.gq_ref, bf16[1152,864]{1,0:T(8,128)(2,1)} %get-tuple-element.65.heads_ref, ...), custom_call_target="tpu_custom_call" | custom-call | flops 22083010560 | bytes 62914560 | tf_op jit(solution)/shard_map/pallas_call | solution.py:628
  735.2 0.0 all-reduce.4.cloned.1.call-done
  735.2 0.1 collective-permute-start.4
  735.3 0.5 collective-permute-start.5
  735.8 0.1 collective-permute-start.6
  735.8 0.8 slice.39
  736.6 0.1 dynamic-slice_bitcast_fusion
  736.7 0.6 slice_reduce_fusion.3
  737.3 3.6 collective-permute-done.6.oo_ref
  740.9 0.0 copy-start.2
  740.9 0.0 collective-permute-done.4.uo_ref
  740.9 0.0 copy-start
  740.9 0.0 collective-permute-done.5.do_ref
  740.9 0.0 copy-start.1
  740.9 0.7 copy-done.2
  741.6 0.4 copy-done
  742.1 0.4 copy-done.1
  742.5 15.6 %shard_map.225 = (f32[832,1152]{1,0:T(8,128)}, f32[832,1152]{1,0:T(8,128)}, f32[832,1152]{1,0:T(8,128)}, f32[576,1152]{1,0:T(8,128)}, f32[288,3456]{1,0:T(8,128)...) custom-call(bf16[832,1152]{1,0:T(8,128)(2,1)} %get-tuple-element.58.lay_ref, ...), custom_call_target="tpu_custom_call" | custom-call | bytes 41943040 | tf_op jit(solution)/shard_map/pallas_call | solution.py:923
  (1 shorter events, 0.0 us)
Async XLA Ops:
  7.2 414.9 %reduce-scatter.10.cloned.1.call-start = ((), (), s32[]{:S(2)}) async-start(), calls=%async_computation.5 | async-start | bytes 1658880
  120.9 45.0 %collective-permute-start.3 = (bf16[144,4608]{1,0:T(8,128)(2,1)S(1)}, bf16[144,4608]{1,0:T(8,128)(2,1)}, u32[]{:S(2)}, u32[]{:S(2)}) collective-permute-start(bf16[144,4608]{1,0:T(8,128)(2,1)S(1)} %constant_dynamic-slice_fusion.1), channel_id=1, source_target_pairs={{0,2},{2,0},{1,3},{3,1},{4,6},{6,4},{5,7},{7,5},{8,10},{10,8},{9,1... | collective-permute-start | bytes 3981320 | tf_op jit(solution)/shard_map/ppermute | solution.py:966
  121.7 44.1 %collective-permute-start.2 = (bf16[144,4608]{1,0:T(8,128)(2,1)S(1)}, bf16[144,4608]{1,0:T(8,128)(2,1)}, u32[]{:S(2)}, u32[]{:S(2)}) collective-permute-start(bf16[144,4608]{1,0:T(8,128)(2,1)S(1)} %constant_dynamic-slice_fusion.1), channel_id=1, source_target_pairs={{0,1},{1,0},{2,3},{3,2},{4,5},{5,4},{6,7},{7,6},{8,9},{9,8},{10,11... | collective-permute-start | bytes 3981320 | tf_op jit(solution)/shard_map/ppermute | solution.py:965
  122.3 43.6 %collective-permute-start.1 = (bf16[144,1152]{1,0:T(8,128)(2,1)S(1)}, bf16[144,1152]{1,0:T(8,128)(2,1)S(1)}, u32[]{:S(2)}, u32[]{:S(2)}) collective-permute-start(bf16[144,1152]{1,0:T(8,128)(2,1)S(1)} %constant_dynamic-slice_fusion), channel_id=1, source_target_pairs={{0,2},{2,0},{1,3},{3,1},{4,6},{6,4},{5,7},{7,5},{8,10},{10,8},{9,1... | collective-permute-start | bytes 995336 | tf_op jit(solution)/shard_map/ppermute | solution.py:966
  122.9 43.0 %collective-permute-start = (bf16[144,1152]{1,0:T(8,128)(2,1)S(1)}, bf16[144,1152]{1,0:T(8,128)(2,1)S(1)}, u32[]{:S(2)}, u32[]{:S(2)}) collective-permute-start(bf16[144,1152]{1,0:T(8,128)(2,1)S(1)} %constant_dynamic-slice_fusion), channel_id=1, source_target_pairs={{0,1},{1,0},{2,3},{3,2},{4,5},{5,4},{6,7},{7,6},{8,9},{9,8},{10,11... | collective-permute-start | bytes 995336 | tf_op jit(solution)/shard_map/ppermute | solution.py:965
  165.8 0.7 copy-start.3
  165.8 0.8 copy-start.4
  353.0 96.9 %reduce-scatter.6.cloned.1.call-start = ((), (), s32[]{:S(2)}) async-start(), calls=%async_computation.3 | async-start | bytes 6635520 | tf_op jit(solution)/shard_map/reduce_scatter | solution.py:1001
  353.8 161.5 %reduce-scatter.8.cloned.1.call-start = ((), (), s32[]{:S(2)}) async-start(), calls=%async_computation.4 | async-start | bytes 6635520 | tf_op jit(solution)/shard_map/reduce_scatter | solution.py:1001
  354.5 380.6 %all-reduce.4.cloned.1.call-start = ((), (), s32[]{:S(2)}) async-start(), calls=%async_computation.6 | async-start | bytes 5971968 | tf_op jit(solution)/shard_map/psum | solution.py:1006
  735.2 5.7 collective-permute-start.4
  735.3 5.6 collective-permute-start.5
  735.8 5.1 collective-permute-start.6
  740.9 0.7 copy-start.2
  740.9 1.2 copy-start
  740.9 1.6 copy-start.1
Sparse Core Ops, SparseCore 0:
  353.2 31.4 reduce-scatter.9
  388.0 61.9 reduce-scatter.5
  453.3 61.9 reduce-scatter.7
  517.9 156.8 all-reduce.3

commit v5 on v4

--- a/solution.py
+++ b/solution.py
@@ -639,9 +639,9 @@
 
 SPLIT=((0,640),(640,512))
 def middle_kernel(hidden_ref,att_ref,g_ref,gain_ref,shift_ref,outw_ref,outx_ref,outy_ref,upw_ref,upx_ref,upy_ref,dnw_ref,
-                  lay_out,gmid_ref,gh_out,gow_out,small_ref,gup_out,gdn_out,uland,dland,
-                  att_in,att_s,outw_s,n2_s,xhat_s,rstd_s,lay_s,act_s,gu_s,upb,dnb,gub,gdb,land_u,land_d,
-                  send,recv,csend,crecv,fetch_sem,flush_sem,local):
+                  lay_out,gmid_ref,gh_out,gow_out,small_ref,gup_out,gdn_out,sxu_out,sxd_out,syu_out,syd_out,uland,dland,ux_out,uy_out,dx_out,dy_out,
+                  att_in,att_s,outw_s,n2_s,xhat_s,rstd_s,lay_s,act_s,gu_s,upb,dnb,gub,gdb,land_u,land_d,low_s,
+                  send,recv,csend,crecv,fetch_sem,flush_sem,local,usem,urecv,bring_sem):
     x,y,c,w,wx,wy,wd=place()
     tokens,d=hidden_ref.shape
     cols=att_ref.shape[1]
@@ -673,7 +673,7 @@
     start(6,"C",outy_ref,outw_s.at[urow(wy,c)],outw_s.at[pl.ds(0,kh)])
     start(7,"Y",upx_ref.at[:,blk(wy)],uland.at[urow(wx,c),blk(wy)],uview)
     start(8,"X",upy_ref.at[:,blk(w)],uland.at[urow(wy,c),blk(w)],uview)
-    order=(w,wx,wy,wd)
+    order=(w,wx,wd,wy)
     def up_core(i):
         start(11+2*i,"C",upx_ref.at[:,blk(order[i])],uland.at[urow(wx,c),blk(order[i])],uview)
         start(12+2*i,"C",upy_ref.at[:,blk(order[i])],uland.at[urow(wy,c),blk(order[i])],uview)
@@ -682,8 +682,8 @@
     outw_s[urow(wx,c),:]=outx_ref[...]
     outw_s[urow(wy,c),:]=outy_ref[...]
 
-    diag_id=(7,8,10,9)
-    def diag_from(i): return "Y" if i in (0,3) else "X"
+    diag_id=(7,8,9,10)
+    def diag_from(i): return "YX"[i%2]
     def up_relay(i):
         view=uland.at[urow(wd,c),blk(order[i])]
         net.got(diag_id[i],diag_from(i),view)
@@ -759,6 +759,7 @@
             act(pltpu.make_async_copy(gub.at[pl.ds(mul(p*kr+c*kh,16),kh)],gup_out.at[pl.ds(p*kh,kh),blk(b)],flush_sem.at[p]))
         act(pltpu.make_async_copy(gdb.at[pl.ds(mul(c*dh,16),dh)],gdn_out.at[pl.ds(mul(b*dh,16),dh)],flush_sem.at[4]))
     go=lambda copy: copy.start()
+    done=lambda copy: copy.wait()
     def finalize(i):
         slot=lax.rem(i,2)
         exchange(slot,lambda copy: copy.wait())
@@ -769,8 +770,24 @@
             r=pl.ds(mul(c*dh+p*dq,16),dq)
             gdb[r,:]=(gdb[r,:].astype(F32)+land_d[slot,pl.ds(p*dq,dq),:].astype(F32)).astype(BF)
     def block_of(i):
-        return 2*lax.rem(y+i//2,2)+lax.rem(x+lax.rem(i,2),2)
-
+        return 2*lax.rem(y+i//2,2)+lax.rem(x+(i+1)//2,2)
+
+    usend=[pl.ds(0,cut),pl.ds(cut,kh-cut)]
+    def ahead(i,b,act):
+        for j,(t,dst) in enumerate((("X",ux_out),("Y",uy_out))):
+            n=usend[j]
+            src=gup_out.at[pl.ds(mul(wd*kh+n.start,16),n.size),blk(b)]
+            act(pltpu.make_async_remote_copy(src_ref=src,dst_ref=dst.at[:,blk(b)],send_sem=usem.at[i,j],recv_sem=urecv.at[i,j],
+                                             device_id=net.to[t],device_id_type=MESH))
+    def ahead_down(act):
+        for j,(t,dst) in enumerate((("X",dx_out),("Y",dy_out))):
+            act(pltpu.make_async_remote_copy(src_ref=gdn_out.at[pl.ds(mul(wd*dh+j*dq,16),dq)],dst_ref=dst,
+                                             send_sem=usem.at[4,j],recv_sem=urecv.at[4,j],device_id=net.to[t],device_id_type=MESH))
+    def weight_grads():
+        for lo,n in SPLIT:
+            f=pl.ds(lo,n)
+            gdb[f,:]=tn(act_s[:,f],g_ref[...]).astype(BF)
+            gub[f,:]=tn(n2_s[:,f],gu_s[...]).astype(BF)
     @pl.loop(0,4)
     def _(i):
         slot=lax.rem(i,2)
@@ -807,25 +824,25 @@
             fetch(1)
         @pl.when(i==1)
         def _():
-            down_relay(26,"Y",wy,0,((32,"C"),))
-            down_core(30,wy,1); down_core(32,wy,0)
             down_relay(27,"Y",wd,0,((33,"C"),))
             down_relay(28,"X",wd,1,((34,"C"),))
+            down_relay(26,"Y",wy,0,((32,"C"),))
+            down_core(33,wd,0); down_core(34,wd,1)
             fetch(2)
         @pl.when(i==2)
         def _():
-            down_core(33,wd,0); down_core(34,wd,1)
+            down_core(30,wy,1); down_core(32,wy,0)
             fetch(3)
         @pl.when(i>=1)
-        def _(): flush(block_of(i-1),lambda copy: copy.wait())
-        for lo,n in SPLIT:
-            f=pl.ds(lo,n)
-            gdb[f,:]=tn(act_s[:,f],g_ref[...]).astype(BF)
-            gub[f,:]=tn(n2_s[:,f],gu_s[...]).astype(BF)
-        exchange(slot,go)
-    act_s[...]=lay_s[...].astype(BF)
-    lay_copy=pltpu.make_async_copy(act_s,lay_out,local.at[1])
-    lay_copy.start()
+        def _():
+            flush(block_of(i-1),done)
+            ahead(i-1,block_of(i-1),go)
+        @pl.when(i==3)
+        def _(): ahead_down(go)
+        @pl.when(i<3)
+        def _():
+            weight_grads()
+            exchange(slot,go)
     small_ref[...]=jnp.zeros_like(small_ref)
     for i in range(4):
         r=pl.ds(i*tc,tc)
@@ -837,31 +854,64 @@
         gm=g_ref[r,:].astype(F32)+back*rstd_s[r,0:1]
         gmid_ref[r,:]=gm
         low=gm.astype(BF)
-        n2_s[r,:]=low
+        low_s[r,:]=low
         ga=nt(low,outw_s[...]).astype(BF)
         for p in range(4): att_in[p,r,:]=ga[:,p*cols:(p+1)*cols]
         for j,(t,b) in enumerate((("X",wx),("Y",wy),("D",wd))):
             start(36+3*i+j,t,att_in.at[b,r],gh_out.at[w,r],gh_out.at[0,pl.ds(0,tc)])
     own_grad=pltpu.make_async_copy(att_in.at[w],gh_out.at[w],local.at[2])
     own_grad.start()
+    weight_grads()
+    exchange(1,go)
+    act_s[...]=lay_s[...].astype(BF)
+    lay_copy=pltpu.make_async_copy(act_s,lay_out,local.at[1])
+    lay_copy.start()
     finalize(3)
-    flush(wd,go)
-    flush(wd,lambda copy: copy.wait())
+    flush(wy,go)
+    flush(wy,done)
+    ahead(3,wy,go)
     for lo,n in SPLIT:
         f=pl.ds(lo,n)
-        gub[f,:]=tn(att_s[:,f],n2_s[...]).astype(BF)
+        gub[f,:]=tn(att_s[:,f],low_s[...]).astype(BF)
     for p in range(4):
         start(48+p,"C",gub.at[pl.ds(mul(p*kr+(1-c)*kh,16),kh)],land_u.at[0,pl.ds(p*kh,kh)],land_u.at[0,pl.ds(0,kh)])
+    def bring(k,src,dst):
+        copy=pltpu.make_async_copy(src,dst,bring_sem.at[k]); copy.start(); return copy
+    def spot(j,b): return pl.ds((4*j+b)*kh,kh)
+    copies=[]
+    for j,b2 in enumerate((wx,wy)):
+        for b in range(4):
+            copies.append(bring(4*j+b,gup_out.at[pl.ds(mul(b2*kh,16),kh),pl.ds(b*d,d)],upb.at[0,spot(j,b)]))
+        copies.append(bring(16+j,gdn_out.at[pl.ds(mul(b2*dh,16),dh)],dnb.at[0,pl.ds(j*dh,dh)]))
+    for i in range(4): ahead(i,order[i],done)
+    ahead_down(done)
+    for j,(src,n) in enumerate(((uy_out,usend[1]),(ux_out,usend[0]))):
+        for b in range(4):
+            copies.append(bring(8+4*j+b,src.at[:,pl.ds(b*d,d)],upb.at[1,pl.ds((4*j+b)*kh,n.size)]))
+    copies.append(bring(18,dy_out,dnb.at[1,pl.ds(0,dq)]))
+    copies.append(bring(19,dx_out,dnb.at[1,pl.ds(dq,dq)]))
+    for copy in copies: copy.wait()
+    copies=[]
+    for j,(uo,do) in enumerate(((sxu_out,sxd_out),(syu_out,syd_out))):
+        n=usend[1-j]
+        for b in range(4):
+            lo=(4*j+b)*kh
+            r=pl.ds(lo+n.start,n.size)
+            upb[0,r,:]=(upb[0,r,:].astype(F32)+upb[1,pl.ds(lo,n.size),:].astype(F32)).astype(BF)
+            copies.append(bring(4*j+b,upb.at[0,spot(j,b)],uo.at[:,pl.ds(b*d,d)]))
+        r=pl.ds(j*dh+(1-j)*dq,dq)
+        dnb[0,r,:]=(dnb[0,r,:].astype(F32)+dnb[1,pl.ds(j*dq,dq),:].astype(F32)).astype(BF)
+        copies.append(bring(16+j,dnb.at[0,pl.ds(j*dh,dh)],do.at[pl.ds(0,dh)]))
     for p in range(4):
         net.got(48+p,"C",land_u.at[0,pl.ds(p*kh,kh)])
         r=pl.ds(mul(p*kr+c*kh,16),kh)
         land_u[1,pl.ds(p*kh,kh),:]=(gub[r,:].astype(F32)+land_u[0,pl.ds(p*kh,kh),:].astype(F32)).astype(BF)
-    out_copy=pltpu.make_async_copy(land_u.at[1],gow_out,local.at[3])
-    out_copy.start()
+    for k,(b,dst) in enumerate(((w,gow_out.at[0]),(wd,gow_out.at[1]),(wx,sxd_out.at[pl.ds(dh,kh)]),(wy,syd_out.at[pl.ds(dh,kh)]))):
+        copies.append(bring(8+k,land_u.at[1,pl.ds(mul(b*kh,16),kh)],dst))
     for i in range(4):
         for j,(t,b) in enumerate((("X",wx),("Y",wy),("D",wd))):
             net.got(36+3*i+j,t,gh_out.at[b,pl.ds(i*tc,tc)])
-    for copy in (lay_copy,own_grad,out_copy): copy.wait()
+    for copy in [lay_copy,own_grad]+copies: copy.wait()
     for k,t,view in left:
         pltpu.make_async_remote_copy(src_ref=view,dst_ref=view,send_sem=send.at[k],recv_sem=recv.at[k],
                                      device_id=net.to[t],device_id_type=MESH).wait_send()
@@ -869,13 +919,16 @@
 def middle(hidden,att,g,gain,shift,outw,outx,outy,upw,upx,upy,dnw):
     tokens,d=hidden.shape; cols=att.shape[1]; ff=upw.shape[1]
     S=jax.ShapeDtypeStruct; V=pltpu.VMEM; D=pltpu.SemaphoreType.DMA
+    kh=d//8; cut=kh//32*16+16
     return pl.pallas_call(middle_kernel,
-        out_shape=(S((tokens,d),BF),S((tokens,d),F32),S((4,tokens,cols),BF),S((d//2,d),BF),S((8,d),F32),S((d//2,ff),BF),S((ff//2,d),BF),
-                   S((d,ff),BF),S((ff,d),BF)),
-        in_specs=[VM,ANY]+[VM]*6+[ANY]*4,out_specs=(ANY,VM,ANY,ANY,VM)+(ANY,)*4,
+        out_shape=(S((tokens,d),BF),S((tokens,d),F32),S((4,tokens,cols),BF),S((2,kh,d),BF),S((8,d),F32),S((d//2,ff),BF),S((ff//2,d),BF),
+                   S((kh,ff),BF),S((ff//8+kh,d),BF),S((kh,ff),BF),S((ff//8+kh,d),BF),
+                   S((d,ff),BF),S((ff,d),BF),S((cut,ff),BF),S((kh-cut,ff),BF),S((ff//16,d),BF),S((ff//16,d),BF)),
+        in_specs=[VM,ANY]+[VM]*6+[ANY]*4,out_specs=(ANY,VM,ANY,ANY,VM)+(ANY,)*12,
         scratch_shapes=[V((4,tokens,cols),BF),V((tokens,d),BF),V((d,d),BF),V((tokens,d),BF),V((tokens,d),F32),V((tokens,128),F32),
             V((tokens,d),F32),V((tokens,d),BF),V((tokens,d),BF),V((2,d,d),BF),V((2,d,d),BF),V((d,d),BF),V((d,d),BF),
-            V((2,d//2,d),BF),V((2,d//2,d),BF),D((52,)),D((52,)),D((2,5)),D((2,5)),D((2,7)),D((5,)),D((4,))],
+            V((2,d//2,d),BF),V((2,d//2,d),BF),V((tokens,d),BF),D((52,)),D((52,)),D((2,5)),D((2,5)),D((2,7)),D((5,)),D((4,)),
+            D((5,2)),D((5,2)),D((20,))],
         compiler_params=pltpu.CompilerParams(vmem_limit_bytes=63*2**20,collective_id=2,has_side_effects=True),
         cost_estimate=pl.CostEstimate(flops=2*tokens*d*(ff*6+d*3),bytes_accessed=60*2**20,transcendentals=tokens*ff*2))(
         hidden,att,g,gain,shift,outw,outx,outy,upw,upx,upy,dnw)
@@ -977,8 +1030,8 @@
         qkv=dot(normed_all,w_heads).astype(BF)
     att,lse=attend(item_lengths,qkv,heads)
     if near:
-        lay,gmid,gatt,gow,small,gup,gdn,_,_=middle(hidden,att,output_grad[0],gain2,shift2,out_weight,out_x,out_y,
-            up_weight,up_x,up_y,down_weight)
+        lay,gmid,gatt,gow,small,gup,gdn,sxu,sxd,syu,syd=middle(hidden,att,output_grad[0],gain2,shift2,out_weight,out_x,out_y,
+            up_weight,up_x,up_y,down_weight)[:11]
     else:
         w_out=gather(out_weight)
         up_mine=gather(pick(up_weight.reshape(d//nw,nw,2,fb),core,2).reshape(d//nw,nw*fb))
@@ -998,10 +1051,22 @@
         cut=grad.reshape(nw,2,-1,grad.shape[1])
         return scatter(pick(cut,core,1).reshape(-1,grad.shape[1]),pick(cut,1-core,1).reshape(-1,grad.shape[1]))
     if near:
-        early=tuple(lax.psum_scatter(v,WIDE,scatter_dimension=0,tiled=True) for v in (gup,gdn,gow))
+        wide=2*lax.axis_index("y")+lax.axis_index("x")
+        part=lambda v: lax.dynamic_index_in_dim(v.reshape(4,-1,v.shape[1]),wide,0,False)
+        from_x=lax.ppermute((sxu,sxd),"x",SWAP)
+        from_y=lax.ppermute((syu,syd),"y",SWAP)
+        from_d=lax.ppermute(gow[1],WIDE,[(i,3-i) for i in range(4)])
     else:
         early=scatter(gupo,guph),scatter(gdno,gdnh),by_rows(gow)
     grad_qkv=attend_back(item_lengths,qkv,grad_heads,lse,heads)
+    if near:
+        grad_qkv,from_x,from_y,from_d=lax.optimization_barrier((grad_qkv,from_x,from_y,from_d))
+        up_sum=part(gup).astype(F32)+from_x[0].astype(F32)+from_y[0].astype(F32)
+        rows=gdn.shape[0]//4
+        pair=from_x[1].astype(F32)+from_y[1].astype(F32)
+        down_sum=part(gdn).astype(F32)+pair[:rows]
+        out_sum=gow[0].astype(F32)+pair[rows:]+from_d.astype(F32)
+        early=up_sum.astype(BF),down_sum.astype(BF),out_sum.astype(BF)
     grad_qkv,early=lax.optimization_barrier((grad_qkv,early))
     early=lax.psum(early,"z")
     if near:

time: 780 us -> 723 us (0.927)
  the two profiles are of different devices: /device:TPU:25 before, /device:TPU:0 now
where the time goes in v5:
time: 723 us; the launch traced here: 714 us
  Pallas kernels  662 us (92%)
  between operations  14.6 us (2%)
  local copies, waits for them, and re-layouts  14 us (2%)
  starting transfers between devices  11.8 us (2%)
  other arithmetic  8.22 us (1%)
    pallas_call x1, Pallas kernels, last(): pl.pallas_call(last_kernel, out_shape=(S((tokens, d), BF), S((tokens, d),...  213 us
    pallas_call x1, Pallas kernels, middle(): pl.pallas_call(middle_kernel, out_shape=(S((tokens, d), BF), S((tokens, d...  205 us
    pallas_call x1, Pallas kernels, first(): pl.pallas_call(first_kernel, out_shape=(S((tokens, d), F32), S((4 * token...  109 us
    pallas_call x1, Pallas kernels, attend_back(): pl.pallas_call(functools.partial(attend_back_kernel, heads), out_shape=ja...  75.2 us
    pallas_call x1, Pallas kernels, attend(): pl.pallas_call(functools.partial(attend_kernel, heads), out_shape=(jax.Sh...  43.8 us
    pallas_call x1, Pallas kernels, assemble(): pl.pallas_call(assemble_kernel, out_shape=(shapes[0],) + shapes, in_specs...  15.6 us
  transfers between devices with their start and end apart: 13, of which 1 were waited for; matrix products, arithmetic and copies ran while one was open for 1% of the time, Pallas kernels for 46%

profile of v5, /device:TPU:0, one launch (start us, length us, event | category | flops | bytes accessed | tf_op | source)
XLA Modules:
  0.0 713.9 jit_solution(11134183806949487638)
XLA Ops:
  7.2 0.0 all-reduce.3.cloned.1.call-start
  7.2 0.7 stack.19
  7.9 0.7 stack.20
  8.6 0.7 stack.21
  9.3 0.7 stack.22
  10.0 0.6 convert_element_type.45.vec_ref
  10.6 1.0 constant_dynamic-slice_fusion
  11.6 1.4 constant_dynamic-slice_fusion.1
  13.0 109.0 %shard_map.220 = (f32[832,1152]{1,0:T(8,128)}, bf16[3328,1152]{1,0:T(8,128)(2,1)}, bf16[3328,864]{1,0:T(8,128)(2,1)}, bf16[1152,864]{1,0:T(8,128)(2,1)}, bf16[23...) custom-call(bf16[832,1152]{1,0:T(8,128)(2,1)} %bitcast.37, bf16[832,1152]{1,0:T(8,128)(2,1)} %bitcast.39, ...), custom_call_target="tpu_custom_call" | custom-call | flops 11041505280 | bytes 41943040 | tf_op jit(solution)/shard_map/pallas_call | solution.py:412
  122.0 1.1 collective-permute-start.3
  123.2 0.6 collective-permute-start.2
  123.8 0.9 collective-permute-start.1
  124.7 1.5 collective-permute-start
  126.2 43.8 %shard_map.221 = (bf16[3328,288]{1,0:T(8,128)(2,1)}, f32[12,12,384]{2,1,0:T(8,128)}) custom-call(s32[1,12]{1,0:T(1,128)} %len_ref.3, bf16[3328,864]{1,0:T(8,128)(2,1)} %get-tuple-element.63.qkv_ref), custom_call_target="tpu_custom_call" | custom-call | flops 12759072768 | bytes 12582912 | tf_op jit(solution)/shard_map/pallas_call | solution.py:131
  170.0 1.0 slice_reduce_fusion
  171.0 0.7 slice.48.shift_ref
  171.7 0.7 slice.46.gain_ref
  172.3 0.0 collective-permute-done.1.outy_ref
  172.3 0.0 copy-start.5
  172.3 0.0 collective-permute-done.outx_ref
  172.4 0.0 collective-permute-done.3.upy_ref
  172.4 0.0 copy-start.4
  172.4 0.0 collective-permute-done.2.upx_ref
  172.4 1.1 copy-done.4
  173.5 0.1 copy-done.5
  173.5 205.3 %shard_map.222 = (bf16[832,1152]{1,0:T(8,128)(2,1)}, f32[832,1152]{1,0:T(8,128)}, bf16[4,832,288]{2,1,0:T(8,128)(2,1)}, bf16[2,144,1152]{2,1,0:T(8,128)(2,1)}, f...) custom-call(f32[832,1152]{1,0:T(8,128)} %get-tuple-element.61.hidden, ...), custom_call_target="tpu_custom_call" | custom-call | flops 59624128512 | bytes 62914560 | tf_op jit(solution)/shard_map/pallas_call | solution.py:923
  378.9 1.0 slice_bitcast_fusion
  379.9 1.9 collective-permute-start.8
  381.7 0.5 collective-permute-start.4
  382.3 1.2 collective-permute-start.6
  383.4 1.4 collective-permute-start.5
  384.8 0.9 collective-permute-start.7
  385.8 75.2 %shard_map.223.gq_ref = bf16[3328,864]{1,0:T(8,128)(2,1)} custom-call(s32[1,12]{1,0:T(1,128)} %len_ref.3, bf16[3328,864]{1,0:T(8,128)(2,1)} %get-tuple-element.63.qkv_ref, bf16[3328,288]{1,0:T(8,128)(2,1)} %bitcast.42, f32[12,12,384]{2,1,0:T(8,128)} %get-tuple-element.70.lse_ref), custom_call_target="tpu_custom_call" | custom-call | flops 31897681920 | bytes 20971520 | tf_op jit(solution)/shard_map/pallas_call | solution.py:139
  461.0 0.0 copy-start.2
  461.0 0.0 collective-permute-done.8
  461.0 0.0 collective-permute-done.4
  461.0 0.0 collective-permute-done.6
  461.0 0.0 collective-permute-done.5
  461.0 0.0 collective-permute-done.7
  461.0 0.4 convert_add_fusion
  461.5 0.6 copy-done.2
  462.1 0.8 fusion.4
  462.9 2.7 fusion
  465.6 3.7 fusion.2
  469.3 0.0 all-reduce.3.cloned.1.call-update
  469.3 0.7 slice.54.gain_ref
  470.0 212.9 %shard_map.224 = (bf16[832,1152]{1,0:T(8,128)(2,1)}, bf16[832,1152]{1,0:T(8,128)(2,1)}, f32[8,1152]{1,0:T(8,128)}, bf16[4,2,144,864]{3,2,1,0:T(8,128)(2,1)}, bf16[2,288,1152]{2,1,0:T(8,128)(2,1)}) custom-call(bf16[3328,864]{1,0:T(8,128)(2,1)} %shard_map.223.gq_ref, bf16[1152,864]{1,0:T(8,128)(2,1)} %get-tuple-element.85.heads_ref, ...), custom_call_target="tpu_custom_call" | custom-call | flops 22083010560 | bytes 62914560 | tf_op jit(solution)/shard_map/pallas_call | solution.py:628
  682.8 0.0 all-reduce.3.cloned.1.call-done
  682.9 1.2 collective-permute-start.9
  684.1 0.1 collective-permute-start.10
  684.1 0.4 collective-permute-start.11
  684.6 0.8 slice.55
  685.4 0.1 dynamic-slice_bitcast_fusion
  685.4 0.6 slice_reduce_fusion.3
  686.0 3.3 collective-permute-done.11.oo_ref
  689.3 0.0 copy-start.3
  689.3 0.0 collective-permute-done.9.uo_ref
  689.3 0.0 copy-start
  689.3 0.0 collective-permute-done.10.do_ref
  689.4 0.0 copy-start.1
  689.4 0.7 copy-done.3
  690.1 0.4 copy-done
  690.5 0.5 copy-done.1
  691.0 15.6 %shard_map.225 = (f32[832,1152]{1,0:T(8,128)}, f32[832,1152]{1,0:T(8,128)}, f32[832,1152]{1,0:T(8,128)}, f32[576,1152]{1,0:T(8,128)}, f32[288,3456]{1,0:T(8,128)...) custom-call(bf16[832,1152]{1,0:T(8,128)(2,1)} %get-tuple-element.68.lay_ref, ...), custom_call_target="tpu_custom_call" | custom-call | bytes 41943040 | tf_op jit(solution)/shard_map/pallas_call | solution.py:976
  (1 shorter events, 0.0 us)
Async XLA Ops:
  7.2 675.7 %all-reduce.3.cloned.1.call-start = ((), (), s32[]{:S(2)}) async-start(), calls=%async_computation | async-start | bytes 5971968 | tf_op jit(solution)/shard_map/psum | solution.py:1071
  122.0 50.3 %collective-permute-start.3 = (bf16[144,4608]{1,0:T(8,128)(2,1)S(1)}, bf16[144,4608]{1,0:T(8,128)(2,1)S(1)}, u32[]{:S(2)}, u32[]{:S(2)}) collective-permute-start(bf16[144,4608]{1,0:T(8,128)(2,1)S(1)} %constant_dynamic-slice_fusion.1), channel_id=1, source_target_pairs={{0,2},{2,0},{1,3},{3,1},{4,6},{6,4},{5,7},{7,5},{8,10},{10,8},{9,1... | collective-permute-start | bytes 3981320 | tf_op jit(solution)/shard_map/ppermute | solution.py:1019
  123.2 49.2 %collective-permute-start.2 = (bf16[144,4608]{1,0:T(8,128)(2,1)S(1)}, bf16[144,4608]{1,0:T(8,128)(2,1)}, u32[]{:S(2)}, u32[]{:S(2)}) collective-permute-start(bf16[144,4608]{1,0:T(8,128)(2,1)S(1)} %constant_dynamic-slice_fusion.1), channel_id=1, source_target_pairs={{0,1},{1,0},{2,3},{3,2},{4,5},{5,4},{6,7},{7,6},{8,9},{9,8},{10,11... | collective-permute-start | bytes 3981320 | tf_op jit(solution)/shard_map/ppermute | solution.py:1018
  123.8 48.5 %collective-permute-start.1 = (bf16[144,1152]{1,0:T(8,128)(2,1)S(1)}, bf16[144,1152]{1,0:T(8,128)(2,1)S(1)}, u32[]{:S(2)}, u32[]{:S(2)}) collective-permute-start(bf16[144,1152]{1,0:T(8,128)(2,1)S(1)} %constant_dynamic-slice_fusion), channel_id=1, source_target_pairs={{0,2},{2,0},{1,3},{3,1},{4,6},{6,4},{5,7},{7,5},{8,10},{10,8},{9,1... | collective-permute-start | bytes 995336 | tf_op jit(solution)/shard_map/ppermute | solution.py:1019
  124.7 47.7 %collective-permute-start = (bf16[144,1152]{1,0:T(8,128)(2,1)S(1)}, bf16[144,1152]{1,0:T(8,128)(2,1)}, u32[]{:S(2)}, u32[]{:S(2)}) collective-permute-start(bf16[144,1152]{1,0:T(8,128)(2,1)S(1)} %constant_dynamic-slice_fusion), channel_id=1, source_target_pairs={{0,1},{1,0},{2,3},{3,2},{4,5},{5,4},{6,7},{7,6},{8,9},{9,8},{10,11... | collective-permute-start | bytes 995336 | tf_op jit(solution)/shard_map/ppermute | solution.py:1018
  172.3 1.2 copy-start.5
  172.4 1.1 copy-start.4
  379.9 81.1 %collective-permute-start.8 = (bf16[144,1152]{1,0:T(8,128)(2,1)S(1)}, bf16[144,1152]{1,0:T(8,128)(2,1)S(1)}, u32[]{:S(2)}, u32[]{:S(2)}) collective-permute-start(bf16[144,1152]{1,0:T(8,128)(2,1)S(1)} %slice_bitcast_fusion), channel_id=1, source_target_pairs={{0,3},{1,2},{2,1},{3,0},{4,7},{5,6},{6,5},{7,4},{8,11},{9,10},{10,... | collective-permute-start | bytes 995336 | tf_op jit(solution)/shard_map/ppermute | solution.py:1058
  381.7 79.2 %collective-permute-start.4 = (bf16[144,4608]{1,0:T(8,128)(2,1)}, bf16[144,4608]{1,0:T(8,128)(2,1)}, u32[]{:S(2)}, u32[]{:S(2)}) collective-permute-start(bf16[144,4608]{1,0:T(8,128)(2,1)} %get-tuple-element.71), channel_id=1, source_target_pairs={{0,1},{1,0},{2,3},{3,2},{4,5},{5,4},{6,7},{7,6},{8,9},{9,8},{10,11... | collective-permute-start | bytes 3981320 | tf_op jit(solution)/shard_map/ppermute | solution.py:1056
  382.3 78.7 %collective-permute-start.6 = (bf16[144,4608]{1,0:T(8,128)(2,1)}, bf16[144,4608]{1,0:T(8,128)(2,1)}, u32[]{:S(2)}, u32[]{:S(2)}) collective-permute-start(bf16[144,4608]{1,0:T(8,128)(2,1)} %get-tuple-element.73), channel_id=1, source_target_pairs={{0,2},{2,0},{1,3},{3,1},{4,6},{6,4},{5,7},{7,5},{8,10},{10,8},{9,1... | collective-permute-start | bytes 3981320 | tf_op jit(solution)/shard_map/ppermute | solution.py:1057
  383.4 77.6 %collective-permute-start.5 = (bf16[720,1152]{1,0:T(8,128)(2,1)}, bf16[720,1152]{1,0:T(8,128)(2,1)S(1)}, u32[]{:S(2)}, u32[]{:S(2)}) collective-permute-start(bf16[720,1152]{1,0:T(8,128)(2,1)} %get-tuple-element.72), channel_id=1, source_target_pairs={{0,1},{1,0},{2,3},{3,2},{4,5},{5,4},{6,7},{7,6},{8,9},{9,8},{10,11... | collective-permute-start | bytes 4976648 | tf_op jit(solution)/shard_map/ppermute | solution.py:1056
  384.8 76.2 %collective-permute-start.7 = (bf16[720,1152]{1,0:T(8,128)(2,1)}, bf16[720,1152]{1,0:T(8,128)(2,1)S(1)}, u32[]{:S(2)}, u32[]{:S(2)}) collective-permute-start(bf16[720,1152]{1,0:T(8,128)(2,1)} %get-tuple-element.74), channel_id=1, source_target_pairs={{0,2},{2,0},{1,3},{3,1},{4,6},{6,4},{5,7},{7,5},{8,10},{10,8},{9,1... | collective-permute-start | bytes 4976648 | tf_op jit(solution)/shard_map/ppermute | solution.py:1057
  461.0 1.1 copy-start.2
  682.9 6.5 collective-permute-start.9
  684.1 5.3 collective-permute-start.10
  684.1 5.2 collective-permute-start.11
  689.3 0.7 copy-start.3
  689.3 1.2 copy-start
  689.4 1.6 copy-start.1
Sparse Core Ops, SparseCore 0:
  469.4 156.9 all-reduce.2

commit v6 on v5

--- a/solution.py
+++ b/solution.py
@@ -419,9 +419,9 @@
         block,long,skipw,qkvw,vecs)
 
 class Chain:
-    def __init__(self,net,k,own,up_in,down_in,up_out,down_out):
+    def __init__(self,net,k,own,up_in,down_in):
         self.net,self.k,self.own=net,k,own
-        self.up_in,self.down_in,self.up_out,self.down_out=up_in,down_in,up_out,down_out
+        self.up_in,self.down_in=up_in,down_in
         self.z,self.n=lax.axis_index("z"),lax.axis_size("z")
     def copy(self,up,src):
         k=self.k+(0 if up else 1)
@@ -430,33 +430,31 @@
             device_id={"z":self.z+1 if up else self.z-1},device_id_type=MESH)
     def hop(self,h):
         for up in (True,False):
-            here=self.z==(h if up else self.n-1-h)
-            inn,out=(self.up_in,self.up_out) if up else (self.down_in,self.down_out)
-            @pl.when(here)
+            inn,other=(self.up_in,self.down_in) if up else (self.down_in,self.up_in)
+            last_one=self.n-1-h<h or (self.n-1-h==h and not up)
+            @pl.when(self.z==(h if up else self.n-1-h))
             def _():
                 if h==0:
                     self.copy(up,self.own).start()
                 else:
                     self.copy(up,inn).wait_recv()
-                    out[...]=(self.own[...].astype(F32)+inn[...].astype(F32)).astype(out.dtype)
-                    self.copy(up,out).start()
+                    mine,came=self.own[...].astype(F32),inn[...].astype(F32)
+                    inn[...]=(mine+came).astype(inn.dtype)
+                    if last_one:
+                        self.own[...]=(other[...].astype(F32)+came).astype(self.own.dtype)
+                    self.copy(up,inn).start()
     def total(self):
         first,final=self.z==0,self.z==self.n-1
-        @pl.when(first)
-        def _():
-            self.copy(False,self.down_in).wait_recv()
-            self.copy(True,self.own).wait_send()
-            self.own[...]=(self.own[...].astype(F32)+self.down_in[...].astype(F32)).astype(self.own.dtype)
-        @pl.when(final)
-        def _():
-            self.copy(True,self.up_in).wait_recv()
-            self.copy(False,self.own).wait_send()
-            self.own[...]=(self.own[...].astype(F32)+self.up_in[...].astype(F32)).astype(self.own.dtype)
+        for end,up,inn in ((first,True,self.down_in),(final,False,self.up_in)):
+            @pl.when(end)
+            def _():
+                self.copy(not up,inn).wait_recv()
+                self.copy(up,self.own).wait_send()
+                self.own[...]=(self.own[...].astype(F32)+inn[...].astype(F32)).astype(self.own.dtype)
         @pl.when(jnp.logical_not(first|final))
         def _():
-            self.copy(True,self.up_out).wait_send()
-            self.copy(False,self.down_out).wait_send()
-            self.own[...]=(self.own[...].astype(F32)+self.up_in[...].astype(F32)+self.down_in[...].astype(F32)).astype(self.own.dtype)
+            self.copy(True,self.up_in).wait_send()
+            self.copy(False,self.down_in).wait_send()
 
 def meet_all(net,who):
     z,n=lax.axis_index("z"),lax.axis_size("z")
@@ -474,9 +472,9 @@
     def _(): pl.semaphore_wait(barrier,len(who)+2)
 
 SEG=3
-def last_kernel(gq_ref,heads_ref,normed_ref,hidden_ref,gmid_ref,gain_ref,block_ref,long_ref,wskip_ref,small_ref,
-                gin_out,gsk_out,small_out,gqkv_out,gskip_out,
-                big,part,rx,ry,dx,dy,gw,gwr,gsr,qz,fq,sdx,sdy,srx,sry,own,sz,fs,sm,sin,smz,send,recv,local):
+def last_kernel(gq_ref,heads_ref,normed_ref,hidden_ref,gmid_ref,gain_ref,block_ref,long_ref,wskip_ref,small_ref,eu_ref,ed_ref,eo_ref,
+                gin_out,gsk_out,small_out,gqkv_out,gskip_out,early_out,late_out,
+                big,part,rx,ry,dx,dy,gw,gwr,gsr,qz,fq,sdx,sdy,srx,sry,own,sz,fs,sm,sin,smz,es,eup,edown,hg,send,recv,local,esem,hsem):
     x,y,c,w,wx,wy,wd=place()
     tokens,d=block_ref.shape
     tc=tokens//4; kr=d//4; kh=kr//2; sr=d//2; sh=sr//2; sq=sh//2
@@ -484,8 +482,26 @@
     net=Links(send,recv)
     load=pltpu.make_async_copy(normed_ref,big,local.at[0])
     load.start()
+    eseg=[pl.ds(i*kh,kh) for i in range(9)]
+    eload=[pltpu.make_async_copy(eu_ref.at[:,pl.ds(i*d,d)] if i<4 else ed_ref.at[pl.ds((i-4)*kh,kh)] if i<8 else eo_ref,es.at[eseg[i]],esem.at[i]) for i in range(9)]
+    for copy in eload: copy.start()
+    ford=(0,2,1,3)
+    def stream(j):
+        r=pl.ds(ford[j]*tc,tc)
+        return [pltpu.make_async_copy(ref.at[r],hg.at[j%2,m],hsem.at[j%2,m]) for m,ref in enumerate((hidden_ref,gmid_ref))]
+    for j in range(2):
+        for copy in stream(j): copy.start()
     meet_all(net,"XYDC")
     def tok(i): return pl.ds(i*tc,tc)
+    early=[Chain(net,56+2*i,es.at[r],eup.at[r],edown.at[r]) for i,r in enumerate(eseg)]
+    for copy in eload: copy.wait()
+    halves=[pl.ds(i*2*kh,2*kh) for i in range(2)]
+    mids=[Chain(net,40+2*i,gwr.at[r],qz.at[0,r],qz.at[1,r]) for i,r in enumerate(halves)]
+    queue=early[:3]+mids+early[3:]
+    for chain in queue[:3]: chain.hop(0)
+    def tick(i):
+        for h in range(1,lax.axis_size("z")-1):
+            if 0<=i-h+1<len(queue): queue[i-h+1].hop(h)
     def pr(s,i): return pl.ds(s*tokens+i*tc,tc)
     def partial(b,i):
         return nt(gq_ref[pl.ds(mul(b*tokens+i*tc,16),tc),:],heads_ref[...])
@@ -515,29 +531,30 @@
     relay(2,"X",wx,rx,6,dy,2,"Y")
     relay(0,"Y",wy,ry,8,dx,0,"X")
     weight_grad(1)
+    tick(0)
     weight_grad(2)
     def rows(b,core): return pl.ds(mul(b*kr+core*kh,16),kh)
     for b in range(4):
         net.start(12+b,"C",gw.at[rows(b,1-c)],gwr.at[pl.ds(b*kh,kh)])
     relay(3,"X",wx,rx,7,dy,3,"Y")
+    tick(1)
     relay(1,"Y",wy,ry,9,dx,1,"X")
+    tick(2)
     for b in range(4):
         r=pl.ds(b*kh,kh)
         net.got(12+b,"C",gwr.at[r])
         gwr[r,:]=(gwr[r,:].astype(F32)+gw[rows(b,c),:].astype(F32)).astype(BF)
-    halves=[pl.ds(i*2*kh,2*kh) for i in range(2)]
-    chains=[Chain(net,40+2*i,gwr.at[r],*[qz.at[j,r] for j in range(4)]) for i,r in enumerate(halves)]
-    for chain in chains: chain.hop(0)
+    for chain in queue[3:]: chain.hop(0)
     gain=gain_ref[...]
     sm[...]=jnp.zeros_like(sm)
-    for h in range(1,lax.axis_size("z")-2):
-        for chain in chains: chain.hop(h)
-    for i in (0,2,1,3):
+    for j,i in enumerate(ford):
         r=tok(i)
+        tick(3+j)
+        for copy in stream(j): copy.wait()
         net.got(4+i,"X",rx.at[r])
         net.got(8+i,"Y",ry.at[r])
         gf=part[pr(3,i),:].astype(F32)+rx[r,:].astype(F32)+ry[r,:].astype(F32)
-        h=hidden_ref[r,:]
+        h=hg[j%2,0]
         cen=h-jnp.mean(h,axis=1,keepdims=True)
         inv=lax.rsqrt(jnp.mean(cen*cen,axis=1,keepdims=True)+1e-5)
         xhat=cen*inv
@@ -545,20 +562,31 @@
         sm[1:2,:]+=jnp.sum(gf,axis=0,keepdims=True)
         e=gf*gain
         back=e-jnp.mean(e,axis=1,keepdims=True)-xhat*jnp.mean(e*xhat,axis=1,keepdims=True)
-        big[pl.ds(2*d+i*tc,tc),:]=(gmid_ref[r,:]+back*inv).astype(BF)
+        big[pl.ds(2*d+i*tc,tc),:]=(hg[j%2,1]+back*inv).astype(BF)
+        if j<2:
+            for copy in stream(j+2): copy.start()
     sm[2:4,:]=small_ref[0:2,:]
+    lates=[pltpu.make_async_copy(block_ref,rx,local.at[2]),pltpu.make_async_copy(long_ref,ry,local.at[3])]
+    for copy in lates: copy.start()
+    tick(7)
+    for chain in mids: chain.total()
+    def qrows(b): return pl.ds(mul(b*kh,16),kh)
+    for j,(t,b) in enumerate((("X",wx),("Y",wy),("D",wd))):
+        net.start(29+j,t,gwr.at[qrows(b)],fq.at[w,c])
+    fq[w,c]=gwr[qrows(w),:]
+    for copy in lates: copy.wait()
     for k in range(6):
-        src=block_ref if k<3 else long_ref
+        src=rx if k<3 else ry
         big[pl.ds(k*cc,cc),:]=tn(src[:,(k%3)*cc:(k%3+1)*cc],big[2*d:2*d+tokens,:]).astype(BF)
     def srows(b,core): return pl.ds(mul(b*sr+core*sh,16),sh)
     for b in range(4):
         net.start(16+b,"C",big.at[srows(b,1-c)],gsr.at[pl.ds(b*sh,sh)])
     net.start(20,"C",sm,sin.at[0])
+    tick(8)
     for copy in net.sent[:16]: copy.wait_send()
     net.sent=net.sent[16:]
     wload=pltpu.make_async_copy(wskip_ref,part.at[pl.ds(0,2*d)],local.at[1])
     wload.start()
-    for chain in chains: chain.hop(lax.axis_size("z")-2)
     for b in range(4):
         r=pl.ds(b*sh,sh)
         net.got(16+b,"C",gsr.at[r])
@@ -569,14 +597,10 @@
     net.start(22,"Y",gsr.at[quarter(wd,1)],sdy)
     net.start(23,"X",gsr.at[quarter(wx,0)],srx.at[top])
     net.start(24,"Y",gsr.at[quarter(wy,1)],sry.at[low])
+    tick(9)
     net.got(20,"C",sin.at[0])
     smz[6]=sm[...]+sin[0]
     net.start(27,"X",smz.at[6],sin.at[1])
-    for chain in chains: chain.total()
-    def qrows(b): return pl.ds(mul(b*kh,16),kh)
-    for j,(t,b) in enumerate((("X",wx),("Y",wy),("D",wd))):
-        net.start(29+j,t,gwr.at[qrows(b)],fq.at[w,c])
-    fq[w,c]=gwr[qrows(w),:]
     wload.wait()
     @pl.loop(0,4)
     def _(i):
@@ -588,12 +612,14 @@
     def put(k,src,dst):
         copy=pltpu.make_async_copy(src,dst,local.at[k]); copy.start(); outs.append(copy)
     put(2,rx,gin_out); put(3,ry,gsk_out)
+    tick(10)
     net.got(21,"X",sdx)
     gsr[quarter(wy,0),:]=(gsr[quarter(wy,0),:].astype(F32)+sdx[...].astype(F32)).astype(BF)
     net.start(25,"Y",gsr.at[quarter(wy,0)],sry.at[top])
     net.got(22,"Y",sdy)
     gsr[quarter(wx,1),:]=(gsr[quarter(wx,1),:].astype(F32)+sdy[...].astype(F32)).astype(BF)
     net.start(26,"X",gsr.at[quarter(wx,1)],srx.at[low])
+    for i in range(11,len(queue)+lax.axis_size("z")-3): tick(i)
     net.got(27,"X",sin.at[1])
     smz[0]=smz[6]+sin[1]
     net.start(28,"Y",smz.at[0],sin.at[2])
@@ -607,35 +633,41 @@
     net.got(24,"Y",sry.at[low]); net.got(26,"X",srx.at[low])
     own[...]=(gsr[pl.ds(mul(w*sh,16),sh),:].astype(F32)+srx[...].astype(F32)+sry[...].astype(F32)).astype(BF)
     seg=sh//SEG
-    chains=[Chain(net,44,smz.at[1],smz.at[2],smz.at[3],smz.at[4],smz.at[5])]
+    chains=[Chain(net,44,smz.at[1],smz.at[2],smz.at[3])]
     for i in range(SEG):
         r=pl.ds(i*seg,seg)
-        chains.append(Chain(net,46+2*i,own.at[r],*[sz.at[j,r] for j in range(4)]))
+        chains.append(Chain(net,46+2*i,own.at[r],sz.at[0,r],sz.at[1,r]))
     for h in range(lax.axis_size("z")-1):
         for chain in chains: chain.hop(h)
     for chain in chains: chain.total()
     net.start(36,"C",own,fs)
+    for i,chain in enumerate(early):
+        chain.total()
+        net.start(74+i,"C",es.at[eseg[i]],late_out.at[eseg[i]])
+    put(8,es,early_out)
     for b in range(4): net.got(32+b,"C",fq.at[b,1-c])
     put(4,fq,gqkv_out); put(5,smz.at[1],small_out); put(6,own,gskip_out.at[c])
     net.got(36,"C",fs)
     put(7,fs,gskip_out.at[1-c])
+    for i,r in enumerate(eseg): net.got(74+i,"C",late_out.at[r])
     for copy in outs: copy.wait()
     net.finish()
 
-def last(gq,heads,normed,hidden,gmid,gain,block,long,wskip,small):
+def last(gq,heads,normed,hidden,gmid,gain,block,long,wskip,small,eu,ed,eo):
     tokens,d=block.shape; S=jax.ShapeDtypeStruct; hd3=gq.shape[1]
     V=pltpu.VMEM
     return pl.pallas_call(last_kernel,
-        out_shape=(S((tokens,d),BF),S((tokens,d),BF),S((8,d),F32),S((4,2,d//8,hd3),BF),S((2,d//4,d),BF)),
-        in_specs=[VM,VM,ANY]+[VM]*5+[ANY,VM],out_specs=(ANY,)*5,
+        out_shape=(S((tokens,d),BF),S((tokens,d),BF),S((8,d),F32),S((4,2,d//8,hd3),BF),S((2,d//4,d),BF),S((9*d//8,d),BF),S((9*d//8,d),BF)),
+        in_specs=[VM,VM,ANY,ANY,ANY,VM,ANY,ANY,ANY,VM,ANY,ANY,ANY],out_specs=(ANY,)*7,
         scratch_shapes=[V((4*tokens,d),BF),V((4*tokens,d),BF),V((tokens,d),BF),V((tokens,d),BF),V((tokens//2,d),BF),V((tokens//2,d),BF),
-            V((d,hd3),BF),V((d//2,hd3),BF),V((d,d),BF),V((4,d//2,hd3),BF),V((4,2,d//8,hd3),BF),
-            V((d//8,d),BF),V((d//8,d),BF),V((d//4,d),BF),V((d//4,d),BF),V((d//4,d),BF),V((4,d//4,d),BF),V((d//4,d),BF),
+            V((d,hd3),BF),V((d//2,hd3),BF),V((d,d),BF),V((2,d//2,hd3),BF),V((4,2,d//8,hd3),BF),
+            V((d//8,d),BF),V((d//8,d),BF),V((d//4,d),BF),V((d//4,d),BF),V((d//4,d),BF),V((2,d//4,d),BF),V((d//4,d),BF),
             V((8,d),F32),V((3,8,d),F32),V((7,8,d),F32),
-            pltpu.SemaphoreType.DMA((52,)),pltpu.SemaphoreType.DMA((52,)),pltpu.SemaphoreType.DMA((8,))],
+            V((9*d//8,d),BF),V((9*d//8,d),BF),V((9*d//8,d),BF),V((2,2,tokens//4,d),F32),
+            pltpu.SemaphoreType.DMA((83,)),pltpu.SemaphoreType.DMA((83,)),pltpu.SemaphoreType.DMA((9,)),pltpu.SemaphoreType.DMA((9,)),pltpu.SemaphoreType.DMA((2,2))],
         compiler_params=pltpu.CompilerParams(vmem_limit_bytes=63*2**20,collective_id=1,has_side_effects=True),
         cost_estimate=pl.CostEstimate(flops=2*tokens*d*d*10,bytes_accessed=60*2**20,transcendentals=0))(
-        gq,heads,normed,hidden,gmid,gain,block,long,wskip,small)
+        gq,heads,normed,hidden,gmid,gain,block,long,wskip,small,eu,ed,eo)
 
 SPLIT=((0,640),(640,512))
 def middle_kernel(hidden_ref,att_ref,g_ref,gain_ref,shift_ref,outw_ref,outx_ref,outy_ref,upw_ref,upx_ref,upy_ref,dnw_ref,
@@ -933,7 +965,7 @@
         cost_estimate=pl.CostEstimate(flops=2*tokens*d*(ff*6+d*3),bytes_accessed=60*2**20,transcendentals=tokens*ff*2))(
         hidden,att,g,gain,shift,outw,outx,outy,upw,upx,upy,dnw)
 
-def assemble_kernel(lay_ref,gin_ref,gsk_ref,skip_ref,gq_ref,um_ref,uo_ref,dm_ref,do_ref,om_ref,oo_ref,
+def assemble_kernel(lay_ref,gin_ref,gsk_ref,skip_ref,gq_ref,em_ref,eo_ref,
                     lay_out,gin_out,gsk_out,skip_out,qkv_out,up_out,down_out,out_out,
                     s0,s1,s2,s3,s4,s5,s6,s7,local):
     first=lax.axis_index("core")==0
@@ -949,16 +981,20 @@
     wide(s7,lay_ref); put(s7,lay_out)
     wide(s0,gin_ref); put(s0,gin_out)
     wide(s1,gsk_ref); put(s1,gsk_out)
-    def pair(dst,mine,other,size=144):
-        h=mine.shape[0]
-        def body(r):
-            m,o=mine[r,:].astype(F32),other[r,:].astype(F32)
-            dst[0,r,:]=jnp.where(first,m,o)
-            dst[1,r,:]=jnp.where(first,o,m)
-        chunks(h,body,size)
-    pair(s5,dm_ref,do_ref); put(s5,down_out)
-    pair(s6,om_ref,oo_ref); put(s6,out_out)
-    pair(s4,um_ref,uo_ref,48); put(s4,up_out)
+    kh=s6.shape[1]; d=s6.shape[2]
+    def pair(dst,seg,rows,cols,size=48):
+        @pl.loop(0,kh//size)
+        def _(i):
+            r=pl.ds(pl.multiple_of(seg*kh+i*size,16),size)
+            to=pl.ds(pl.multiple_of(rows+i*size,16),size)
+            m,o=em_ref[r,:].astype(F32),eo_ref[r,:].astype(F32)
+            dst[0,to,cols]=jnp.where(first,m,o)
+            dst[1,to,cols]=jnp.where(first,o,m)
+    for b in range(4): pair(s4,b,0,pl.ds(b*d,d))
+    put(s4,up_out)
+    for b in range(4): pair(s5,4+b,b*kh,pl.ds(0,d))
+    put(s5,down_out)
+    pair(s6,8,0,pl.ds(0,d)); put(s6,out_out)
     def skip(r): s2[r,:]=skip_ref[r,:].astype(F32)
     chunks(s2.shape[0],skip); put(s2,skip_out)
     hd=gq_ref.shape[3]//3; kh=gq_ref.shape[2]
@@ -969,15 +1005,15 @@
     put(s3,qkv_out)
     for copy in copies: copy.wait()
 
-def assemble(lay,gin,gsk,skip,gq,um,uo,dm,do,om,oo):
+def assemble(lay,gin,gsk,skip,gq,em,eo):
     S=lambda *s: jax.ShapeDtypeStruct(s,F32)
     tokens,d=gin.shape
-    shapes=(S(tokens,d),S(tokens,d),S(*skip.shape),S(d//4,3*d),S(2,*um.shape),S(2,*dm.shape),S(2,*om.shape))
-    return pl.pallas_call(assemble_kernel,out_shape=(shapes[0],)+shapes,in_specs=[VM]*11,out_specs=(ANY,)*8,
+    shapes=(S(tokens,d),S(tokens,d),S(*skip.shape),S(d//4,3*d),S(2,d//8,4*d),S(2,d//2,d),S(2,d//8,d))
+    return pl.pallas_call(assemble_kernel,out_shape=(shapes[0],)+shapes,in_specs=[VM]*7,out_specs=(ANY,)*8,
         scratch_shapes=[pltpu.VMEM(s.shape,F32) for s in shapes+shapes[:1]]+[pltpu.SemaphoreType.DMA((8,))],
         compiler_params=pltpu.CompilerParams(vmem_limit_bytes=60*2**20),
         cost_estimate=pl.CostEstimate(flops=0,bytes_accessed=40*2**20,transcendentals=0))(
-        lay,gin,gsk,skip,gq,um,uo,dm,do,om,oo)
+        lay,gin,gsk,skip,gq,em,eo)
 
 from jax.sharding import Mesh, PartitionSpec as P
 WIDE=("y","x"); ROWS=("z","core")
@@ -1068,13 +1104,10 @@
         out_sum=gow[0].astype(F32)+pair[rows:]+from_d.astype(F32)
         early=up_sum.astype(BF),down_sum.astype(BF),out_sum.astype(BF)
     grad_qkv,early=lax.optimization_barrier((grad_qkv,early))
-    early=lax.psum(early,"z")
+    if not near: early=lax.psum(early,"z")
     if near:
-        gin,gsk,smalls,gqkv,gskip=last(grad_qkv,w_heads,normed_all,hidden,gmid,gain1,block_input[0],long_skip[0],w_skip,small)
-        gskip,early=lax.optimization_barrier((gskip,early))
-        others=swap_cores(early)
-        lay,gin,gsk,skip_share,qkv_share,up_share,down_share,out_share=assemble(lay,gin,gsk,gskip.reshape(-1,d),gqkv,
-            early[0],others[0],early[1],others[1],early[2],others[2])
+        gin,gsk,smalls,gqkv,gskip,mine,other=last(grad_qkv,w_heads,normed_all,hidden,gmid,gain1,block_input[0],long_skip[0],w_skip,small,*early)
+        lay,gin,gsk,skip_share,qkv_share,up_share,down_share,out_share=assemble(lay,gin,gsk,gskip.reshape(-1,d),gqkv,mine,other)
         up_share,down_share,out_share=up_share.reshape(-1,ff),down_share.reshape(-1,d),out_share.reshape(-1,d)
         smalls=lax.dynamic_slice_in_dim(smalls[:4],(2*lax.axis_index("y")+lax.axis_index("x"))*(d//nw),d//nw,axis=1).T
     else:

time: 723 us -> 645 us (0.89)
  Pallas kernels: 662 us -> 602 us
  between operations: 14.6 us -> 1.22 us
    pallas_call x1, Pallas kernels: 213 us -> 153 us  [last(): pl.pallas_call(last_kernel, out_shape=(S((tokens, d), BF), S((tokens, d),...]
  transfers between devices with their start and end apart: 13 -> 9, of which waited for: 1 -> 0; matrix products, arithmetic and copies ran while one was open for 1% -> 0% of each run, Pallas kernels for 46% -> 19%
where the time goes in v6:
time: 645 us; the launch traced here: 634 us
  Pallas kernels  602 us (93%)
  local copies, waits for them, and re-layouts  12.4 us (2%)
  starting transfers between devices  10 us (2%)
  other arithmetic  8.22 us (1%)
    pallas_call x1, Pallas kernels, middle(): pl.pallas_call(middle_kernel, out_shape=(S((tokens, d), BF), S((tokens, d...  205 us
    pallas_call x1, Pallas kernels, last(): pl.pallas_call(last_kernel, out_shape=(S((tokens, d), BF), S((tokens, d),...  153 us
    pallas_call x1, Pallas kernels, first(): pl.pallas_call(first_kernel, out_shape=(S((tokens, d), F32), S((4 * token...  109 us
    pallas_call x1, Pallas kernels, attend_back(): pl.pallas_call(functools.partial(attend_back_kernel, heads), out_shape=ja...  75.2 us
    pallas_call x1, Pallas kernels, attend(): pl.pallas_call(functools.partial(attend_kernel, heads), out_shape=(jax.Sh...  43.7 us
    pallas_call x1, Pallas kernels, assemble(): pl.pallas_call(assemble_kernel, out_shape=(shapes[0],) + shapes, in_specs...  15.7 us
  transfers between devices with their start and end apart: 9, of which 0 were waited for; matrix products, arithmetic and copies ran while one was open for 0% of the time, Pallas kernels for 19%

profile of v6, /device:TPU:0, one launch (start us, length us, event | category | flops | bytes accessed | tf_op | source)
XLA Modules:
  0.0 634.3 jit_solution(16262274832906447642)
XLA Ops:
  0.6 0.7 stack.19
  1.3 0.7 stack.20
  2.0 0.7 stack.21
  2.7 0.7 stack.22
  3.4 0.6 convert_element_type.45.vec_ref
  4.0 1.0 constant_dynamic-slice_fusion
  5.0 1.4 constant_dynamic-slice_fusion.1
  6.4 109.0 %shard_map.220 = (f32[832,1152]{1,0:T(8,128)}, bf16[3328,1152]{1,0:T(8,128)(2,1)}, bf16[3328,864]{1,0:T(8,128)(2,1)}, bf16[1152,864]{1,0:T(8,128)(2,1)}, bf16[23...) custom-call(bf16[832,1152]{1,0:T(8,128)(2,1)} %bitcast.37, bf16[832,1152]{1,0:T(8,128)(2,1)} %bitcast.39, ...), custom_call_target="tpu_custom_call" | custom-call | flops 11041505280 | bytes 41943040 | tf_op jit(solution)/shard_map/pallas_call | solution.py:412
  115.4 1.1 collective-permute-start.3
  116.6 0.6 collective-permute-start.2
  117.2 0.9 collective-permute-start.1
  118.1 1.5 collective-permute-start
  119.6 43.7 %shard_map.221 = (bf16[3328,288]{1,0:T(8,128)(2,1)}, f32[12,12,384]{2,1,0:T(8,128)}) custom-call(s32[1,12]{1,0:T(1,128)} %len_ref.3, bf16[3328,864]{1,0:T(8,128)(2,1)} %get-tuple-element.61.qkv_ref), custom_call_target="tpu_custom_call" | custom-call | flops 12759072768 | bytes 12582912 | tf_op jit(solution)/shard_map/pallas_call | solution.py:131
  163.3 1.0 slice_reduce_fusion
  164.2 0.7 slice.54.gain_ref
  164.9 0.7 slice.48.shift_ref
  165.6 0.7 slice.46.gain_ref
  166.3 0.0 collective-permute-done.1.outy_ref
  166.3 0.0 copy-start.2
  166.3 0.0 collective-permute-done.outx_ref
  166.3 0.0 collective-permute-done.3.upy_ref
  166.3 0.0 copy-start.1
  166.3 0.0 collective-permute-done.2.upx_ref
  166.3 1.1 copy-done.1
  167.4 0.1 copy-done.2
  167.5 205.3 %shard_map.222 = (bf16[832,1152]{1,0:T(8,128)(2,1)}, f32[832,1152]{1,0:T(8,128)}, bf16[4,832,288]{2,1,0:T(8,128)(2,1)}, bf16[2,144,1152]{2,1,0:T(8,128)(2,1)}, f...) custom-call(f32[832,1152]{1,0:T(8,128)} %get-tuple-element.59.hidden, ...), custom_call_target="tpu_custom_call" | custom-call | flops 59624128512 | bytes 62914560 | tf_op jit(solution)/shard_map/pallas_call | solution.py:955
  372.8 1.0 slice_bitcast_fusion
  373.8 1.9 collective-permute-start.8
  375.7 0.5 collective-permute-start.4
  376.2 1.2 collective-permute-start.6
  377.4 1.4 collective-permute-start.5
  378.8 1.0 collective-permute-start.7
  379.7 75.2 %shard_map.223.gq_ref = bf16[3328,864]{1,0:T(8,128)(2,1)} custom-call(s32[1,12]{1,0:T(1,128)} %len_ref.3, bf16[3328,864]{1,0:T(8,128)(2,1)} %get-tuple-element.61.qkv_ref, bf16[3328,288]{1,0:T(8,128)(2,1)} %bitcast.42, f32[12,12,384]{2,1,0:T(8,128)} %get-tuple-element.68.lse_ref), custom_call_target="tpu_custom_call" | custom-call | flops 31897681920 | bytes 20971520 | tf_op jit(solution)/shard_map/pallas_call | solution.py:139
  454.9 0.0 copy-start
  454.9 0.0 collective-permute-done.8
  454.9 0.0 collective-permute-done.4
  454.9 0.0 collective-permute-done.6
  454.9 0.0 collective-permute-done.5
  454.9 0.0 collective-permute-done.7
  454.9 0.4 convert_add_fusion
  455.4 0.6 copy-done
  456.0 0.8 fusion.4.eo_ref
  456.8 2.7 fusion.ed_ref
  459.5 3.7 fusion.2.eu_ref
  463.2 153.5 %shard_map.224 = (bf16[832,1152]{1,0:T(8,128)(2,1)}, bf16[832,1152]{1,0:T(8,128)(2,1)}, f32[8,1152]{1,0:T(8,128)}, bf16[4,2,144,864]{3,2,1,0:T(8,128)(2,1)}, bf1...) custom-call(bf16[3328,864]{1,0:T(8,128)(2,1)} %shard_map.223.gq_ref, ...), custom_call_target="tpu_custom_call" | custom-call | flops 22083010560 | bytes 62914560 | tf_op jit(solution)/shard_map/pallas_call | solution.py:659
  616.6 0.8 slice.55
  617.4 0.1 dynamic-slice_bitcast_fusion
  617.5 0.6 slice_reduce_fusion.3
  618.1 15.7 %shard_map.225 = (f32[832,1152]{1,0:T(8,128)}, f32[832,1152]{1,0:T(8,128)}, f32[832,1152]{1,0:T(8,128)}, f32[576,1152]{1,0:T(8,128)}, f32[288,3456]{1,0:T(8,128)...) custom-call(bf16[832,1152]{1,0:T(8,128)(2,1)} %get-tuple-element.66.lay_ref, ...), custom_call_target="tpu_custom_call" | custom-call | bytes 41943040 | tf_op jit(solution)/shard_map/pallas_call | solution.py:1012
  (1 shorter events, 0.0 us)
Async XLA Ops:
  115.4 50.9 %collective-permute-start.3 = (bf16[144,4608]{1,0:T(8,128)(2,1)S(1)}, bf16[144,4608]{1,0:T(8,128)(2,1)S(1)}, u32[]{:S(2)}, u32[]{:S(2)}) collective-permute-start(bf16[144,4608]{1,0:T(8,128)(2,1)S(1)} %constant_dynamic-slice_fusion.1), channel_id=1, source_target_pairs={{0,2},{2,0},{1,3},{3,1},{4,6},{6,4},{5,7},{7,5},{8,10},{10,8},{9,1... | collective-permute-start | bytes 3981320 | tf_op jit(solution)/shard_map/ppermute | solution.py:1055
  116.6 49.7 %collective-permute-start.2 = (bf16[144,4608]{1,0:T(8,128)(2,1)S(1)}, bf16[144,4608]{1,0:T(8,128)(2,1)}, u32[]{:S(2)}, u32[]{:S(2)}) collective-permute-start(bf16[144,4608]{1,0:T(8,128)(2,1)S(1)} %constant_dynamic-slice_fusion.1), channel_id=1, source_target_pairs={{0,1},{1,0},{2,3},{3,2},{4,5},{5,4},{6,7},{7,6},{8,9},{9,8},{10,11... | collective-permute-start | bytes 3981320 | tf_op jit(solution)/shard_map/ppermute | solution.py:1054
  117.2 49.1 %collective-permute-start.1 = (bf16[144,1152]{1,0:T(8,128)(2,1)S(1)}, bf16[144,1152]{1,0:T(8,128)(2,1)S(1)}, u32[]{:S(2)}, u32[]{:S(2)}) collective-permute-start(bf16[144,1152]{1,0:T(8,128)(2,1)S(1)} %constant_dynamic-slice_fusion), channel_id=1, source_target_pairs={{0,2},{2,0},{1,3},{3,1},{4,6},{6,4},{5,7},{7,5},{8,10},{10,8},{9,1... | collective-permute-start | bytes 995336 | tf_op jit(solution)/shard_map/ppermute | solution.py:1055
  118.1 48.2 %collective-permute-start = (bf16[144,1152]{1,0:T(8,128)(2,1)S(1)}, bf16[144,1152]{1,0:T(8,128)(2,1)}, u32[]{:S(2)}, u32[]{:S(2)}) collective-permute-start(bf16[144,1152]{1,0:T(8,128)(2,1)S(1)} %constant_dynamic-slice_fusion), channel_id=1, source_target_pairs={{0,1},{1,0},{2,3},{3,2},{4,5},{5,4},{6,7},{7,6},{8,9},{9,8},{10,11... | collective-permute-start | bytes 995336 | tf_op jit(solution)/shard_map/ppermute | solution.py:1054
  166.3 1.2 copy-start.2
  166.3 1.1 copy-start.1
  373.8 81.1 %collective-permute-start.8 = (bf16[144,1152]{1,0:T(8,128)(2,1)S(1)}, bf16[144,1152]{1,0:T(8,128)(2,1)S(1)}, u32[]{:S(2)}, u32[]{:S(2)}) collective-permute-start(bf16[144,1152]{1,0:T(8,128)(2,1)S(1)} %slice_bitcast_fusion), channel_id=1, source_target_pairs={{0,3},{1,2},{2,1},{3,0},{4,7},{5,6},{6,5},{7,4},{8,11},{9,10},{10,... | collective-permute-start | bytes 995336 | tf_op jit(solution)/shard_map/ppermute | solution.py:1094
  375.7 79.2 %collective-permute-start.4 = (bf16[144,4608]{1,0:T(8,128)(2,1)}, bf16[144,4608]{1,0:T(8,128)(2,1)}, u32[]{:S(2)}, u32[]{:S(2)}) collective-permute-start(bf16[144,4608]{1,0:T(8,128)(2,1)} %get-tuple-element.69), channel_id=1, source_target_pairs={{0,1},{1,0},{2,3},{3,2},{4,5},{5,4},{6,7},{7,6},{8,9},{9,8},{10,11... | collective-permute-start | bytes 3981320 | tf_op jit(solution)/shard_map/ppermute | solution.py:1092
  376.2 78.7 %collective-permute-start.6 = (bf16[144,4608]{1,0:T(8,128)(2,1)}, bf16[144,4608]{1,0:T(8,128)(2,1)}, u32[]{:S(2)}, u32[]{:S(2)}) collective-permute-start(bf16[144,4608]{1,0:T(8,128)(2,1)} %get-tuple-element.71), channel_id=1, source_target_pairs={{0,2},{2,0},{1,3},{3,1},{4,6},{6,4},{5,7},{7,5},{8,10},{10,8},{9,1... | collective-permute-start | bytes 3981320 | tf_op jit(solution)/shard_map/ppermute | solution.py:1093
  377.4 77.5 %collective-permute-start.5 = (bf16[720,1152]{1,0:T(8,128)(2,1)}, bf16[720,1152]{1,0:T(8,128)(2,1)S(1)}, u32[]{:S(2)}, u32[]{:S(2)}) collective-permute-start(bf16[720,1152]{1,0:T(8,128)(2,1)} %get-tuple-element.70), channel_id=1, source_target_pairs={{0,1},{1,0},{2,3},{3,2},{4,5},{5,4},{6,7},{7,6},{8,9},{9,8},{10,11... | collective-permute-start | bytes 4976648 | tf_op jit(solution)/shard_map/ppermute | solution.py:1092
  378.8 76.1 %collective-permute-start.7 = (bf16[720,1152]{1,0:T(8,128)(2,1)}, bf16[720,1152]{1,0:T(8,128)(2,1)S(1)}, u32[]{:S(2)}, u32[]{:S(2)}) collective-permute-start(bf16[720,1152]{1,0:T(8,128)(2,1)} %get-tuple-element.72), channel_id=1, source_target_pairs={{0,2},{2,0},{1,3},{3,1},{4,6},{6,4},{5,7},{7,5},{8,10},{10,8},{9,1... | collective-permute-start | bytes 4976648 | tf_op jit(solution)/shard_map/ppermute | solution.py:1093
  454.9 1.1 copy-start

commit v7 on v6

--- a/solution.py
+++ b/solution.py
@@ -44,6 +44,29 @@
         for j in range(ref.shape[0]):
             ref[j,r,:]=jnp.zeros((chunk,ref.shape[2]),ref.dtype)
 
+LANES=256
+def pack_heads(src_ref, dst_ref, tail_ref, count):
+    size=tail_ref.shape[0]//4
+    @pl.loop(0,4)
+    def _(b):
+        tails=[]
+        for j in range(4):
+            r=pl.ds(pl.multiple_of((4*b+j)*size,16),size)
+            row=jnp.concatenate([src_ref[h,r,:] for h in range(count)],axis=1)
+            dst_ref[r,:]=row[:,:LANES]
+            tails.append(row[:,LANES:])
+        tail_ref[pl.ds(pl.multiple_of(b*size,16),size),:]=jnp.concatenate(tails,axis=1)
+
+def unpack_heads(src_ref, tail_ref, dst_ref, count):
+    size=tail_ref.shape[0]//4; width=tail_ref.shape[1]//4
+    @pl.loop(0,4)
+    def _(b):
+        tail=tail_ref[pl.ds(pl.multiple_of(b*size,16),size),:]
+        for j in range(4):
+            r=pl.ds(pl.multiple_of((4*b+j)*size,16),size)
+            row=jnp.concatenate([src_ref[r,:],tail[:,j*width:(j+1)*width]],axis=1)
+            for h in range(count): dst_ref[h,r,:]=row[:,h*HEAD:(h+1)*HEAD]
+
 def for_items(len_ref, one):
     def step(i, start):
         size=len_ref[0,i]
@@ -62,7 +85,8 @@
     high=jnp.where(top+body<off+size,values[body:],fill)
     return jnp.concatenate([low,values[32:body],high],axis=0)
 
-def attend_kernel(heads, len_ref, qkv_ref, out_ref, lse_ref, split_ref, acc_ref):
+def attend_kernel(heads, len_ref, qkv_ref, *refs):
+    *outs, lse_ref, split_ref, acc_ref=refs
     row_len=qkv_ref.shape[0]
     split_heads(qkv_ref, split_ref, 3*heads)
     zero(acc_ref)
@@ -86,12 +110,15 @@
                 acc_ref[h,qr,:]+=o.T.astype(jnp.bfloat16)
                 lse_ref[item,pl.ds(t*heads+h,1),:]=m*(SCALE*LOG2E)+jnp.log2(l)
     for_items(len_ref,one)
-    join_heads(acc_ref,out_ref,heads)
-
-def attend_back_kernel(heads, len_ref, qkv_ref, grad_ref, lse_ref, out_ref, split_ref, gsplit_ref, acc_ref, dk_ref, dv_ref):
+    if len(outs)==2: pack_heads(acc_ref,*outs,heads)
+    else: join_heads(acc_ref,outs[0],heads)
+
+def attend_back_kernel(heads, len_ref, qkv_ref, *refs):
+    *grads, lse_ref, out_ref, split_ref, gsplit_ref, acc_ref, dk_ref, dv_ref=refs
     row_len=qkv_ref.shape[0]
     split_heads(qkv_ref, split_ref, 3*heads)
-    split_heads(grad_ref, gsplit_ref, heads)
+    if len(grads)==2: unpack_heads(*grads,gsplit_ref,heads)
+    else: split_heads(grads[0],gsplit_ref,heads)
     zero(acc_ref)
     def one(item,start,size):
         k0,q0=windows(start,size,row_len)
@@ -125,24 +152,25 @@
     join_heads(acc_ref,out_ref,3*heads)
 
 VM=pl.BlockSpec(memory_space=pltpu.VMEM); SM=pl.BlockSpec(memory_space=pltpu.SMEM)
-def attend(lens,qkv,heads):
+def attend(lens,qkv,heads,packed=False):
     n=qkv.shape[0]
     nt_=heads*(qwin(LONG)//QT)
+    shapes=((n,LANES),(n//4,4*(heads*HEAD-LANES))) if packed else ((n,heads*HEAD),)
     return pl.pallas_call(functools.partial(attend_kernel,heads),
-      out_shape=(jax.ShapeDtypeStruct((n,heads*HEAD),jnp.bfloat16),jax.ShapeDtypeStruct((NITEM,nt_,QT),jnp.float32)),
-      in_specs=[SM,VM],out_specs=(VM,VM),
+      out_shape=tuple(jax.ShapeDtypeStruct(s,jnp.bfloat16) for s in shapes)+(jax.ShapeDtypeStruct((NITEM,nt_,QT),jnp.float32),),
+      in_specs=[SM,VM],out_specs=(VM,)*(len(shapes)+1),
       scratch_shapes=[pltpu.VMEM((3*heads,n,HEAD),jnp.bfloat16),pltpu.VMEM((heads,n,HEAD),jnp.bfloat16)],
       compiler_params=pltpu.CompilerParams(vmem_limit_bytes=56*2**20),
       cost_estimate=pl.CostEstimate(flops=heads*n*n*HEAD*4,bytes_accessed=12*2**20,transcendentals=heads*n*n//3))(lens,qkv)
-def attend_back(lens,qkv,grad,lse,heads):
+def attend_back(lens,qkv,grads,lse,heads):
     n=qkv.shape[0]
     return pl.pallas_call(functools.partial(attend_back_kernel,heads),
       out_shape=jax.ShapeDtypeStruct((n,3*heads*HEAD),jnp.bfloat16),
-      in_specs=[SM,VM,VM,VM],out_specs=VM,
+      in_specs=[SM,VM]+[VM]*len(grads)+[VM],out_specs=VM,
       scratch_shapes=[pltpu.VMEM((3*heads,n,HEAD),jnp.bfloat16),pltpu.VMEM((heads,n,HEAD),jnp.bfloat16),pltpu.VMEM((3*heads,n,HEAD),jnp.bfloat16),
         pltpu.VMEM((heads,kwin(LONG),HEAD),jnp.float32),pltpu.VMEM((heads,kwin(LONG),HEAD),jnp.float32)],
       compiler_params=pltpu.CompilerParams(vmem_limit_bytes=60*2**20),
-      cost_estimate=pl.CostEstimate(flops=heads*n*n*HEAD*10,bytes_accessed=20*2**20,transcendentals=heads*n*n//3))(lens,qkv,grad,lse)
+      cost_estimate=pl.CostEstimate(flops=heads*n*n*HEAD*10,bytes_accessed=20*2**20,transcendentals=heads*n*n//3))(lens,qkv,*grads,lse)
 
 
 F32=jnp.float32; BF=jnp.bfloat16
@@ -670,13 +698,13 @@
         gq,heads,normed,hidden,gmid,gain,block,long,wskip,small,eu,ed,eo)
 
 SPLIT=((0,640),(640,512))
-def middle_kernel(hidden_ref,att_ref,g_ref,gain_ref,shift_ref,outw_ref,outx_ref,outy_ref,upw_ref,upx_ref,upy_ref,dnw_ref,
-                  lay_out,gmid_ref,gh_out,gow_out,small_ref,gup_out,gdn_out,sxu_out,sxd_out,syu_out,syd_out,uland,dland,ux_out,uy_out,dx_out,dy_out,
-                  att_in,att_s,outw_s,n2_s,xhat_s,rstd_s,lay_s,act_s,gu_s,upb,dnb,gub,gdb,land_u,land_d,low_s,
+def middle_kernel(hidden_ref,att_ref,tail_ref,g_ref,gain_ref,shift_ref,outw_ref,outx_ref,outy_ref,upw_ref,upx_ref,upy_ref,dnw_ref,
+                  lay_out,gmid_ref,gh_out,ght_out,gow_out,small_ref,gup_out,gdn_out,sxu_out,sxd_out,syu_out,syd_out,uland,dland,ux_out,uy_out,dx_out,dy_out,
+                  att_in,tail_in,att_s,outw_s,n2_s,xhat_s,rstd_s,lay_s,act_s,gu_s,upb,dnb,gub,gdb,land_u,land_d,low_s,
                   send,recv,csend,crecv,fetch_sem,flush_sem,local,usem,urecv,bring_sem):
     x,y,c,w,wx,wy,wd=place()
     tokens,d=hidden_ref.shape
-    cols=att_ref.shape[1]
+    wide_cols=att_ref.shape[1]; quarter=tail_ref.shape[1]//4; cols=wide_cols+quarter
     kr=d//4; kh=kr//2; dh=d//2; dq=dh//2
     tc=tokens//4; th=tokens//2
     mul=pl.multiple_of
@@ -690,13 +718,15 @@
     def urow(b,core): return pl.ds(mul(b*kr+core*kh,16),kh)
     def drow(b,core,p): return pl.ds(mul(b*d+core*dh+p*dq,16),dq)
     def trow(b): return pl.ds(mul(b*tokens,16),tokens)
+    def tails(b): return pl.ds(mul(b*tc,16),tc)
     uview=uland.at[pl.ds(0,kh),pl.ds(0,d)]
     dview=dland.at[pl.ds(0,dq)]
     net.meet("XYDC")
     for j,(t,b) in enumerate((("X",wx),("Y",wy),("D",wd))):
         start(j,t,att_ref.at[trow(b)],att_in.at[w],att_in.at[0])
-    own_att=pltpu.make_async_copy(att_ref.at[trow(w)],att_in.at[w],local.at[0])
-    own_att.start()
+        start(52+j,t,tail_ref.at[tails(b)],tail_in.at[w],tail_in.at[0])
+    own_att=[pltpu.make_async_copy(att_ref.at[trow(w)],att_in.at[w],local.at[0]),pltpu.make_async_copy(tail_ref.at[tails(w)],tail_in.at[w],local.at[3])]
+    for copy in own_att: copy.start()
     cut=kh//32*16+16
     def orow(b,core,lo,n): return pl.ds(mul(b*kr+core*kh+lo,16),n)
     start(3,"Y",outx_ref.at[pl.ds(0,cut)],outw_s.at[orow(wx,c,0,cut)],outw_s.at[pl.ds(0,cut)])
@@ -747,6 +777,7 @@
 
     for j,(t,b) in enumerate((("X",wx),("Y",wy),("D",wd))):
         net.got(j,t,att_in.at[b])
+        net.got(52+j,t,tail_in.at[b])
     start(9,"Y",upx_ref.at[:,blk(wx)],uland.at[urow(wx,c),blk(wx)],uview)
     start(10,"X",upy_ref.at[:,blk(wd)],uland.at[urow(wy,c),blk(wd)],uview)
     def dmine(p): return dnw_ref.at[pl.ds(mul(c*dh+p*dq,16),dq)]
@@ -761,13 +792,12 @@
     for i in (1,2,3): up_core(i)
     net.got(5,"C",outw_s.at[urow(wx,1-c)]); net.got(6,"C",outw_s.at[urow(wy,1-c)])
     net.got(35,"C",outw_s.at[urow(wd,1-c)])
-    own_att.wait()
+    for copy in own_att: copy.wait()
     fetch(0)
     gain=gain_ref[...]; shift=shift_ref[...]
-    @pl.loop(0,4)
-    def _(i):
-        r=pl.ds(mul(i*tc,16),tc)
-        joined=jnp.concatenate([att_in[p,r,:] for p in range(4)],axis=1)
+    for i in range(4):
+        r=pl.ds(i*tc,tc)
+        joined=jnp.concatenate([v for p in range(4) for v in (att_in[p,r,:],tail_in[p,:,i*quarter:(i+1)*quarter])],axis=1)
         att_s[r,:]=joined
         mid=hidden_ref[r,:]+nn(joined,outw_s[...])
         lay_s[r,:]=mid
@@ -888,11 +918,15 @@
         low=gm.astype(BF)
         low_s[r,:]=low
         ga=nt(low,outw_s[...]).astype(BF)
-        for p in range(4): att_in[p,r,:]=ga[:,p*cols:(p+1)*cols]
+        for p in range(4):
+            att_in[p,r,:]=ga[:,p*cols:p*cols+wide_cols]
+            tail_in[p,:,i*quarter:(i+1)*quarter]=ga[:,p*cols+wide_cols:(p+1)*cols]
         for j,(t,b) in enumerate((("X",wx),("Y",wy),("D",wd))):
             start(36+3*i+j,t,att_in.at[b,r],gh_out.at[w,r],gh_out.at[0,pl.ds(0,tc)])
-    own_grad=pltpu.make_async_copy(att_in.at[w],gh_out.at[w],local.at[2])
-    own_grad.start()
+    for j,(t,b) in enumerate((("X",wx),("Y",wy),("D",wd))):
+        start(55+j,t,tail_in.at[b],ght_out.at[w],tail_in.at[0])
+    own_grad=[pltpu.make_async_copy(att_in.at[w],gh_out.at[w],local.at[2]),pltpu.make_async_copy(tail_in.at[w],ght_out.at[w],local.at[0])]
+    for copy in own_grad: copy.start()
     weight_grads()
     exchange(1,go)
     act_s[...]=lay_s[...].astype(BF)
@@ -943,27 +977,28 @@
     for i in range(4):
         for j,(t,b) in enumerate((("X",wx),("Y",wy),("D",wd))):
             net.got(36+3*i+j,t,gh_out.at[b,pl.ds(i*tc,tc)])
-    for copy in [lay_copy,own_grad]+copies: copy.wait()
+    for j,(t,b) in enumerate((('X',wx),('Y',wy),('D',wd))): net.got(55+j,t,ght_out.at[b])
+    for copy in [lay_copy]+own_grad+copies: copy.wait()
     for k,t,view in left:
         pltpu.make_async_remote_copy(src_ref=view,dst_ref=view,send_sem=send.at[k],recv_sem=recv.at[k],
                                      device_id=net.to[t],device_id_type=MESH).wait_send()
 
-def middle(hidden,att,g,gain,shift,outw,outx,outy,upw,upx,upy,dnw):
+def middle(hidden,att,tail,g,gain,shift,outw,outx,outy,upw,upx,upy,dnw):
     tokens,d=hidden.shape; cols=att.shape[1]; ff=upw.shape[1]
     S=jax.ShapeDtypeStruct; V=pltpu.VMEM; D=pltpu.SemaphoreType.DMA
     kh=d//8; cut=kh//32*16+16
     return pl.pallas_call(middle_kernel,
-        out_shape=(S((tokens,d),BF),S((tokens,d),F32),S((4,tokens,cols),BF),S((2,kh,d),BF),S((8,d),F32),S((d//2,ff),BF),S((ff//2,d),BF),
+        out_shape=(S((tokens,d),BF),S((tokens,d),F32),S((4,tokens,cols),BF),S((4,tokens//4,tail.shape[1]),BF),S((2,kh,d),BF),S((8,d),F32),S((d//2,ff),BF),S((ff//2,d),BF),
                    S((kh,ff),BF),S((ff//8+kh,d),BF),S((kh,ff),BF),S((ff//8+kh,d),BF),
                    S((d,ff),BF),S((ff,d),BF),S((cut,ff),BF),S((kh-cut,ff),BF),S((ff//16,d),BF),S((ff//16,d),BF)),
-        in_specs=[VM,ANY]+[VM]*6+[ANY]*4,out_specs=(ANY,VM,ANY,ANY,VM)+(ANY,)*12,
-        scratch_shapes=[V((4,tokens,cols),BF),V((tokens,d),BF),V((d,d),BF),V((tokens,d),BF),V((tokens,d),F32),V((tokens,128),F32),
+        in_specs=[VM,ANY,ANY]+[VM]*6+[ANY]*4,out_specs=(ANY,VM,ANY,ANY,ANY,VM)+(ANY,)*12,
+        scratch_shapes=[V((4,tokens,cols),BF),V((4,tokens//4,tail.shape[1]),BF),V((tokens,d),BF),V((d,d),BF),V((tokens,d),BF),V((tokens,d),F32),V((tokens,128),F32),
             V((tokens,d),F32),V((tokens,d),BF),V((tokens,d),BF),V((2,d,d),BF),V((2,d,d),BF),V((d,d),BF),V((d,d),BF),
-            V((2,d//2,d),BF),V((2,d//2,d),BF),V((tokens,d),BF),D((52,)),D((52,)),D((2,5)),D((2,5)),D((2,7)),D((5,)),D((4,)),
+            V((2,d//2,d),BF),V((2,d//2,d),BF),V((tokens,d),BF),D((58,)),D((58,)),D((2,5)),D((2,5)),D((2,7)),D((5,)),D((4,)),
             D((5,2)),D((5,2)),D((20,))],
         compiler_params=pltpu.CompilerParams(vmem_limit_bytes=63*2**20,collective_id=2,has_side_effects=True),
         cost_estimate=pl.CostEstimate(flops=2*tokens*d*(ff*6+d*3),bytes_accessed=60*2**20,transcendentals=tokens*ff*2))(
-        hidden,att,g,gain,shift,outw,outx,outy,upw,upx,upy,dnw)
+        hidden,att,tail,g,gain,shift,outw,outx,outy,upw,upx,upy,dnw)
 
 def assemble_kernel(lay_ref,gin_ref,gsk_ref,skip_ref,gq_ref,em_ref,eo_ref,
                     lay_out,gin_out,gsk_out,skip_out,qkv_out,up_out,down_out,out_out,
@@ -1064,19 +1099,19 @@
         xhat1,inv1=norm(hidden)
         normed_all=gather((xhat1*gain1+shift1).astype(BF))
         qkv=dot(normed_all,w_heads).astype(BF)
-    att,lse=attend(item_lengths,qkv,heads)
+    *att,lse=attend(item_lengths,qkv,heads,near)
     if near:
-        lay,gmid,gatt,gow,small,gup,gdn,sxu,sxd,syu,syd=middle(hidden,att,output_grad[0],gain2,shift2,out_weight,out_x,out_y,
-            up_weight,up_x,up_y,down_weight)[:11]
+        lay,gmid,gatt,gtail,gow,small,gup,gdn,sxu,sxd,syu,syd=middle(hidden,*att,output_grad[0],gain2,shift2,out_weight,out_x,out_y,
+            up_weight,up_x,up_y,down_weight)[:12]
+        grad_heads=gatt.reshape(nw*tokens,-1),gtail.reshape(tokens,-1)
     else:
         w_out=gather(out_weight)
         up_mine=gather(pick(up_weight.reshape(d//nw,nw,2,fb),core,2).reshape(d//nw,nw*fb))
         down_mine=gather(pick(down_weight.reshape(2,fb,d),core,0))
         up_other,down_other=swap_cores(up_mine),swap_cores(down_mine)
-        att=lax.all_to_all(att.reshape(nw,tokens,hd),WIDE,0,0)
+        att=lax.all_to_all(att[0].reshape(nw,tokens,hd),WIDE,0,0)
         lay,gmid,gatt,gow,small,gupo,guph,gdno,gdnh=mlp(hidden,att,w_out,gain2,shift2,output_grad[0],up_mine,up_other,down_mine,down_other)
-        gatt=lax.all_to_all(gatt,WIDE,0,0)
-    grad_heads=gatt.reshape(nw*tokens,hd)
+        grad_heads=(lax.all_to_all(gatt,WIDE,0,0).reshape(nw*tokens,hd),)
 
     def scatter(mine,other):
         both=(mine.astype(F32)+swap_cores(other).astype(F32)).astype(BF)

time: 645 us -> 629 us (0.975)
  Pallas kernels: 602 us -> 591 us
    pallas_call x1, Pallas kernels: 205 us -> 192 us  [middle(): pl.pallas_call(middle_kernel, out_shape=(S((tokens, d), BF), S((tokens, d...]
where the time goes in v7:
time: 629 us; the launch traced here: 623 us
  Pallas kernels  591 us (94%)
  local copies, waits for them, and re-layouts  12.4 us (2%)
  starting transfers between devices  10 us (2%)
  other arithmetic  8.22 us (1%)
    pallas_call x1, Pallas kernels, middle(): pl.pallas_call(middle_kernel, out_shape=(S((tokens, d), BF), S((tokens, d...  192 us
    pallas_call x1, Pallas kernels, last(): pl.pallas_call(last_kernel, out_shape=(S((tokens, d), BF), S((tokens, d),...  156 us
    pallas_call x1, Pallas kernels, first(): pl.pallas_call(first_kernel, out_shape=(S((tokens, d), F32), S((4 * token...  109 us
    pallas_call x1, Pallas kernels, attend_back(): pl.pallas_call(functools.partial(attend_back_kernel, heads), out_shape=ja...  74.5 us
    pallas_call x1, Pallas kernels, attend(): pl.pallas_call(functools.partial(attend_kernel, heads), out_shape=tuple((...  43.5 us
    pallas_call x1, Pallas kernels, assemble(): pl.pallas_call(assemble_kernel, out_shape=(shapes[0],) + shapes, in_specs...  15.7 us
  transfers between devices with their start and end apart: 9, of which 0 were waited for; matrix products, arithmetic and copies ran while one was open for 0% of the time, Pallas kernels for 19%

profile of v7, /device:TPU:0, one launch (start us, length us, event | category | flops | bytes accessed | tf_op | source)
XLA Modules:
  0.0 622.6 jit_solution(11755602471815245826)
XLA Ops:
  0.6 0.7 stack.19
  1.3 0.7 stack.20
  2.0 0.7 stack.21
  2.7 0.7 stack.22
  3.4 0.6 convert_element_type.45.vec_ref
  4.0 1.0 constant_dynamic-slice_fusion
  5.0 1.4 constant_dynamic-slice_fusion.1
  6.4 109.0 %shard_map.220 = (f32[832,1152]{1,0:T(8,128)}, bf16[3328,1152]{1,0:T(8,128)(2,1)}, bf16[3328,864]{1,0:T(8,128)(2,1)}, bf16[1152,864]{1,0:T(8,128)(2,1)}, bf16[23...) custom-call(bf16[832,1152]{1,0:T(8,128)(2,1)} %bitcast.38, bf16[832,1152]{1,0:T(8,128)(2,1)} %bitcast.40, ...), custom_call_target="tpu_custom_call" | custom-call | flops 11041505280 | bytes 41943040 | tf_op jit(solution)/shard_map/pallas_call | solution.py:440
  115.4 1.1 collective-permute-start.3
  116.6 0.6 collective-permute-start.2
  117.2 0.9 collective-permute-start.1
  118.1 1.5 collective-permute-start
  119.6 43.5 %shard_map.221 = (bf16[3328,256]{1,0:T(8,128)(2,1)}, bf16[832,128]{1,0:T(8,128)(2,1)}, f32[12,12,384]{2,1,0:T(8,128)}) custom-call(s32[1,12]{1,0:T(1,128)} %len_ref.3, bf16[3328,864]{1,0:T(8,128)(2,1)} %get-tuple-element.63.qkv_ref), custom_call_target="tpu_custom_call" | custom-call | flops 12759072768 | bytes 12582912 | tf_op jit(solution)/shard_map/pallas_call | solution.py:159
  163.0 1.0 slice_reduce_fusion
  164.0 0.7 slice.54.gain_ref
  164.7 0.7 slice.48.shift_ref
  165.4 0.7 slice.46.gain_ref
  166.0 0.0 collective-permute-done.1.outy_ref
  166.0 0.0 copy-start.2
  166.0 0.0 collective-permute-done.outx_ref
  166.0 0.0 collective-permute-done.3.upy_ref
  166.1 0.0 copy-start.1
  166.1 0.0 collective-permute-done.2.upx_ref
  166.1 1.1 copy-done.1
  167.1 0.1 copy-done.2
  167.2 191.7 %shard_map.222 = (bf16[832,1152]{1,0:T(8,128)(2,1)}, f32[832,1152]{1,0:T(8,128)}, bf16[4,832,256]{2,1,0:T(8,128)(2,1)}, bf16[4,208,128]{2,1,0:T(8,128)(2,1)}, bf...) custom-call(f32[832,1152]{1,0:T(8,128)} %get-tuple-element.61.hidden, ...), custom_call_target="tpu_custom_call" | custom-call | flops 59624128512 | bytes 62914560 | tf_op jit(solution)/shard_map/pallas_call | solution.py:990
  358.9 1.0 slice_bitcast_fusion
  359.9 1.9 collective-permute-start.8
  361.8 0.5 collective-permute-start.4
  362.3 1.2 collective-permute-start.6
  363.5 1.4 collective-permute-start.5
  364.9 0.9 collective-permute-start.7
  365.9 74.5 %shard_map.223.gq_ref = bf16[3328,864]{1,0:T(8,128)(2,1)} custom-call(s32[1,12]{1,0:T(1,128)} %len_ref.3, bf16[3328,864]{1,0:T(8,128)(2,1)} %get-tuple-element.63.qkv_ref, bf16[3328,256]{1,0:T(8,128)(2,1)} %bitcast.43, bf16[832,128]{1,0:T(8,128)(2,1)} %bitcast.44, f32[12,12,384]{2,1,0:T(8,128)} %get-tuple-element.72.refs_2_), custom_call_target="tpu_custom_call" | custom-call | flops 31897681920 | bytes 20971520 | tf_op jit(solution)/shard_map/pallas_call | solution.py:167
  440.4 0.0 copy-start
  440.4 0.0 collective-permute-done.8
  440.4 0.0 collective-permute-done.4
  440.4 0.0 collective-permute-done.6
  440.4 0.0 collective-permute-done.5
  440.4 0.0 collective-permute-done.7
  440.4 0.4 convert_add_fusion
  440.9 0.6 copy-done
  441.5 0.8 fusion.4.eo_ref
  442.3 2.7 fusion.ed_ref
  445.0 3.7 fusion.2.eu_ref
  448.7 156.3 %shard_map.224 = (bf16[832,1152]{1,0:T(8,128)(2,1)}, bf16[832,1152]{1,0:T(8,128)(2,1)}, f32[8,1152]{1,0:T(8,128)}, bf16[4,2,144,864]{3,2,1,0:T(8,128)(2,1)}, bf1...) custom-call(bf16[3328,864]{1,0:T(8,128)(2,1)} %shard_map.223.gq_ref, ...), custom_call_target="tpu_custom_call" | custom-call | flops 22083010560 | bytes 62914560 | tf_op jit(solution)/shard_map/pallas_call | solution.py:687
  605.0 0.8 slice.55
  605.8 0.1 dynamic-slice_bitcast_fusion
  605.8 0.6 slice_reduce_fusion.3
  606.4 15.7 %shard_map.225 = (f32[832,1152]{1,0:T(8,128)}, f32[832,1152]{1,0:T(8,128)}, f32[832,1152]{1,0:T(8,128)}, f32[576,1152]{1,0:T(8,128)}, f32[288,3456]{1,0:T(8,128)...) custom-call(bf16[832,1152]{1,0:T(8,128)(2,1)} %get-tuple-element.69.lay_ref, ...), custom_call_target="tpu_custom_call" | custom-call | bytes 41943040 | tf_op jit(solution)/shard_map/pallas_call | solution.py:1047
  (1 shorter events, 0.0 us)
Async XLA Ops:
  115.4 50.6 %collective-permute-start.3 = (bf16[144,4608]{1,0:T(8,128)(2,1)S(1)}, bf16[144,4608]{1,0:T(8,128)(2,1)S(1)}, u32[]{:S(2)}, u32[]{:S(2)}) collective-permute-start(bf16[144,4608]{1,0:T(8,128)(2,1)S(1)} %constant_dynamic-slice_fusion.1), channel_id=1, source_target_pairs={{0,2},{2,0},{1,3},{3,1},{4,6},{6,4},{5,7},{7,5},{8,10},{10,8},{9,1... | collective-permute-start | bytes 3981320 | tf_op jit(solution)/shard_map/ppermute | solution.py:1090
  116.6 49.5 %collective-permute-start.2 = (bf16[144,4608]{1,0:T(8,128)(2,1)S(1)}, bf16[144,4608]{1,0:T(8,128)(2,1)}, u32[]{:S(2)}, u32[]{:S(2)}) collective-permute-start(bf16[144,4608]{1,0:T(8,128)(2,1)S(1)} %constant_dynamic-slice_fusion.1), channel_id=1, source_target_pairs={{0,1},{1,0},{2,3},{3,2},{4,5},{5,4},{6,7},{7,6},{8,9},{9,8},{10,11... | collective-permute-start | bytes 3981320 | tf_op jit(solution)/shard_map/ppermute | solution.py:1089
  117.2 48.8 %collective-permute-start.1 = (bf16[144,1152]{1,0:T(8,128)(2,1)S(1)}, bf16[144,1152]{1,0:T(8,128)(2,1)S(1)}, u32[]{:S(2)}, u32[]{:S(2)}) collective-permute-start(bf16[144,1152]{1,0:T(8,128)(2,1)S(1)} %constant_dynamic-slice_fusion), channel_id=1, source_target_pairs={{0,2},{2,0},{1,3},{3,1},{4,6},{6,4},{5,7},{7,5},{8,10},{10,8},{9,1... | collective-permute-start | bytes 995336 | tf_op jit(solution)/shard_map/ppermute | solution.py:1090
  118.1 47.9 %collective-permute-start = (bf16[144,1152]{1,0:T(8,128)(2,1)S(1)}, bf16[144,1152]{1,0:T(8,128)(2,1)}, u32[]{:S(2)}, u32[]{:S(2)}) collective-permute-start(bf16[144,1152]{1,0:T(8,128)(2,1)S(1)} %constant_dynamic-slice_fusion), channel_id=1, source_target_pairs={{0,1},{1,0},{2,3},{3,2},{4,5},{5,4},{6,7},{7,6},{8,9},{9,8},{10,11... | collective-permute-start | bytes 995336 | tf_op jit(solution)/shard_map/ppermute | solution.py:1089
  166.0 1.2 copy-start.2
  166.1 1.1 copy-start.1
  359.9 80.5 %collective-permute-start.8 = (bf16[144,1152]{1,0:T(8,128)(2,1)S(1)}, bf16[144,1152]{1,0:T(8,128)(2,1)S(1)}, u32[]{:S(2)}, u32[]{:S(2)}) collective-permute-start(bf16[144,1152]{1,0:T(8,128)(2,1)S(1)} %slice_bitcast_fusion), channel_id=1, source_target_pairs={{0,3},{1,2},{2,1},{3,0},{4,7},{5,6},{6,5},{7,4},{8,11},{9,10},{10,... | collective-permute-start | bytes 995336 | tf_op jit(solution)/shard_map/ppermute | solution.py:1129
  361.8 78.6 %collective-permute-start.4 = (bf16[144,4608]{1,0:T(8,128)(2,1)}, bf16[144,4608]{1,0:T(8,128)(2,1)}, u32[]{:S(2)}, u32[]{:S(2)}) collective-permute-start(bf16[144,4608]{1,0:T(8,128)(2,1)} %get-tuple-element.73), channel_id=1, source_target_pairs={{0,1},{1,0},{2,3},{3,2},{4,5},{5,4},{6,7},{7,6},{8,9},{9,8},{10,11... | collective-permute-start | bytes 3981320 | tf_op jit(solution)/shard_map/ppermute | solution.py:1127
  362.3 78.1 %collective-permute-start.6 = (bf16[144,4608]{1,0:T(8,128)(2,1)}, bf16[144,4608]{1,0:T(8,128)(2,1)}, u32[]{:S(2)}, u32[]{:S(2)}) collective-permute-start(bf16[144,4608]{1,0:T(8,128)(2,1)} %get-tuple-element.75), channel_id=1, source_target_pairs={{0,2},{2,0},{1,3},{3,1},{4,6},{6,4},{5,7},{7,5},{8,10},{10,8},{9,1... | collective-permute-start | bytes 3981320 | tf_op jit(solution)/shard_map/ppermute | solution.py:1128
  363.5 76.9 %collective-permute-start.5 = (bf16[720,1152]{1,0:T(8,128)(2,1)}, bf16[720,1152]{1,0:T(8,128)(2,1)S(1)}, u32[]{:S(2)}, u32[]{:S(2)}) collective-permute-start(bf16[720,1152]{1,0:T(8,128)(2,1)} %get-tuple-element.74), channel_id=1, source_target_pairs={{0,1},{1,0},{2,3},{3,2},{4,5},{5,4},{6,7},{7,6},{8,9},{9,8},{10,11... | collective-permute-start | bytes 4976648 | tf_op jit(solution)/shard_map/ppermute | solution.py:1127
  364.9 75.5 %collective-permute-start.7 = (bf16[720,1152]{1,0:T(8,128)(2,1)}, bf16[720,1152]{1,0:T(8,128)(2,1)S(1)}, u32[]{:S(2)}, u32[]{:S(2)}) collective-permute-start(bf16[720,1152]{1,0:T(8,128)(2,1)} %get-tuple-element.76), channel_id=1, source_target_pairs={{0,2},{2,0},{1,3},{3,1},{4,6},{6,4},{5,7},{7,5},{8,10},{10,8},{9,1... | collective-permute-start | bytes 4976648 | tf_op jit(solution)/shard_map/ppermute | solution.py:1128
  440.4 1.1 copy-start

commit v8 on v7

--- a/solution.py
+++ b/solution.py
@@ -10,6 +10,7 @@
 
 def kwin(n): return (n + 29 + 31)//32*32
 def qwin(n): return (n + 15 + QT-1)//QT*QT
+def qtile(n): return qwin(n) if n==LONG else QT
 
 def nt(a,b): return lax.dot_general(a,b,(((1,),(1,)),((),())),preferred_element_type=jnp.float32)
 def nn(a,b): return lax.dot_general(a,b,(((1,),(0,)),((),())),preferred_element_type=jnp.float32)
@@ -94,10 +95,11 @@
     def one(item,start,size):
         k0,q0=windows(start,size,row_len)
         kr=pl.ds(k0,kwin(size))
-        @pl.loop(0,qwin(size)//QT)
+        qt=qtile(size)
+        @pl.loop(0,qwin(size)//qt)
         def _(t):
-            qr=pl.ds(pl.multiple_of(q0+t*QT,16),QT)
-            col=q0+t*QT+lax.broadcasted_iota(jnp.int32,(1,QT),1)
+            qr=pl.ds(pl.multiple_of(q0+t*qt,16),qt)
+            col=q0+t*qt+lax.broadcasted_iota(jnp.int32,(1,qt),1)
             live=(col>=start)&(col<start+size)
             for h in range(heads):
                 s=nt(split_ref[heads+h,kr,:],split_ref[h,qr,:])
@@ -108,7 +110,7 @@
                 o=tn(split_ref[2*heads+h,kr,:],p.astype(jnp.bfloat16))
                 o=jnp.where(live,o/l,0.0)
                 acc_ref[h,qr,:]+=o.T.astype(jnp.bfloat16)
-                lse_ref[item,pl.ds(t*heads+h,1),:]=m*(SCALE*LOG2E)+jnp.log2(l)
+                lse_ref[item,pl.ds(t*heads+h,1),:qt]=m*(SCALE*LOG2E)+jnp.log2(l)
     for_items(len_ref,one)
     if len(outs)==2: pack_heads(acc_ref,*outs,heads)
     else: join_heads(acc_ref,outs[0],heads)
@@ -127,14 +129,15 @@
         for h in range(heads):
             dk_ref[h,:kw,:]=jnp.zeros((kw,HEAD),jnp.float32)
             dv_ref[h,:kw,:]=jnp.zeros((kw,HEAD),jnp.float32)
-        @pl.loop(0,qwin(size)//QT)
+        qt=qtile(size)
+        @pl.loop(0,qwin(size)//qt)
         def _(t):
-            qr=pl.ds(pl.multiple_of(q0+t*QT,16),QT)
-            col=q0+t*QT+lax.broadcasted_iota(jnp.int32,(1,QT),1)
+            qr=pl.ds(pl.multiple_of(q0+t*qt,16),qt)
+            col=q0+t*qt+lax.broadcasted_iota(jnp.int32,(1,qt),1)
             live=(col>=start)&(col<start+size)
             for h in range(heads):
                 k=split_ref[heads+h,kr,:]; q=split_ref[h,qr,:]; g=gsplit_ref[h,qr,:]
-                lse=jnp.where(live,lse_ref[item,pl.ds(t*heads+h,1),:],1e30)
+                lse=jnp.where(live,lse_ref[item,pl.ds(t*heads+h,1),:qt],1e30)
                 s=nt(k,q)
                 p=jnp.exp2(s*(SCALE*LOG2E)-lse)
                 p=mask_edges(p,start,k0,size,0.0)
@@ -154,10 +157,10 @@
 VM=pl.BlockSpec(memory_space=pltpu.VMEM); SM=pl.BlockSpec(memory_space=pltpu.SMEM)
 def attend(lens,qkv,heads,packed=False):
     n=qkv.shape[0]
-    nt_=heads*(qwin(LONG)//QT)
+    nt_=max(8,heads*(qwin(LONG)//qtile(LONG)))
     shapes=((n,LANES),(n//4,4*(heads*HEAD-LANES))) if packed else ((n,heads*HEAD),)
     return pl.pallas_call(functools.partial(attend_kernel,heads),
-      out_shape=tuple(jax.ShapeDtypeStruct(s,jnp.bfloat16) for s in shapes)+(jax.ShapeDtypeStruct((NITEM,nt_,QT),jnp.float32),),
+      out_shape=tuple(jax.ShapeDtypeStruct(s,jnp.bfloat16) for s in shapes)+(jax.ShapeDtypeStruct((NITEM,nt_,qtile(LONG)),jnp.float32),),
       in_specs=[SM,VM],out_specs=(VM,)*(len(shapes)+1),
       scratch_shapes=[pltpu.VMEM((3*heads,n,HEAD),jnp.bfloat16),pltpu.VMEM((heads,n,HEAD),jnp.bfloat16)],
       compiler_params=pltpu.CompilerParams(vmem_limit_bytes=56*2**20),
@@ -697,7 +700,7 @@
         cost_estimate=pl.CostEstimate(flops=2*tokens*d*d*10,bytes_accessed=60*2**20,transcendentals=0))(
         gq,heads,normed,hidden,gmid,gain,block,long,wskip,small,eu,ed,eo)
 
-SPLIT=((0,640),(640,512))
+SPLIT=((0,1152),)
 def middle_kernel(hidden_ref,att_ref,tail_ref,g_ref,gain_ref,shift_ref,outw_ref,outx_ref,outy_ref,upw_ref,upx_ref,upy_ref,dnw_ref,
                   lay_out,gmid_ref,gh_out,ght_out,gow_out,small_ref,gup_out,gdn_out,sxu_out,sxd_out,syu_out,syd_out,uland,dland,ux_out,uy_out,dx_out,dy_out,
                   att_in,tail_in,att_s,outw_s,n2_s,xhat_s,rstd_s,lay_s,act_s,gu_s,upb,dnb,gub,gdb,land_u,land_d,low_s,

time: 629 us -> 613 us (0.975)
  Pallas kernels: 591 us -> 572 us
    pallas_call x1, Pallas kernels: 43.5 us -> 33.7 us  [attend(): pl.pallas_call(functools.partial(attend_kernel, heads), out_shape=tuple((...]
    pallas_call x1, Pallas kernels: 74.5 us -> 66 us  [attend_back(): pl.pallas_call(functools.partial(attend_back_kernel, heads), out_shape=ja...]
  transfers between devices with their start and end apart: 9 -> 9, of which waited for: 0 -> 2; matrix products, arithmetic and copies ran while one was open for 0% -> 0% of each run, Pallas kernels for 19% -> 17%
where the time goes in v8:
time: 613 us; the launch traced here: 604 us
  Pallas kernels  572 us (93%)
  local copies, waits for them, and re-layouts  11.8 us (2%)
  starting transfers between devices  10 us (2%)
  other arithmetic  8.22 us (1%)
    pallas_call x1, Pallas kernels, middle(): pl.pallas_call(middle_kernel, out_shape=(S((tokens, d), BF), S((tokens, d...  190 us
    pallas_call x1, Pallas kernels, last(): pl.pallas_call(last_kernel, out_shape=(S((tokens, d), BF), S((tokens, d),...  158 us
    pallas_call x1, Pallas kernels, first(): pl.pallas_call(first_kernel, out_shape=(S((tokens, d), F32), S((4 * token...  109 us
    pallas_call x1, Pallas kernels, attend_back(): pl.pallas_call(functools.partial(attend_back_kernel, heads), out_shape=ja...  66 us
    pallas_call x1, Pallas kernels, attend(): pl.pallas_call(functools.partial(attend_kernel, heads), out_shape=tuple((...  33.7 us
    pallas_call x1, Pallas kernels, assemble(): pl.pallas_call(assemble_kernel, out_shape=(shapes[0],) + shapes, in_specs...  15.7 us
  transfers between devices with their start and end apart: 9, of which 2 were waited for; matrix products, arithmetic and copies ran while one was open for 0% of the time, Pallas kernels for 17%

profile of v8, /device:TPU:0, one launch (start us, length us, event | category | flops | bytes accessed | tf_op | source)
XLA Modules:
  0.0 603.9 jit_solution(1413656149854142088)
XLA Ops:
  0.6 0.7 stack.19
  1.3 0.7 stack.20
  2.0 0.7 stack.21
  2.7 0.7 stack.22
  3.4 0.6 convert_element_type.45.vec_ref
  4.0 1.0 constant_dynamic-slice_fusion
  5.0 1.4 constant_dynamic-slice_fusion.1
  6.4 109.0 %shard_map.220 = (f32[832,1152]{1,0:T(8,128)}, bf16[3328,1152]{1,0:T(8,128)(2,1)}, bf16[3328,864]{1,0:T(8,128)(2,1)}, bf16[1152,864]{1,0:T(8,128)(2,1)}, bf16[23...) custom-call(bf16[832,1152]{1,0:T(8,128)(2,1)} %bitcast.38, bf16[832,1152]{1,0:T(8,128)(2,1)} %bitcast.40, ...), custom_call_target="tpu_custom_call" | custom-call | flops 11041505280 | bytes 41943040 | tf_op jit(solution)/shard_map/pallas_call | solution.py:443
  115.4 1.1 collective-permute-start.3
  116.6 0.6 collective-permute-start.2
  117.2 0.9 collective-permute-start.1
  118.1 1.5 collective-permute-start
  119.6 33.7 %shard_map.221 = (bf16[3328,256]{1,0:T(8,128)(2,1)}, bf16[832,128]{1,0:T(8,128)(2,1)}, f32[12,8,1152]{2,1,0:T(8,128)}) custom-call(s32[1,12]{1,0:T(1,128)} %len_ref.3, bf16[3328,864]{1,0:T(8,128)(2,1)} %get-tuple-element.63.qkv_ref), custom_call_target="tpu_custom_call" | custom-call | flops 12759072768 | bytes 12582912 | tf_op jit(solution)/shard_map/pallas_call | solution.py:162
  153.2 1.0 slice_reduce_fusion
  154.2 0.7 slice.54.gain_ref
  154.9 0.7 slice.48.shift_ref
  155.6 0.7 slice.46.gain_ref
  156.2 0.0 collective-permute-done.1.outy_ref
  156.2 0.0 copy-start.2
  156.2 0.0 collective-permute-done.outx_ref
  156.3 0.0 collective-permute-done.3.upy_ref
  156.3 0.0 copy-start.1
  156.3 0.0 collective-permute-done.2.upx_ref
  156.3 1.1 copy-done.1
  157.4 0.1 copy-done.2
  157.4 190.1 %shard_map.222 = (bf16[832,1152]{1,0:T(8,128)(2,1)}, f32[832,1152]{1,0:T(8,128)}, bf16[4,832,256]{2,1,0:T(8,128)(2,1)}, bf16[4,208,128]{2,1,0:T(8,128)(2,1)}, bf...) custom-call(f32[832,1152]{1,0:T(8,128)} %get-tuple-element.61.hidden, ...), custom_call_target="tpu_custom_call" | custom-call | flops 59624128512 | bytes 62914560 | tf_op jit(solution)/shard_map/pallas_call | solution.py:993
  347.5 1.0 slice_bitcast_fusion
  348.5 1.9 collective-permute-start.8
  350.3 0.5 collective-permute-start.4
  350.9 1.2 collective-permute-start.6
  352.0 1.4 collective-permute-start.5
  353.5 0.9 collective-permute-start.7
  354.4 66.0 %shard_map.223.gq_ref = bf16[3328,864]{1,0:T(8,128)(2,1)} custom-call(s32[1,12]{1,0:T(1,128)} %len_ref.3, bf16[3328,864]{1,0:T(8,128)(2,1)} %get-tuple-element.63.qkv_ref, bf16[3328,256]{1,0:T(8,128)(2,1)} %bitcast.43, bf16[832,128]{1,0:T(8,128)(2,1)} %bitcast.44, f32[12,8,1152]{2,1,0:T(8,128)} %get-tuple-element.72.refs_2_), custom_call_target="tpu_custom_call" | custom-call | flops 31897681920 | bytes 20971520 | tf_op jit(solution)/shard_map/pallas_call | solution.py:170
  420.4 0.0 copy-start
  420.4 0.0 collective-permute-done.8
  420.4 0.0 collective-permute-done.4
  420.4 0.0 collective-permute-done.6
  420.4 0.2 collective-permute-done.5
  420.6 0.6 collective-permute-done.7
  421.2 0.4 convert_add_fusion
  421.6 0.0 copy-done
  421.6 0.8 fusion.4.eo_ref
  422.5 2.7 fusion.ed_ref
  425.2 3.7 fusion.2.eu_ref
  428.8 157.7 %shard_map.224 = (bf16[832,1152]{1,0:T(8,128)(2,1)}, bf16[832,1152]{1,0:T(8,128)(2,1)}, f32[8,1152]{1,0:T(8,128)}, bf16[4,2,144,864]{3,2,1,0:T(8,128)(2,1)}, bf1...) custom-call(bf16[3328,864]{1,0:T(8,128)(2,1)} %shard_map.223.gq_ref, ...), custom_call_target="tpu_custom_call" | custom-call | flops 22083010560 | bytes 62914560 | tf_op jit(solution)/shard_map/pallas_call | solution.py:690
  586.5 0.8 slice.55
  587.3 0.1 dynamic-slice_bitcast_fusion
  587.3 0.6 slice_reduce_fusion.3
  588.0 15.7 %shard_map.225 = (f32[832,1152]{1,0:T(8,128)}, f32[832,1152]{1,0:T(8,128)}, f32[832,1152]{1,0:T(8,128)}, f32[576,1152]{1,0:T(8,128)}, f32[288,3456]{1,0:T(8,128)...) custom-call(bf16[832,1152]{1,0:T(8,128)(2,1)} %get-tuple-element.69.lay_ref, ...), custom_call_target="tpu_custom_call" | custom-call | bytes 41943040 | tf_op jit(solution)/shard_map/pallas_call | solution.py:1050
  (1 shorter events, 0.0 us)
Async XLA Ops:
  115.4 40.8 %collective-permute-start.3 = (bf16[144,4608]{1,0:T(8,128)(2,1)S(1)}, bf16[144,4608]{1,0:T(8,128)(2,1)S(1)}, u32[]{:S(2)}, u32[]{:S(2)}) collective-permute-start(bf16[144,4608]{1,0:T(8,128)(2,1)S(1)} %constant_dynamic-slice_fusion.1), channel_id=1, source_target_pairs={{0,2},{2,0},{1,3},{3,1},{4,6},{6,4},{5,7},{7,5},{8,10},{10,8},{9,1... | collective-permute-start | bytes 3981320 | tf_op jit(solution)/shard_map/ppermute | solution.py:1093
  116.6 39.7 %collective-permute-start.2 = (bf16[144,4608]{1,0:T(8,128)(2,1)S(1)}, bf16[144,4608]{1,0:T(8,128)(2,1)}, u32[]{:S(2)}, u32[]{:S(2)}) collective-permute-start(bf16[144,4608]{1,0:T(8,128)(2,1)S(1)} %constant_dynamic-slice_fusion.1), channel_id=1, source_target_pairs={{0,1},{1,0},{2,3},{3,2},{4,5},{5,4},{6,7},{7,6},{8,9},{9,8},{10,11... | collective-permute-start | bytes 3981320 | tf_op jit(solution)/shard_map/ppermute | solution.py:1092
  117.2 39.0 %collective-permute-start.1 = (bf16[144,1152]{1,0:T(8,128)(2,1)S(1)}, bf16[144,1152]{1,0:T(8,128)(2,1)S(1)}, u32[]{:S(2)}, u32[]{:S(2)}) collective-permute-start(bf16[144,1152]{1,0:T(8,128)(2,1)S(1)} %constant_dynamic-slice_fusion), channel_id=1, source_target_pairs={{0,2},{2,0},{1,3},{3,1},{4,6},{6,4},{5,7},{7,5},{8,10},{10,8},{9,1... | collective-permute-start | bytes 995336 | tf_op jit(solution)/shard_map/ppermute | solution.py:1093
  118.1 38.2 %collective-permute-start = (bf16[144,1152]{1,0:T(8,128)(2,1)S(1)}, bf16[144,1152]{1,0:T(8,128)(2,1)}, u32[]{:S(2)}, u32[]{:S(2)}) collective-permute-start(bf16[144,1152]{1,0:T(8,128)(2,1)S(1)} %constant_dynamic-slice_fusion), channel_id=1, source_target_pairs={{0,1},{1,0},{2,3},{3,2},{4,5},{5,4},{6,7},{7,6},{8,9},{9,8},{10,11... | collective-permute-start | bytes 995336 | tf_op jit(solution)/shard_map/ppermute | solution.py:1092
  156.2 1.2 copy-start.2
  156.3 1.1 copy-start.1
  348.5 72.0 %collective-permute-start.8 = (bf16[144,1152]{1,0:T(8,128)(2,1)S(1)}, bf16[144,1152]{1,0:T(8,128)(2,1)S(1)}, u32[]{:S(2)}, u32[]{:S(2)}) collective-permute-start(bf16[144,1152]{1,0:T(8,128)(2,1)S(1)} %slice_bitcast_fusion), channel_id=1, source_target_pairs={{0,3},{1,2},{2,1},{3,0},{4,7},{5,6},{6,5},{7,4},{8,11},{9,10},{10,... | collective-permute-start | bytes 995336 | tf_op jit(solution)/shard_map/ppermute | solution.py:1132
  350.3 70.1 %collective-permute-start.4 = (bf16[144,4608]{1,0:T(8,128)(2,1)}, bf16[144,4608]{1,0:T(8,128)(2,1)}, u32[]{:S(2)}, u32[]{:S(2)}) collective-permute-start(bf16[144,4608]{1,0:T(8,128)(2,1)} %get-tuple-element.73), channel_id=1, source_target_pairs={{0,1},{1,0},{2,3},{3,2},{4,5},{5,4},{6,7},{7,6},{8,9},{9,8},{10,11... | collective-permute-start | bytes 3981320 | tf_op jit(solution)/shard_map/ppermute | solution.py:1130
  350.9 69.6 %collective-permute-start.6 = (bf16[144,4608]{1,0:T(8,128)(2,1)}, bf16[144,4608]{1,0:T(8,128)(2,1)}, u32[]{:S(2)}, u32[]{:S(2)}) collective-permute-start(bf16[144,4608]{1,0:T(8,128)(2,1)} %get-tuple-element.75), channel_id=1, source_target_pairs={{0,2},{2,0},{1,3},{3,1},{4,6},{6,4},{5,7},{7,5},{8,10},{10,8},{9,1... | collective-permute-start | bytes 3981320 | tf_op jit(solution)/shard_map/ppermute | solution.py:1131
  352.0 68.6 %collective-permute-start.5 = (bf16[720,1152]{1,0:T(8,128)(2,1)}, bf16[720,1152]{1,0:T(8,128)(2,1)S(1)}, u32[]{:S(2)}, u32[]{:S(2)}) collective-permute-start(bf16[720,1152]{1,0:T(8,128)(2,1)} %get-tuple-element.74), channel_id=1, source_target_pairs={{0,1},{1,0},{2,3},{3,2},{4,5},{5,4},{6,7},{7,6},{8,9},{9,8},{10,11... | collective-permute-start | bytes 4976648 | tf_op jit(solution)/shard_map/ppermute | solution.py:1130
  353.5 67.7 %collective-permute-start.7 = (bf16[720,1152]{1,0:T(8,128)(2,1)}, bf16[720,1152]{1,0:T(8,128)(2,1)S(1)}, u32[]{:S(2)}, u32[]{:S(2)}) collective-permute-start(bf16[720,1152]{1,0:T(8,128)(2,1)} %get-tuple-element.76), channel_id=1, source_target_pairs={{0,2},{2,0},{1,3},{3,1},{4,6},{6,4},{5,7},{7,5},{8,10},{10,8},{9,1... | collective-permute-start | bytes 4976648 | tf_op jit(solution)/shard_map/ppermute | solution.py:1131
  420.4 1.2 copy-start

commit v9 on v8

--- a/solution.py
+++ b/solution.py
@@ -418,6 +418,10 @@
     def project(b,i): qs[nrows(b,i),:]=nn(ns[nrows(b,i),:],hs[...]).astype(BF)
     @pl.loop(0,4)
     def _(i): project(w,i)
+    def put_block(k,b):
+        r=pl.ds(mul(b*tokens,16),tokens)
+        put(k,ns.at[r],normed_out.at[r]); put(k+4,qs.at[r],qkv_out.at[r])
+    put_block(8,w)
     for i,t,b,k,k2,t2 in ((0,"X",wx,18,26,"Y"),(1,"Y",wy,22,27,"X"),(2,"X",wx,18,28,"Y"),(3,"Y",wy,22,29,"X")):
         net.got(k+i,t,ns.at[nrows(b,i)])
         net.start(k2,t2,ns.at[nrows(b,i)],ns.at[nrows(b,i)])
@@ -430,10 +434,11 @@
         project(wx,i)
         net.got(22+i-1,"Y",ns.at[nrows(wy,i-1)])
         project(wy,i-1)
+    put_block(9,wx); put_block(10,wy)
     for i,t,k in ((0,"Y",26),(1,"X",27),(2,"Y",28),(3,"X",29)):
         net.got(k,t,ns.at[nrows(wd,i)])
         project(wd,i)
-    put(5,ns,normed_out); put(6,qs,qkv_out)
+    put_block(11,wd)
     for copy in outs: copy.wait()
     net.finish()
 
@@ -444,7 +449,7 @@
         out_shape=(S((tokens,d),F32),S((4*tokens,d),BF),S((4*tokens,hd3),BF),S((d,hd3),BF),S((2*d,d),BF),S((4,)+vecs.shape,F32)),
         in_specs=[VM]*5,out_specs=(ANY,)*6,
         scratch_shapes=[V((2*d,d),BF),V((4*tokens,d),BF),V((d,hd3),BF),V((4,d//4,hd3),BF),V((tokens,d),F32),V((4*tokens,hd3),BF),V((4,)+vecs.shape,F32),
-            pltpu.SemaphoreType.DMA((33,)),pltpu.SemaphoreType.DMA((33,)),pltpu.SemaphoreType.DMA((8,))],
+            pltpu.SemaphoreType.DMA((33,)),pltpu.SemaphoreType.DMA((33,)),pltpu.SemaphoreType.DMA((16,))],
         compiler_params=pltpu.CompilerParams(vmem_limit_bytes=56*2**20,collective_id=0,has_side_effects=True),
         cost_estimate=pl.CostEstimate(flops=2*tokens*d*d*5,bytes_accessed=40*2**20,transcendentals=0))(
         block,long,skipw,qkvw,vecs)

time: 613 us -> 610 us (level)
  transfers between devices with their start and end apart: 9 -> 9, of which waited for: 2 -> 2; matrix products, arithmetic and copies ran while one was open for 0% -> 1% of each run, Pallas kernels for 17% -> 17%
where the time goes in v9:
time: 610 us; the launch traced here: 601 us
  Pallas kernels  569 us (93%)
  local copies, waits for them, and re-layouts  11.8 us (2%)
  starting transfers between devices  9.96 us (2%)
  other arithmetic  8.22 us (1%)
    pallas_call x1, Pallas kernels, middle(): pl.pallas_call(middle_kernel, out_shape=(S((tokens, d), BF), S((tokens, d...  190 us
    pallas_call x1, Pallas kernels, last(): pl.pallas_call(last_kernel, out_shape=(S((tokens, d), BF), S((tokens, d),...  158 us
    pallas_call x1, Pallas kernels, first(): pl.pallas_call(first_kernel, out_shape=(S((tokens, d), F32), S((4 * token...  106 us
    pallas_call x1, Pallas kernels, attend_back(): pl.pallas_call(functools.partial(attend_back_kernel, heads), out_shape=ja...  66 us
    pallas_call x1, Pallas kernels, attend(): pl.pallas_call(functools.partial(attend_kernel, heads), out_shape=tuple((...  33.7 us
    pallas_call x1, Pallas kernels, assemble(): pl.pallas_call(assemble_kernel, out_shape=(shapes[0],) + shapes, in_specs...  15.7 us
  transfers between devices with their start and end apart: 9, of which 2 were waited for; matrix products, arithmetic and copies ran while one was open for 1% of the time, Pallas kernels for 17%

profile of v9, /device:TPU:0, one launch (start us, length us, event | category | flops | bytes accessed | tf_op | source)
XLA Modules:
  0.0 601.0 jit_solution(2174606547244918814)
XLA Ops:
  0.6 0.7 stack.19
  1.3 0.7 stack.20
  2.0 0.7 stack.21
  2.7 0.7 stack.22
  3.4 0.6 convert_element_type.45.vec_ref
  4.0 1.0 constant_dynamic-slice_fusion
  5.0 1.4 constant_dynamic-slice_fusion.1
  6.4 106.1 %shard_map.220 = (f32[832,1152]{1,0:T(8,128)}, bf16[3328,1152]{1,0:T(8,128)(2,1)}, bf16[3328,864]{1,0:T(8,128)(2,1)}, bf16[1152,864]{1,0:T(8,128)(2,1)}, bf16[23...) custom-call(bf16[832,1152]{1,0:T(8,128)(2,1)} %bitcast.38, bf16[832,1152]{1,0:T(8,128)(2,1)} %bitcast.40, ...), custom_call_target="tpu_custom_call" | custom-call | flops 11041505280 | bytes 41943040 | tf_op jit(solution)/shard_map/pallas_call | solution.py:448
  112.5 1.1 collective-permute-start.3
  113.6 0.7 collective-permute-start.2
  114.4 0.8 collective-permute-start.1
  115.2 1.5 collective-permute-start
  116.6 33.7 %shard_map.221 = (bf16[3328,256]{1,0:T(8,128)(2,1)}, bf16[832,128]{1,0:T(8,128)(2,1)}, f32[12,8,1152]{2,1,0:T(8,128)}) custom-call(s32[1,12]{1,0:T(1,128)} %len_ref.3, bf16[3328,864]{1,0:T(8,128)(2,1)} %get-tuple-element.63.qkv_ref), custom_call_target="tpu_custom_call" | custom-call | flops 12759072768 | bytes 12582912 | tf_op jit(solution)/shard_map/pallas_call | solution.py:162
  150.3 1.0 slice_reduce_fusion
  151.3 0.7 slice.54.gain_ref
  152.0 0.7 slice.48.shift_ref
  152.6 0.7 slice.46.gain_ref
  153.3 0.0 collective-permute-done.1.outy_ref
  153.3 0.0 copy-start.2
  153.3 0.0 collective-permute-done.outx_ref
  153.3 0.0 collective-permute-done.3.upy_ref
  153.3 0.0 copy-start.1
  153.4 0.0 collective-permute-done.2.upx_ref
  153.4 1.1 copy-done.1
  154.4 0.1 copy-done.2
  154.5 190.1 %shard_map.222 = (bf16[832,1152]{1,0:T(8,128)(2,1)}, f32[832,1152]{1,0:T(8,128)}, bf16[4,832,256]{2,1,0:T(8,128)(2,1)}, bf16[4,208,128]{2,1,0:T(8,128)(2,1)}, bf...) custom-call(f32[832,1152]{1,0:T(8,128)} %get-tuple-element.61.hidden, ...), custom_call_target="tpu_custom_call" | custom-call | flops 59624128512 | bytes 62914560 | tf_op jit(solution)/shard_map/pallas_call | solution.py:998
  344.6 1.0 slice_bitcast_fusion
  345.6 1.8 collective-permute-start.8
  347.4 0.5 collective-permute-start.4
  348.0 1.2 collective-permute-start.6
  349.2 1.3 collective-permute-start.5
  350.5 1.0 collective-permute-start.7
  351.5 66.0 %shard_map.223.gq_ref = bf16[3328,864]{1,0:T(8,128)(2,1)} custom-call(s32[1,12]{1,0:T(1,128)} %len_ref.3, bf16[3328,864]{1,0:T(8,128)(2,1)} %get-tuple-element.63.qkv_ref, bf16[3328,256]{1,0:T(8,128)(2,1)} %bitcast.43, bf16[832,128]{1,0:T(8,128)(2,1)} %bitcast.44, f32[12,8,1152]{2,1,0:T(8,128)} %get-tuple-element.72.refs_2_), custom_call_target="tpu_custom_call" | custom-call | flops 31897681920 | bytes 20971520 | tf_op jit(solution)/shard_map/pallas_call | solution.py:170
  417.5 0.0 copy-start
  417.5 0.0 collective-permute-done.8
  417.5 0.0 collective-permute-done.4
  417.5 0.0 collective-permute-done.6
  417.5 0.2 collective-permute-done.5
  417.7 0.6 collective-permute-done.7
  418.4 0.4 convert_add_fusion
  418.8 0.0 copy-done
  418.8 0.8 fusion.4.eo_ref
  419.7 2.7 fusion.ed_ref
  422.3 3.7 fusion.2.eu_ref
  426.0 157.6 %shard_map.224 = (bf16[832,1152]{1,0:T(8,128)(2,1)}, bf16[832,1152]{1,0:T(8,128)(2,1)}, f32[8,1152]{1,0:T(8,128)}, bf16[4,2,144,864]{3,2,1,0:T(8,128)(2,1)}, bf1...) custom-call(bf16[3328,864]{1,0:T(8,128)(2,1)} %shard_map.223.gq_ref, ...), custom_call_target="tpu_custom_call" | custom-call | flops 22083010560 | bytes 62914560 | tf_op jit(solution)/shard_map/pallas_call | solution.py:695
  583.6 0.8 slice.55
  584.3 0.1 dynamic-slice_bitcast_fusion
  584.4 0.6 slice_reduce_fusion.3
  585.0 15.7 %shard_map.225 = (f32[832,1152]{1,0:T(8,128)}, f32[832,1152]{1,0:T(8,128)}, f32[832,1152]{1,0:T(8,128)}, f32[576,1152]{1,0:T(8,128)}, f32[288,3456]{1,0:T(8,128)...) custom-call(bf16[832,1152]{1,0:T(8,128)(2,1)} %get-tuple-element.69.lay_ref, ...), custom_call_target="tpu_custom_call" | custom-call | bytes 41943040 | tf_op jit(solution)/shard_map/pallas_call | solution.py:1055
  (1 shorter events, 0.0 us)
Async XLA Ops:
  112.5 40.8 %collective-permute-start.3 = (bf16[144,4608]{1,0:T(8,128)(2,1)S(1)}, bf16[144,4608]{1,0:T(8,128)(2,1)S(1)}, u32[]{:S(2)}, u32[]{:S(2)}) collective-permute-start(bf16[144,4608]{1,0:T(8,128)(2,1)S(1)} %constant_dynamic-slice_fusion.1), channel_id=1, source_target_pairs={{0,2},{2,0},{1,3},{3,1},{4,6},{6,4},{5,7},{7,5},{8,10},{10,8},{9,1... | collective-permute-start | bytes 3981320 | tf_op jit(solution)/shard_map/ppermute | solution.py:1098
  113.6 39.7 %collective-permute-start.2 = (bf16[144,4608]{1,0:T(8,128)(2,1)S(1)}, bf16[144,4608]{1,0:T(8,128)(2,1)}, u32[]{:S(2)}, u32[]{:S(2)}) collective-permute-start(bf16[144,4608]{1,0:T(8,128)(2,1)S(1)} %constant_dynamic-slice_fusion.1), channel_id=1, source_target_pairs={{0,1},{1,0},{2,3},{3,2},{4,5},{5,4},{6,7},{7,6},{8,9},{9,8},{10,11... | collective-permute-start | bytes 3981320 | tf_op jit(solution)/shard_map/ppermute | solution.py:1097
  114.4 39.0 %collective-permute-start.1 = (bf16[144,1152]{1,0:T(8,128)(2,1)S(1)}, bf16[144,1152]{1,0:T(8,128)(2,1)S(1)}, u32[]{:S(2)}, u32[]{:S(2)}) collective-permute-start(bf16[144,1152]{1,0:T(8,128)(2,1)S(1)} %constant_dynamic-slice_fusion), channel_id=1, source_target_pairs={{0,2},{2,0},{1,3},{3,1},{4,6},{6,4},{5,7},{7,5},{8,10},{10,8},{9,1... | collective-permute-start | bytes 995336 | tf_op jit(solution)/shard_map/ppermute | solution.py:1098
  115.2 38.1 %collective-permute-start = (bf16[144,1152]{1,0:T(8,128)(2,1)S(1)}, bf16[144,1152]{1,0:T(8,128)(2,1)}, u32[]{:S(2)}, u32[]{:S(2)}) collective-permute-start(bf16[144,1152]{1,0:T(8,128)(2,1)S(1)} %constant_dynamic-slice_fusion), channel_id=1, source_target_pairs={{0,1},{1,0},{2,3},{3,2},{4,5},{5,4},{6,7},{7,6},{8,9},{9,8},{10,11... | collective-permute-start | bytes 995336 | tf_op jit(solution)/shard_map/ppermute | solution.py:1097
  153.3 1.2 copy-start.2
  153.3 1.1 copy-start.1
  345.6 71.9 %collective-permute-start.8 = (bf16[144,1152]{1,0:T(8,128)(2,1)S(1)}, bf16[144,1152]{1,0:T(8,128)(2,1)S(1)}, u32[]{:S(2)}, u32[]{:S(2)}) collective-permute-start(bf16[144,1152]{1,0:T(8,128)(2,1)S(1)} %slice_bitcast_fusion), channel_id=1, source_target_pairs={{0,3},{1,2},{2,1},{3,0},{4,7},{5,6},{6,5},{7,4},{8,11},{9,10},{10,... | collective-permute-start | bytes 995336 | tf_op jit(solution)/shard_map/ppermute | solution.py:1137
  347.4 70.1 %collective-permute-start.4 = (bf16[144,4608]{1,0:T(8,128)(2,1)}, bf16[144,4608]{1,0:T(8,128)(2,1)}, u32[]{:S(2)}, u32[]{:S(2)}) collective-permute-start(bf16[144,4608]{1,0:T(8,128)(2,1)} %get-tuple-element.73), channel_id=1, source_target_pairs={{0,1},{1,0},{2,3},{3,2},{4,5},{5,4},{6,7},{7,6},{8,9},{9,8},{10,11... | collective-permute-start | bytes 3981320 | tf_op jit(solution)/shard_map/ppermute | solution.py:1135
  348.0 69.6 %collective-permute-start.6 = (bf16[144,4608]{1,0:T(8,128)(2,1)}, bf16[144,4608]{1,0:T(8,128)(2,1)}, u32[]{:S(2)}, u32[]{:S(2)}) collective-permute-start(bf16[144,4608]{1,0:T(8,128)(2,1)} %get-tuple-element.75), channel_id=1, source_target_pairs={{0,2},{2,0},{1,3},{3,1},{4,6},{6,4},{5,7},{7,5},{8,10},{10,8},{9,1... | collective-permute-start | bytes 3981320 | tf_op jit(solution)/shard_map/ppermute | solution.py:1136
  349.2 68.5 %collective-permute-start.5 = (bf16[720,1152]{1,0:T(8,128)(2,1)}, bf16[720,1152]{1,0:T(8,128)(2,1)S(1)}, u32[]{:S(2)}, u32[]{:S(2)}) collective-permute-start(bf16[720,1152]{1,0:T(8,128)(2,1)} %get-tuple-element.74), channel_id=1, source_target_pairs={{0,1},{1,0},{2,3},{3,2},{4,5},{5,4},{6,7},{7,6},{8,9},{9,8},{10,11... | collective-permute-start | bytes 4976648 | tf_op jit(solution)/shard_map/ppermute | solution.py:1135
  350.5 67.8 %collective-permute-start.7 = (bf16[720,1152]{1,0:T(8,128)(2,1)}, bf16[720,1152]{1,0:T(8,128)(2,1)S(1)}, u32[]{:S(2)}, u32[]{:S(2)}) collective-permute-start(bf16[720,1152]{1,0:T(8,128)(2,1)} %get-tuple-element.76), channel_id=1, source_target_pairs={{0,2},{2,0},{1,3},{3,1},{4,6},{6,4},{5,7},{7,5},{8,10},{10,8},{9,1... | collective-permute-start | bytes 4976648 | tf_op jit(solution)/shard_map/ppermute | solution.py:1136
  417.5 1.3 copy-start
